TPU v7x, 32 devices: a whole 2x2x4 slice. The times are simulated.
32 devices in a mesh: seq: 8 (over y, x, core), dp: 4 (over z).
Axes of the slice: x: 2, y: 2, z: 4, core: 2. Of those that a mesh axis runs over, the one named last changes fastest.
Arguments:
- queries: bfloat16 [4, 1024, 2048], P('dp', 'seq'), may hold values from -6 to 6
- keys: bfloat16 [4, 1024, 2048], P('dp', 'seq'), may hold values from -6 to 6
- values: bfloat16 [4, 1024, 2048], P('dp', 'seq'), may hold values from -6 to 6
- master: float32 [2048, 1024], P(('seq', 'dp')), may hold values from -0.24 to 0.24
- moment: float32 [2048, 1024], P(('seq', 'dp')), may hold values from -0.06 to 0.06
- second: float32 [2048, 1024], P(('seq', 'dp')), may hold values from 1e-06 to 0.0001
- gradient: float32 [2048, 1024], P(('seq', 'dp')), may hold values from -0.18 to 0.18
Outputs:
- projected: bfloat16 [4, 1024, 1024], P('dp', 'seq')
- new_master: float32 [2048, 1024], P(('seq', 'dp'))
All inputs are finite; a program needn't handle non-finite values.
Results may differ from a plain program's by a relative error of at most 0.0063.
Values may be sent and summed in bfloat16 or wider, within the bound.
No kernel may reach another device: no remote copies, remote signals or barrier semaphores. Data moves between devices by JAX's collectives and lax.ppermute only.
A program may use at most 64 MiB of HBM per device.

v0:
```python
import jax
import jax.numpy as jnp
from jax import lax
from jax.sharding import PartitionSpec as P

HEAD_DIM = 128


beta_first = 0.9
beta_second = 0.999
learning_rate = 0.1
weight_decay = 0.1
epsilon = 1e-08
step_count = 10.0


def adamw(master, moment, second, gradient):
    moment_new = beta_first * moment + (1.0 - beta_first) * gradient
    second_new = beta_second * second + (1.0 - beta_second) * gradient * gradient
    moment_hat = moment_new / (1.0 - beta_first**step_count)
    second_hat = second_new / (1.0 - beta_second**step_count)
    return master - learning_rate * (
        moment_hat / (jnp.sqrt(second_hat) + epsilon) + weight_decay * master
    )


def causal_attention(head_queries, head_keys, head_values):
    seq_length = head_queries.shape[0]
    block_rows = min(512, seq_length)
    results = []
    for first_row in range(0, seq_length, block_rows):
        last_key = first_row + block_rows
        query_block = head_queries[first_row:last_key]
        scores = jnp.einsum(
            "qhd,khd->hqk", query_block, head_keys[:last_key], preferred_element_type=jnp.float32
        )
        scores = scores * HEAD_DIM ** (-0.5)
        causal = (first_row + jnp.arange(block_rows))[:, None] >= jnp.arange(last_key)[None, :]
        scores = jnp.where(causal[None], scores, -jnp.inf)
        highest = jnp.max(scores, axis=2, keepdims=True)
        expons = jnp.exp(scores - highest)
        denominator = jnp.sum(expons, axis=2, keepdims=True)
        probs = (expons / denominator).astype(jnp.bfloat16)
        attended = jnp.einsum(
            "hqk,khd->qhd", probs, head_values[:last_key], preferred_element_type=jnp.float32
        )
        results.append(attended.astype(jnp.bfloat16))
    return jnp.concatenate(results, axis=0)


def body(queries, keys, values, master, moment, second, gradient):
    tok_rows = queries.shape[1]
    feature_count = queries.shape[2]
    head_count = feature_count // HEAD_DIM
    head_queries, head_keys, head_values = (
        lax.all_to_all(
            queries.reshape(tok_rows, head_count, HEAD_DIM),
            "seq",
            split_axis=1,
            concat_axis=0,
            tiled=True,
        ),
        lax.all_to_all(
            keys.reshape(tok_rows, head_count, HEAD_DIM),
            "seq",
            split_axis=1,
            concat_axis=0,
            tiled=True,
        ),
        lax.all_to_all(
            values.reshape(tok_rows, head_count, HEAD_DIM),
            "seq",
            split_axis=1,
            concat_axis=0,
            tiled=True,
        ),
    )
    attended = causal_attention(head_queries, head_keys, head_values)
    returned = lax.all_to_all(attended, "seq", split_axis=0, concat_axis=1, tiled=True)
    token_rows = returned.reshape(tok_rows, feature_count)
    new_master = adamw(master, moment, second, gradient)
    weight = new_master.astype(jnp.bfloat16)
    whole_weight = lax.all_gather(weight, ("seq", "dp"), axis=0, tiled=True)
    projected = jnp.dot(token_rows, whole_weight, preferred_element_type=jnp.float32)
    return (projected.astype(jnp.bfloat16).reshape(1, tok_rows, weight.shape[1]), new_master)


def solution(mesh):
    placed = (
        P("dp", "seq", None),
        P("dp", "seq", None),
        P("dp", "seq", None),
        P(("seq", "dp"), None),
        P(("seq", "dp"), None),
        P(("seq", "dp"), None),
        P(("seq", "dp"), None),
    )
    return jax.shard_map(
        body,
        mesh=mesh,
        in_specs=placed,
        out_specs=(P("dp", "seq", None), P(("seq", "dp"), None)),
        check_vma=False,
    )
```

profile of v0, /device:TPU:0, one launch (start us, length us, event | category | flops | bytes accessed | tf_op | source)
XLA Modules:
  0.0 87.9 jit_solution(16663134866864418012)
XLA Ops:
  7.2 0.0 copy-start
  7.2 0.0 all-gather.2.cloned.1.call-start
  7.2 2.2 %fusion.33 = (bf16[64,1024]{1,0:T(8,128)(2,1)}, f32[64,1024]{1,0:T(8,128)}) fusion(f32[64,1024]{1,0:T(8,128)} %param.10, f32[64,1024]{1,0:T(8,128)} %param.13, f32[64,1024]{1,0:T(8,128)} %param.12, f32[64,1024]{1,0:T(8,128)} %param.11), kind=kLoop, calls=%fused_computation.43 | loop fusion | flops 1048576 | bytes 1441792 | tf_op jit(solution)/shard_map/convert_element_type | solution.py:82
  9.4 0.0 all-gather.2.cloned.1.call-update
  9.4 0.0 copy-start.1
  9.5 2.1 %copy.46 = bf16[1,128,2048]{1,2,0:T(8,128)(2,1)} copy(bf16[1,128,2048]{2,1,0:T(8,128)(2,1)} %param.7) | data formatting | bytes 1048576 | tf_op args[0]
  11.6 5.2 %all-to-all-start = ((bf16[128,16,128]{0,2,1:T(8,128)(2,1)}), bf16[128,16,128]{0,2,1:T(8,128)(2,1)S(1)}, u32[]{:S(2)}, u32[]{:S(2)}) async-start(bf16[128,16,128]{0,2,1:T(8,128)(2,1)} %bitcast), calls=%async_computation | async-start | bytes 1048576 | tf_op jit(solution)/shard_map/all_to_all | solution.py:56
  16.7 0.0 copy-done
  16.8 1.0 %copy.49 = bf16[1,128,2048]{1,2,0:T(8,128)(2,1)} copy(bf16[1,128,2048]{2,1,0:T(8,128)(2,1)S(1)} %copy-done) | data formatting | bytes 1048576 | tf_op args[1]
  17.8 9.7 %all-to-all-done = bf16[128,16,128]{0,2,1:T(8,128)(2,1)S(1)} async-done(((bf16[128,16,128]{0,2,1:T(8,128)(2,1)}), bf16[128,16,128]{0,2,1:T(8,128)(2,1)S(1)}, u32[]{:S(2)}, u32[]{:S(2)}) %all-to-all-start) | async-done | bytes 524320 | tf_op jit(solution)/shard_map/all_to_all | solution.py:56
  27.4 3.5 %all-to-all-start.1 = ((bf16[128,16,128]{0,2,1:T(8,128)(2,1)}), bf16[128,16,128]{0,2,1:T(8,128)(2,1)S(1)}, u32[]{:S(2)}, u32[]{:S(2)}) async-start(bf16[128,16,128]{0,2,1:T(8,128)(2,1)} %bitcast.4), calls=%async_computation.1 | async-start | bytes 1048576 | tf_op jit(solution)/shard_map/all_to_all | solution.py:63
  30.9 0.0 copy-done.1
  30.9 1.0 %copy.52 = bf16[1,128,2048]{1,2,0:T(8,128)(2,1)} copy(bf16[1,128,2048]{2,1,0:T(8,128)(2,1)S(1)} %copy-done.1) | data formatting | bytes 1048576 | tf_op args[2]
  32.0 0.1 iota_compare_fusion.1
  32.1 8.6 %all-to-all-done.1 = bf16[128,16,128]{0,2,1:T(8,128)(2,1)S(1)} async-done(((bf16[128,16,128]{0,2,1:T(8,128)(2,1)}), bf16[128,16,128]{0,2,1:T(8,128)(2,1)S(1)}, u32[]{:S(2)}, u32[]{:S(2)}) %all-to-all-start.1) | async-done | bytes 524320 | tf_op jit(solution)/shard_map/all_to_all | solution.py:63
  40.6 3.5 %all-to-all-start.2 = ((bf16[128,16,128]{0,2,1:T(8,128)(2,1)}), bf16[128,16,128]{0,2,1:T(8,128)(2,1)S(1)}, u32[]{:S(2)}, u32[]{:S(2)}) async-start(bf16[128,16,128]{0,2,1:T(8,128)(2,1)} %bitcast.8), calls=%async_computation.2 | async-start | bytes 1048576 | tf_op jit(solution)/shard_map/all_to_all | solution.py:70
  44.1 0.4 iota_compare_fusion
  44.5 0.3 copy.47
  44.8 0.3 copy.50
  45.2 8.6 %all-to-all-done.2 = bf16[128,16,128]{0,2,1:T(8,128)(2,1)S(1)} async-done(((bf16[128,16,128]{0,2,1:T(8,128)(2,1)}), bf16[128,16,128]{0,2,1:T(8,128)(2,1)S(1)}, u32[]{:S(2)}, u32[]{:S(2)}) %all-to-all-start.2) | async-done | bytes 524320 | tf_op jit(solution)/shard_map/all_to_all | solution.py:70
  53.8 0.3 copy.53
  54.1 0.7 copy.54
  54.8 0.3 copy.57
  55.1 0.3 copy.58
  55.4 0.0 copy-start.2
  55.4 0.9 %fusion.36 = f32[2,512]{1,0:T(2,128)S(1)} fusion(pred[512,512]{0,1:T(8,128)(4,1)S(1)} %iota_compare_fusion.1, bf16[512,2,128]{2,0,1:T(8,128)(2,1)S(1)} %bitcast.51, bf16[512,2,128]{2,0,1:T(8,128)(2,1)S(1)} %bitcast.53), kind=kOutput, calls=%fused_computation.46 | convolution fusion | flops 136315392 | bytes 790528 | tf_op jit(solution)/shard_map/sub | solution.py:41
  56.3 0.0 copy-done.2
  56.4 1.3 %fusion.11 = bf16[512,2,128]{2,0,1:T(8,128)(2,1)S(1)} fusion(bf16[512,2,128]{2,0,1:T(8,128)(2,1)S(1)} %bitcast.56, f32[2,512]{1,0:T(2,128)S(1)} %fusion.36, pred[512,512]{0,1:T(8,128)(4,1)S(1)} %iota_compare_fusion.1, bf16[512,2,128]{2,0,1:T(8,128)(2,1)S(1)} %bitcast.52, bf16[512,2,128]{2,0,1:T(8,128)(2,1)S(1)} %bitcast.54), kind=kOutput, calls=%fused_computation.20 | convolution fusion | flops 271189504 | bytes 1314816 | tf_op jit(solution)/shard_map/hqk,khd->qhd/dot_general | solution.py:44
  57.7 3.5 %fusion.35 = (f32[2,512]{1,0:T(2,128)S(1)}, f32[2,512,1024]{2,1,0:T(8,128)}) fusion(pred[512,1024]{1,0:T(8,128)(4,1)S(1)} %iota_compare_fusion, bf16[512,2,128]{2,0,1:T(8,128)(2,1)S(1)} %bitcast.55, bf16[1024,2,128]{2,0,1:T(8,128)(2,1)S(1)} %bitcast.50), kind=kOutput, calls=%fused_computation.45 | convolution fusion | flops 272630784 | bytes 5509120 | tf_op jit(solution)/shard_map/sub | solution.py:41
  61.2 3.0 %fusion.10 = bf16[512,2,128]{2,0,1:T(8,128)(2,1)S(1)} fusion(bf16[1024,2,128]{2,0,1:T(8,128)(2,1)S(1)} %bitcast.49, f32[2,512,1024]{2,1,0:T(8,128)} %get-tuple-element.7, f32[2,512]{1,0:T(2,128)S(1)} %get-tuple-element.6), kind=kOutput, calls=%fused_computation.19 | convolution fusion | flops 270663680 | bytes 4984832 | tf_op jit(solution)/shard_map/hqk,khd->qhd/dot_general | solution.py:44
  64.3 0.5 copy.59
  64.8 12.2 %all_to_all.66 = bf16[1024,2,128]{2,1,0:T(2,128)(2,1)S(1)} all-to-all(bf16[1024,2,128]{2,1,0:T(2,128)(2,1)S(1)} %copy.59), channel_id=1, replica_groups=mesh['seq'=8,'dp'=4] {'seq'}, dimensions={0} | all-to-all | bytes 1048576 | tf_op jit(solution)/shard_map/all_to_all | solution.py:79
  77.0 0.1 copy.60
  77.1 0.3 copy.61
  77.3 0.0 all-gather.2.cloned.1.call-done
  77.4 3.6 %fusion.9 = bf16[1,128,1024]{2,1,0:T(8,128)(2,1)} fusion(bf16[128,2048]{0,1:T(8,128)(2,1)S(1)} %bitcast.44, bf16[2048,1024]{1,0:T(8,128)(2,1)} %all-gather.2.cloned.1.call-done), kind=kOutput, calls=%fused_computation.18 | convolution fusion | flops 537001984 | bytes 4980736 | tf_op jit(solution)/shard_map/dot_general | solution.py:84
  (8 shorter events, 0.2 us)
Async XLA Ops:
  7.2 9.6 %copy-start = (bf16[1,128,2048]{2,1,0:T(8,128)(2,1)S(1)}, bf16[1,128,2048]{2,1,0:T(8,128)(2,1)}, u32[]{:S(2)}) copy-start(bf16[1,128,2048]{2,1,0:T(8,128)(2,1)} %param.8) | copy-start | bytes 1572868
  7.2 70.2 %all-gather.2.cloned.1.call-start = ((), (), s32[]{:S(2)}) async-start(), calls=%async_computation.4 | async-start | bytes 4325376 | tf_op jit(solution)/shard_map/all_gather | solution.py:83
  9.4 21.5 %copy-start.1 = (bf16[1,128,2048]{2,1,0:T(8,128)(2,1)S(1)}, bf16[1,128,2048]{2,1,0:T(8,128)(2,1)}, u32[]{:S(2)}) copy-start(bf16[1,128,2048]{2,1,0:T(8,128)(2,1)} %param.9) | copy-start | bytes 1572868
  11.6 15.9 %all-to-all-start = ((bf16[128,16,128]{0,2,1:T(8,128)(2,1)}), bf16[128,16,128]{0,2,1:T(8,128)(2,1)S(1)}, u32[]{:S(2)}, u32[]{:S(2)}) async-start(bf16[128,16,128]{0,2,1:T(8,128)(2,1)} %bitcast), calls=%async_computation | async-start | bytes 1048576 | tf_op jit(solution)/shard_map/all_to_all | solution.py:56
  27.4 13.2 %all-to-all-start.1 = ((bf16[128,16,128]{0,2,1:T(8,128)(2,1)}), bf16[128,16,128]{0,2,1:T(8,128)(2,1)S(1)}, u32[]{:S(2)}, u32[]{:S(2)}) async-start(bf16[128,16,128]{0,2,1:T(8,128)(2,1)} %bitcast.4), calls=%async_computation.1 | async-start | bytes 1048576 | tf_op jit(solution)/shard_map/all_to_all | solution.py:63
  40.6 13.2 %all-to-all-start.2 = ((bf16[128,16,128]{0,2,1:T(8,128)(2,1)}), bf16[128,16,128]{0,2,1:T(8,128)(2,1)S(1)}, u32[]{:S(2)}, u32[]{:S(2)}) async-start(bf16[128,16,128]{0,2,1:T(8,128)(2,1)} %bitcast.8), calls=%async_computation.2 | async-start | bytes 1048576 | tf_op jit(solution)/shard_map/all_to_all | solution.py:70
  55.4 1.0 %copy-start.2 = (bf16[4,128,2,128]{3,1,0,2:T(8,128)(2,1)S(1)}, bf16[4,128,2,128]{3,1,0,2:T(8,128)(2,1)}, u32[]{:S(2)}) copy-start(bf16[4,128,2,128]{3,1,0,2:T(8,128)(2,1)} %copy.54) | copy-start | bytes 786436
Sparse Core Ops, SparseCore 0:
  11.0 64.7 all-gather.1
where the time goes:
time: 88.4 us; the launch traced here: 87.9 us
  waiting for transfers between devices  26.9 us (30%)
  between operations  14.2 us (16%)
  matrix products  12.4 us (14%)
  starting transfers between devices  12.2 us (14%)
  blocking collectives  12.2 us (14%)
  local copies, waits for them, and re-layouts  7.34 us (8%)
  other arithmetic  2.68 us (3%)
    all_to_all x1, blocking collectives, body(): lax.all_to_all(attended, 'seq', split_axis=0, concat_axis=1, tiled=True)  12.2 us
    all_to_all x1, waiting for transfers between devices, body(): lax.all_to_all(queries.reshape(tok_rows, head_count, HEAD_DIM), 'seq', sp...  9.69 us
    all_to_all x1, waiting for transfers between devices, body(): lax.all_to_all(values.reshape(tok_rows, head_count, HEAD_DIM), 'seq', spl...  8.6 us
    all_to_all x1, waiting for transfers between devices, body(): lax.all_to_all(keys.reshape(tok_rows, head_count, HEAD_DIM), 'seq', split...  8.56 us
    all_to_all x1, starting transfers between devices, body(): lax.all_to_all(queries.reshape(tok_rows, head_count, HEAD_DIM), 'seq', sp...  5.17 us
    sub x2, matrix products, causal_attention(): expons = jnp.exp(scores - highest)  4.46 us
    dot_general x2, matrix products, causal_attention(): jnp.einsum('hqk,khd->qhd', probs, head_values[:last_key], preferred_eleme...  4.31 us
    unnamed x9, local copies, waits for them, and re-layouts  4.18 us
  transfers between devices with their start and end apart: 4, of which 3 were waited for; matrix products, arithmetic and copies ran while one was open for 19% of the time, Pallas kernels for 0%

commit v1 on v0

v1 whole, which is shorter than its diff:
```python
import jax
import jax.numpy as jnp
from jax import lax
from jax.sharding import PartitionSpec as P

HEAD_DIM = 128


beta_first = 0.9
beta_second = 0.999
learning_rate = 0.1
weight_decay = 0.1
epsilon = 1e-08
step_count = 10.0


def adamw(master, moment, second, gradient):
    moment_new = beta_first * moment + (1.0 - beta_first) * gradient
    second_new = beta_second * second + (1.0 - beta_second) * gradient * gradient
    moment_hat = moment_new / (1.0 - beta_first**step_count)
    second_hat = second_new / (1.0 - beta_second**step_count)
    return master - learning_rate * (
        moment_hat / (jnp.sqrt(second_hat) + epsilon) + weight_decay * master
    )


def causal_attention(head_queries, head_keys, head_values):
    seq_length = head_queries.shape[0]
    block_rows = min(512, seq_length)
    results = []
    for first_row in range(0, seq_length, block_rows):
        last_key = first_row + block_rows
        query_block = head_queries[first_row:last_key]
        scores = jnp.einsum(
            "qhd,khd->hqk", query_block, head_keys[:last_key], preferred_element_type=jnp.float32
        )
        scores = scores * HEAD_DIM ** (-0.5)
        causal = (first_row + jnp.arange(block_rows))[:, None] >= jnp.arange(last_key)[None, :]
        scores = jnp.where(causal[None], scores, -jnp.inf)
        highest = jnp.max(scores, axis=2, keepdims=True)
        expons = jnp.exp(scores - highest)
        denominator = jnp.sum(expons, axis=2, keepdims=True)
        probs = (expons / denominator).astype(jnp.bfloat16)
        attended = jnp.einsum(
            "hqk,khd->qhd", probs, head_values[:last_key], preferred_element_type=jnp.float32
        )
        results.append(attended.astype(jnp.bfloat16))
    return jnp.concatenate(results, axis=0)


def swap(array, axis, count, distance):
    return lax.ppermute(array, axis, [(i, i ^ distance) for i in range(count)])


def make_body(seq_count, dp_count):
    def body(queries, keys, values, master, moment, second, gradient):
        tok_rows = queries.shape[1]
        feature_count = queries.shape[2]
        own_features = feature_count // seq_count
        out_features = master.shape[1]
        me = lax.axis_index("seq")
        place = lax.axis_index("dp")

        packed = jnp.stack([queries[0], keys[0], values[0]]).reshape(
            3, tok_rows, seq_count, own_features
        )
        packed = packed.transpose(2, 0, 1, 3)
        parts = []
        for distance in range(seq_count):
            part = lax.dynamic_index_in_dim(packed, me ^ distance, 0, keepdims=False)
            parts.append(swap(part, "seq", seq_count, distance) if distance else part)

        new_master = adamw(master, moment, second, gradient)
        rows = new_master.astype(jnp.bfloat16)[None]
        distance = 1
        while distance < dp_count:
            rows = jnp.concatenate([rows, swap(rows, "dp", dp_count, distance)], axis=0)
            distance *= 2
        rows = jnp.take(rows, place ^ jnp.arange(dp_count), axis=0)
        own_weight = rows.reshape(own_features, out_features)
        their_weight = swap(own_weight, "seq", seq_count, 1)

        whole = jnp.zeros((seq_count, 3, tok_rows, own_features), queries.dtype)
        for distance in range(seq_count):
            whole = lax.dynamic_update_index_in_dim(whole, parts[distance], me ^ distance, 0)
        whole = whole.transpose(1, 0, 2, 3).reshape(
            3, seq_count * tok_rows, own_features // HEAD_DIM, HEAD_DIM
        )
        attended = causal_attention(whole[0], whole[1], whole[2])

        pairs = attended.reshape(seq_count // 2, 2, tok_rows, own_features)
        core = me % 2
        kept = lax.dynamic_index_in_dim(pairs, core, 1, keepdims=False)
        given = lax.dynamic_index_in_dim(pairs, 1 - core, 1, keepdims=False)
        taken = swap(given, "seq", seq_count, 1)
        partial = jnp.einsum(
            "crf,fo->cro", kept, own_weight, preferred_element_type=jnp.float32
        ) + jnp.einsum("crf,fo->cro", taken, their_weight, preferred_element_type=jnp.float32)
        projected = lax.dynamic_index_in_dim(partial, me // 2, 0, keepdims=False)
        for distance in range(1, seq_count // 2):
            sent = lax.dynamic_index_in_dim(partial, (me // 2) ^ distance, 0, keepdims=False)
            got = swap(sent.astype(jnp.bfloat16), "seq", seq_count, 2 * distance)
            projected = projected + got.astype(jnp.float32)
        return (projected.astype(jnp.bfloat16)[None], new_master)

    return body


def solution(mesh):
    tokens = P("dp", "seq", None)
    rows = P(("seq", "dp"), None)
    return jax.shard_map(
        make_body(mesh.shape["seq"], mesh.shape["dp"]),
        mesh=mesh,
        in_specs=(tokens,) * 3 + (rows,) * 4,
        out_specs=(tokens, rows),
        check_vma=False,
    )
```

time: 88.4 us -> 149 us (1.69)
  local copies, waits for them, and re-layouts: 7.34 us -> 95.6 us
  between operations: 14.2 us -> 1.3 us
  blocking collectives: 12.2 us -> 0 us
  waiting for transfers between devices: 26.9 us -> 17.4 us
  other arithmetic: 2.68 us -> 6.89 us
  starting transfers between devices: 12.2 us -> 16.3 us
  matrix products: 12.4 us -> 10.8 us
    dynamic_update_slice x0 -> x8, local copies, waits for them, and re-layouts: none -> 70.5 us  [body(): lax.dynamic_update_index_in_dim(whole, parts[distance], me ^ distance, 0)]
    all_to_all x3 -> x0, waiting for transfers between devices: 26.8 us -> none  [the longest x1 9.69 us: body(): lax.all_to_all(queries.reshape(tok_rows, head_count, HEAD_DIM), 'seq', sp...]
    ppermute x0 -> x14, waiting for transfers between devices: none -> 17.4 us  [swap(): return lax.ppermute(array, axis, [(i, i ^ distance) for i in range(count)])]
    ppermute x0 -> x14, starting transfers between devices: none -> 16.3 us  [swap(): return lax.ppermute(array, axis, [(i, i ^ distance) for i in range(count)])]
    all_to_all x1 -> x0, blocking collectives: 12.2 us -> none  [body(): lax.all_to_all(attended, 'seq', split_axis=0, concat_axis=1, tiled=True)]
    all_to_all x3 -> x0, starting transfers between devices: 12.2 us -> none  [the longest x1 5.17 us: body(): lax.all_to_all(queries.reshape(tok_rows, head_count, HEAD_DIM), 'seq', sp...]
    broadcast_in_dim x0 -> x10, local copies, waits for them, and re-layouts: none -> 10.5 us  [the longest x7 10.1 us: body(): lax.dynamic_update_index_in_dim(whole, parts[distance], me ^ distance, 0)]
    another operation x0 -> x8, local copies, waits for them, and re-layouts: none -> 3.92 us
  transfers between devices with their start and end apart: 4 -> 14, of which waited for: 3 -> 4; matrix products, arithmetic and copies ran while one was open for 19% -> 72% of each run, Pallas kernels for 0% -> 0%
where the time goes in v1:
time: 149 us; the launch traced here: 148 us
  local copies, waits for them, and re-layouts  95.6 us (64%)
  waiting for transfers between devices  17.4 us (12%)
  starting transfers between devices  16.3 us (11%)
  matrix products  10.8 us (7%)
  other arithmetic  6.89 us (5%)
    dynamic_update_slice x8, local copies, waits for them, and re-layouts, body(): lax.dynamic_update_index_in_dim(whole, parts[distance], me ^ distance, 0)  70.5 us
    ppermute x14, waiting for transfers between devices, swap(): return lax.ppermute(array, axis, [(i, i ^ distance) for i in range(count)])  17.4 us
    ppermute x14, starting transfers between devices, swap(): return lax.ppermute(array, axis, [(i, i ^ distance) for i in range(count)])  16.3 us
    broadcast_in_dim x7, local copies, waits for them, and re-layouts, body(): lax.dynamic_update_index_in_dim(whole, parts[distance], me ^ distance, 0)  10.1 us
    dot_general x2, matrix products, causal_attention(): jnp.einsum('hqk,khd->qhd', probs, head_values[:last_key], preferred_eleme...  5.42 us
    sub x2, matrix products, causal_attention(): expons = jnp.exp(scores - highest)  4.55 us
    another operation x8, local copies, waits for them, and re-layouts  3.92 us
    unnamed x35, local copies, waits for them, and re-layouts  3.02 us
  transfers between devices with their start and end apart: 14, of which 4 were waited for; matrix products, arithmetic and copies ran while one was open for 72% of the time, Pallas kernels for 0%

profile of v1, /device:TPU:0, one launch (start us, length us, event | category | flops | bytes accessed | tf_op | source)
XLA Modules:
  0.0 148.4 jit_solution(13004751095887181041)
XLA Ops:
  0.7 1.4 copy.60
  2.0 1.3 copy.61
  4.1 0.8 copy.65
  5.5 2.6 %collective-permute-start.1 = (bf16[3,128,256]{2,1,0:T(8,128)(2,1)S(1)}, bf16[3,128,256]{2,1,0:T(8,128)(2,1)}, u32[]{:S(2)}, u32[]{:S(2)}) collective-permute-start(bf16[3,128,256]{2,1,0:T(8,128)(2,1)S(1)} %bitcast.93), channel_id=1, source_target_pairs={{0,8},{4,12},{8,0},{12,4},{16,24},{20,28},{24,16},{28,20},{1,9},{5... | collective-permute-start | bytes 589832 | tf_op jit(solution)/shard_map/ppermute | solution.py:52
  8.6 1.8 %collective-permute-start.3 = (bf16[3,128,256]{2,1,0:T(8,128)(2,1)S(1)}, bf16[3,128,256]{2,1,0:T(8,128)(2,1)}, u32[]{:S(2)}, u32[]{:S(2)}) collective-permute-start(bf16[3,128,256]{2,1,0:T(8,128)(2,1)S(1)} %bitcast.91), channel_id=1, source_target_pairs={{0,16},{4,20},{8,24},{12,28},{16,0},{20,4},{24,8},{28,12},{1,17},{... | collective-permute-start | bytes 589832 | tf_op jit(solution)/shard_map/ppermute | solution.py:52
  10.4 0.9 convert_bitcast_fusion
  11.3 1.6 %collective-permute-start.7 = (bf16[1,64,1024]{2,1,0:T(8,128)(2,1)S(1)}, bf16[1,64,1024]{2,1,0:T(8,128)(2,1)S(1)}, u32[]{:S(2)}, u32[]{:S(2)}) collective-permute-start(bf16[1,64,1024]{2,1,0:T(8,128)(2,1)S(1)} %get-tuple-element.2), channel_id=1, source_target_pairs={{0,1},{1,0},{2,3},{3,2},{4,5},{5,4},{6,7},{7,6},{8,9},{9,8},{10,11... | collective-permute-start | bytes 393224 | tf_op jit(solution)/shard_map/ppermute | solution.py:52
  12.9 1.2 iota_compare_fusion
  14.4 0.8 copy.73
  15.3 0.8 copy.75
  16.1 0.8 copy.77
  17.3 8.8 %dynamic_update_slice.25 = bf16[8,3,128,256]{2,0,3,1:T(8,128)(2,1)S(1)} dynamic-update-slice(bf16[8,3,128,256]{2,0,3,1:T(8,128)(2,1)S(1)} %broadcast_in_dim.84, bf16[1,3,128,256]{2,0,3,1:T(2,128)(2,1)S(1)} %copy.64, s32[]{:T(128)S(6)} %select_n.108, s32[]{:T(128)} %constant.119.clone.1, s32[]{:T(128)} %constant.119.clone.1, s32[]{:T(128)} %constant.119.clone.1) | dynamic-update-slice | bytes 393220 | tf_op jit(solution)/shard_map/jit(dynamic_update_index_in_dim)/dynamic_update_slice | solution.py:85
  26.1 0.8 iota_compare_fusion.1
  26.9 2.3 %collective-permute-start.5 = (bf16[3,128,256]{2,1,0:T(8,128)(2,1)}, bf16[3,128,256]{2,1,0:T(8,128)(2,1)}, u32[]{:S(2)}, u32[]{:S(2)}) collective-permute-start(bf16[3,128,256]{2,1,0:T(8,128)(2,1)} %bitcast.12), channel_id=1, source_target_pairs={{0,24},{4,28},{8,16},{12,20},{16,8},{20,12},{24,0},{28,4},{1,25},{... | collective-permute-start | bytes 589832 | tf_op jit(solution)/shard_map/ppermute | solution.py:52
  29.2 0.6 collective-permute-start.6
  29.8 0.7 pad_maximum_fusion.3
  30.5 1.2 copy.66
  31.8 1.3 copy.68
  33.1 2.7 %collective-permute-start.8 = (bf16[2,64,1024]{2,1,0:T(8,128)(2,1)}, bf16[2,64,1024]{2,1,0:T(8,128)(2,1)}, u32[]{:S(2)}, u32[]{:S(2)}) collective-permute-start(bf16[2,64,1024]{2,1,0:T(8,128)(2,1)} %pad_maximum_fusion.3), channel_id=1, source_target_pairs={{0,2},{1,3},{2,0},{3,1},{4,6},{5,7},{6,4},{7,5},{8,10},{9,11},{10,... | collective-permute-start | bytes 786440 | tf_op jit(solution)/shard_map/ppermute | solution.py:52
  35.7 1.2 copy.70
  37.0 1.3 copy.72
  38.2 4.5 %collective-permute-done.4 = bf16[3,128,256]{2,1,0:T(8,128)(2,1)} collective-permute-done((bf16[3,128,256]{2,1,0:T(8,128)(2,1)}, bf16[3,128,256]{2,1,0:T(8,128)(2,1)}, u32[]{:S(2)}, u32[]{:S(2)}) %collective-permute-start.4) | collective-permute-done | bytes 196640 | tf_op jit(solution)/shard_map/ppermute | solution.py:52
  42.8 1.2 copy.74
  44.0 1.9 %copy.76 = bf16[1,3,128,256]{2,0,3,1:T(2,128)(2,1)} copy(bf16[1,3,128,256]{3,2,1,0:T(8,128)(2,1)} %bitcast.13) | data formatting | bytes 393216 | tf_op jit(solution)/shard_map/jit(dynamic_update_index_in_dim)/broadcast_in_dim | solution.py:85
  46.0 1.9 %copy.78 = bf16[1,3,128,256]{2,0,3,1:T(2,128)(2,1)} copy(bf16[1,3,128,256]{3,2,1,0:T(8,128)(2,1)} %bitcast.15) | data formatting | bytes 393216 | tf_op jit(solution)/shard_map/jit(dynamic_update_index_in_dim)/broadcast_in_dim | solution.py:85
  47.9 8.8 %dynamic_update_slice.26 = bf16[8,3,128,256]{2,0,3,1:T(8,128)(2,1)S(1)} dynamic-update-slice(bf16[8,3,128,256]{2,0,3,1:T(8,128)(2,1)S(1)} %dynamic_update_slice.25, bf16[1,3,128,256]{2,0,3,1:T(2,128)(2,1)S(1)} %copy.66, s32[]{:T(128)S(6)} %select_n.109, s32[]{:T(128)} %constant.119.clone.1, s32[]{:T(128)} %constant.119.clone.1, s32[]{:T(128)} %constant.119.clone.1) | dynamic-update-slice | bytes 393220 | tf_op jit(solution)/shard_map/jit(dynamic_update_index_in_dim)/dynamic_update_slice | solution.py:85
  56.7 8.8 %dynamic_update_slice.27 = bf16[8,3,128,256]{2,0,3,1:T(8,128)(2,1)S(1)} dynamic-update-slice(bf16[8,3,128,256]{2,0,3,1:T(8,128)(2,1)S(1)} %dynamic_update_slice.26, bf16[1,3,128,256]{2,0,3,1:T(2,128)(2,1)S(1)} %copy.68, s32[]{:T(128)S(6)} %select_n.110, s32[]{:T(128)} %constant.119.clone.1, s32[]{:T(128)} %constant.119.clone.1, s32[]{:T(128)} %constant.119.clone.1) | dynamic-update-slice | bytes 393220 | tf_op jit(solution)/shard_map/jit(dynamic_update_index_in_dim)/dynamic_update_slice | solution.py:85
  65.5 8.8 %dynamic_update_slice.28 = bf16[8,3,128,256]{2,0,3,1:T(8,128)(2,1)S(1)} dynamic-update-slice(bf16[8,3,128,256]{2,0,3,1:T(8,128)(2,1)S(1)} %dynamic_update_slice.27, bf16[1,3,128,256]{2,0,3,1:T(2,128)(2,1)S(1)} %copy.70, s32[]{:T(128)S(6)} %select_n.111, s32[]{:T(128)} %constant.119.clone.1, s32[]{:T(128)} %constant.119.clone.1, s32[]{:T(128)} %constant.119.clone.1) | dynamic-update-slice | bytes 393220 | tf_op jit(solution)/shard_map/jit(dynamic_update_index_in_dim)/dynamic_update_slice | solution.py:85
  74.3 8.8 %dynamic_update_slice.29 = bf16[8,3,128,256]{2,0,3,1:T(8,128)(2,1)S(1)} dynamic-update-slice(bf16[8,3,128,256]{2,0,3,1:T(8,128)(2,1)S(1)} %dynamic_update_slice.28, bf16[1,3,128,256]{2,0,3,1:T(2,128)(2,1)S(1)} %copy.72, s32[]{:T(128)S(6)} %select_n.112, s32[]{:T(128)} %constant.119.clone.1, s32[]{:T(128)} %constant.119.clone.1, s32[]{:T(128)} %constant.119.clone.1) | dynamic-update-slice | bytes 393220 | tf_op jit(solution)/shard_map/jit(dynamic_update_index_in_dim)/dynamic_update_slice | solution.py:85
  83.1 8.8 %dynamic_update_slice.30 = bf16[8,3,128,256]{2,0,3,1:T(8,128)(2,1)S(1)} dynamic-update-slice(bf16[8,3,128,256]{2,0,3,1:T(8,128)(2,1)S(1)} %dynamic_update_slice.29, bf16[1,3,128,256]{2,0,3,1:T(2,128)(2,1)S(1)} %copy.74, s32[]{:T(128)S(6)} %select_n.113, s32[]{:T(128)} %constant.119.clone.1, s32[]{:T(128)} %constant.119.clone.1, s32[]{:T(128)} %constant.119.clone.1) | dynamic-update-slice | bytes 393220 | tf_op jit(solution)/shard_map/jit(dynamic_update_index_in_dim)/dynamic_update_slice | solution.py:85
  91.9 8.8 %dynamic_update_slice.31 = bf16[8,3,128,256]{2,0,3,1:T(8,128)(2,1)S(1)} dynamic-update-slice(bf16[8,3,128,256]{2,0,3,1:T(8,128)(2,1)S(1)} %dynamic_update_slice.30, bf16[1,3,128,256]{2,0,3,1:T(2,128)(2,1)S(1)} %copy-done, s32[]{:T(128)S(6)} %select_n.114, s32[]{:T(128)} %constant.119.clone.1, s32[]{:T(128)} %constant.119.clone.1, s32[]{:T(128)} %constant.119.clone.1) | dynamic-update-slice | bytes 393220 | tf_op jit(solution)/shard_map/jit(dynamic_update_index_in_dim)/dynamic_update_slice | solution.py:85
  100.7 9.0 %dynamic_update_slice.32 = bf16[8,3,128,256]{2,0,3,1:T(8,128)(2,1)S(1)} dynamic-update-slice(bf16[8,3,128,256]{2,0,3,1:T(8,128)(2,1)S(1)} %dynamic_update_slice.31, bf16[1,3,128,256]{2,0,3,1:T(2,128)(2,1)S(1)} %copy-done.1, s32[]{:T(128)S(6)} %select_n.115, s32[]{:T(128)} %constant.119.clone.1, s32[]{:T(128)} %constant.119.clone.1, s32[]{:T(128)} %constant.119.clone.1) | dynamic-update-slice | bytes 393220 | tf_op jit(solution)/shard_map/jit(dynamic_update_index_in_dim)/dynamic_update_slice | solution.py:85
  109.7 1.0 fusion.43
  110.8 1.1 reshape.144
  111.9 0.8 reshape.145
  112.7 0.8 slice.39
  114.1 1.0 fusion.46
  115.1 2.3 %fusion.10 = bf16[512,2,128]{0,2,1:T(8,128)(2,1)S(1)} fusion(bf16[512,2,128]{0,2,1:T(8,128)(2,1)S(1)} %copy-done.11, f32[2,512]{1,0:T(2,128)S(1)} %fusion.46, pred[512,512]{0,1:T(8,128)(4,1)} %iota_compare_fusion.1, bf16[512,2,128]{0,2,1:T(8,128)(2,1)} %copy-done.9, bf16[512,2,128]{0,2,1:T(8,128)(2,1)S(1)} %copy-done.10), kind=kOutput, calls=%fused_computation.21 | convolution fusion | flops 271189504 | bytes 1314816 | tf_op jit(solution)/shard_map/hqk,khd->qhd/dot_general | solution.py:44
  117.4 3.6 %fusion.45 = (f32[2,512]{1,0:T(2,128)S(1)}, f32[2,512,1024]{2,1,0:T(8,128)}) fusion(pred[512,1024]{1,0:T(8,128)(4,1)S(1)} %copy-done.5, bf16[512,2,128]{0,2,1:T(8,128)(2,1)S(1)} %reshape.146, bf16[1024,2,128]{0,2,1:T(8,128)(2,1)S(1)} %squeeze.52), kind=kOutput, calls=%fused_computation.80 | convolution fusion | flops 272630784 | bytes 5509120 | tf_op jit(solution)/shard_map/sub | solution.py:41
  121.0 3.1 %fusion.9 = bf16[512,2,128]{0,2,1:T(8,128)(2,1)S(1)} fusion(bf16[1024,2,128]{0,2,1:T(8,128)(2,1)S(1)} %squeeze.51, f32[2,512,1024]{2,1,0:T(8,128)} %get-tuple-element.24, f32[2,512]{1,0:T(2,128)S(1)} %get-tuple-element.23), kind=kOutput, calls=%fused_computation.20 | convolution fusion | flops 270663680 | bytes 4984832 | tf_op jit(solution)/shard_map/hqk,khd->qhd/dot_general | solution.py:44
  124.6 1.1 constant_dynamic-slice_fusion
  126.7 1.0 pad_maximum_fusion.2
  129.6 1.0 collective-permute-done.10
  131.1 1.6 %collective-permute-start.11 = (bf16[128,1024]{1,0:T(8,128)(2,1)S(1)}, bf16[128,1024]{1,0:T(8,128)(2,1)S(1)}, u32[]{:S(2)}, u32[]{:S(2)}) collective-permute-start(bf16[128,1024]{1,0:T(8,128)(2,1)S(1)} %get-tuple-element.4), channel_id=1, source_target_pairs={{0,8},{4,12},{8,0},{12,4},{16,24},{20,28},{24,16},{28,20},{1,9},{5... | collective-permute-start | bytes 786440 | tf_op jit(solution)/shard_map/ppermute | solution.py:52
  133.2 1.4 collective-permute-start.13
  134.7 5.6 %collective-permute-done.11 = bf16[128,1024]{1,0:T(8,128)(2,1)S(1)} collective-permute-done((bf16[128,1024]{1,0:T(8,128)(2,1)S(1)}, bf16[128,1024]{1,0:T(8,128)(2,1)S(1)}, u32[]{:S(2)}, u32[]{:S(2)}) %collective-permute-start.11) | collective-permute-done | bytes 262176 | tf_op jit(solution)/shard_map/ppermute | solution.py:52
  140.3 6.3 %collective-permute-done.12 = bf16[128,1024]{1,0:T(8,128)(2,1)S(1)} collective-permute-done((bf16[128,1024]{1,0:T(8,128)(2,1)S(1)}, bf16[128,1024]{1,0:T(8,128)(2,1)S(1)}, u32[]{:S(2)}, u32[]{:S(2)}) %collective-permute-start.12) | collective-permute-done | bytes 262176 | tf_op jit(solution)/shard_map/ppermute | solution.py:52
  146.6 1.8 %fusion.29 = bf16[1,128,1024]{2,1,0:T(8,128)(2,1)} fusion(bf16[128,1024]{1,0:T(8,128)(2,1)} %collective-permute-done.13, bf16[128,1024]{1,0:T(8,128)(2,1)S(1)} %collective-permute-done.12, bf16[128,1024]{1,0:T(8,128)(2,1)S(1)} %collective-permute-done.11, f32[4,128,1024]{2,1,0:T(8,128)S(1)} %convolution_add_fusion, s32[]{:T(128)S(6)} %select_n.127), kind=kLoop, calls=%fused_computation.49 | loop fusion | flops 917504 | bytes 1572868 | tf_op jit(solution)/shard_map/broadcast_in_dim | solution.py:104
  (76 shorter events, 7.5 us)
Async XLA Ops:
  0.6 2.7 %copy-start.4 = (bf16[1,128,2048]{2,1,0:T(8,128)(2,1)S(1)}, bf16[1,128,2048]{2,1,0:T(8,128)(2,1)}, u32[]{:S(2)}) copy-start(bf16[1,128,2048]{2,1,0:T(8,128)(2,1)} %param.9) | copy-start | bytes 1572868
  3.9 6.5 %copy-start.12 = (f32[64,1024]{1,0:T(8,128)S(1)}, f32[64,1024]{1,0:T(8,128)}, u32[]{:S(2)}) copy-start(f32[64,1024]{1,0:T(8,128)} %param.10) | copy-start | bytes 786436
  3.9 6.5 %copy-start.13 = (f32[64,1024]{1,0:T(8,128)S(1)}, f32[64,1024]{1,0:T(8,128)}, u32[]{:S(2)}) copy-start(f32[64,1024]{1,0:T(8,128)} %param.13) | copy-start | bytes 786436
  3.9 6.5 %copy-start.14 = (f32[64,1024]{1,0:T(8,128)S(1)}, f32[64,1024]{1,0:T(8,128)}, u32[]{:S(2)}) copy-start(f32[64,1024]{1,0:T(8,128)} %param.12) | copy-start | bytes 786436
  3.9 6.5 %copy-start.15 = (f32[64,1024]{1,0:T(8,128)S(1)}, f32[64,1024]{1,0:T(8,128)}, u32[]{:S(2)}) copy-start(f32[64,1024]{1,0:T(8,128)} %param.11) | copy-start | bytes 786436
  4.9 22.0 %collective-permute-start = (bf16[3,128,256]{2,1,0:T(8,128)(2,1)}, bf16[3,128,256]{2,1,0:T(8,128)(2,1)}, u32[]{:S(2)}, u32[]{:S(2)}) collective-permute-start(bf16[3,128,256]{2,1,0:T(8,128)(2,1)} %bitcast.2), channel_id=1, source_target_pairs={{0,4},{4,0},{8,12},{12,8},{16,20},{20,16},{24,28},{28,24},{1,5},{5... | collective-permute-start | bytes 589832 | tf_op jit(solution)/shard_map/ppermute | solution.py:52
  5.5 23.7 %collective-permute-start.1 = (bf16[3,128,256]{2,1,0:T(8,128)(2,1)S(1)}, bf16[3,128,256]{2,1,0:T(8,128)(2,1)}, u32[]{:S(2)}, u32[]{:S(2)}) collective-permute-start(bf16[3,128,256]{2,1,0:T(8,128)(2,1)S(1)} %bitcast.93), channel_id=1, source_target_pairs={{0,8},{4,12},{8,0},{12,4},{16,24},{20,28},{24,16},{28,20},{1,9},{5... | collective-permute-start | bytes 589832 | tf_op jit(solution)/shard_map/ppermute | solution.py:52
  8.2 24.8 %collective-permute-start.2 = (bf16[3,128,256]{2,1,0:T(8,128)(2,1)S(1)}, bf16[3,128,256]{2,1,0:T(8,128)(2,1)}, u32[]{:S(2)}, u32[]{:S(2)}) collective-permute-start(bf16[3,128,256]{2,1,0:T(8,128)(2,1)S(1)} %bitcast.92), channel_id=1, source_target_pairs={{0,12},{4,8},{8,4},{12,0},{16,28},{20,24},{24,20},{28,16},{1,13},{... | collective-permute-start | bytes 589832 | tf_op jit(solution)/shard_map/ppermute | solution.py:52
  8.6 28.4 %collective-permute-start.3 = (bf16[3,128,256]{2,1,0:T(8,128)(2,1)S(1)}, bf16[3,128,256]{2,1,0:T(8,128)(2,1)}, u32[]{:S(2)}, u32[]{:S(2)}) collective-permute-start(bf16[3,128,256]{2,1,0:T(8,128)(2,1)S(1)} %bitcast.91), channel_id=1, source_target_pairs={{0,16},{4,20},{8,24},{12,28},{16,0},{20,4},{24,8},{28,12},{1,17},{... | collective-permute-start | bytes 589832 | tf_op jit(solution)/shard_map/ppermute | solution.py:52
  11.3 18.5 %copy-start.2 = (bf16[1,64,1024]{2,1,0:T(8,128)(2,1)}, bf16[1,64,1024]{2,1,0:T(8,128)(2,1)S(1)}, u32[]{:S(2)}) copy-start(bf16[1,64,1024]{2,1,0:T(8,128)(2,1)S(1)} %get-tuple-element.2) | copy-start | bytes 393220
  11.3 15.6 %collective-permute-start.7 = (bf16[1,64,1024]{2,1,0:T(8,128)(2,1)S(1)}, bf16[1,64,1024]{2,1,0:T(8,128)(2,1)S(1)}, u32[]{:S(2)}, u32[]{:S(2)}) collective-permute-start(bf16[1,64,1024]{2,1,0:T(8,128)(2,1)S(1)} %get-tuple-element.2), channel_id=1, source_target_pairs={{0,1},{1,0},{2,3},{3,2},{4,5},{5,4},{6,7},{7,6},{8,9},{9,8},{10,11... | collective-permute-start | bytes 393224 | tf_op jit(solution)/shard_map/ppermute | solution.py:52
  26.9 3.6 %copy-start.6 = (bf16[1,64,1024]{2,1,0:T(8,128)(2,1)}, bf16[1,64,1024]{2,1,0:T(8,128)(2,1)S(1)}, u32[]{:S(2)}) copy-start(bf16[1,64,1024]{2,1,0:T(8,128)(2,1)S(1)} %collective-permute-done.7) | copy-start | bytes 393220
  26.9 15.8 %collective-permute-start.4 = (bf16[3,128,256]{2,1,0:T(8,128)(2,1)}, bf16[3,128,256]{2,1,0:T(8,128)(2,1)}, u32[]{:S(2)}, u32[]{:S(2)}) collective-permute-start(bf16[3,128,256]{2,1,0:T(8,128)(2,1)} %bitcast.10), channel_id=1, source_target_pairs={{0,20},{4,16},{8,28},{12,24},{16,4},{20,0},{24,12},{28,8},{1,21},{... | collective-permute-start | bytes 589832 | tf_op jit(solution)/shard_map/ppermute | solution.py:52
  26.9 17.1 %collective-permute-start.5 = (bf16[3,128,256]{2,1,0:T(8,128)(2,1)}, bf16[3,128,256]{2,1,0:T(8,128)(2,1)}, u32[]{:S(2)}, u32[]{:S(2)}) collective-permute-start(bf16[3,128,256]{2,1,0:T(8,128)(2,1)} %bitcast.12), channel_id=1, source_target_pairs={{0,24},{4,28},{8,16},{12,20},{16,8},{20,12},{24,0},{28,4},{1,25},{... | collective-permute-start | bytes 589832 | tf_op jit(solution)/shard_map/ppermute | solution.py:52
  29.2 16.8 %collective-permute-start.6 = (bf16[3,128,256]{2,1,0:T(8,128)(2,1)}, bf16[3,128,256]{2,1,0:T(8,128)(2,1)}, u32[]{:S(2)}, u32[]{:S(2)}) collective-permute-start(bf16[3,128,256]{2,1,0:T(8,128)(2,1)} %bitcast.14), channel_id=1, source_target_pairs={{0,28},{4,24},{8,20},{12,16},{16,12},{20,8},{24,4},{28,0},{1,29},{... | collective-permute-start | bytes 589832 | tf_op jit(solution)/shard_map/ppermute | solution.py:52
  33.1 93.7 %collective-permute-start.8 = (bf16[2,64,1024]{2,1,0:T(8,128)(2,1)}, bf16[2,64,1024]{2,1,0:T(8,128)(2,1)}, u32[]{:S(2)}, u32[]{:S(2)}) collective-permute-start(bf16[2,64,1024]{2,1,0:T(8,128)(2,1)} %pad_maximum_fusion.3), channel_id=1, source_target_pairs={{0,2},{1,3},{2,0},{3,1},{4,6},{5,7},{6,4},{7,5},{8,10},{9,11},{10,... | collective-permute-start | bytes 786440 | tf_op jit(solution)/shard_map/ppermute | solution.py:52
  56.7 35.2 %copy-start = (bf16[1,3,128,256]{2,0,3,1:T(2,128)(2,1)S(1)}, bf16[1,3,128,256]{2,0,3,1:T(2,128)(2,1)}, u32[]{:S(2)}) copy-start(bf16[1,3,128,256]{2,0,3,1:T(2,128)(2,1)} %copy.76) | copy-start | bytes 589828
  65.5 35.2 %copy-start.1 = (bf16[1,3,128,256]{2,0,3,1:T(2,128)(2,1)S(1)}, bf16[1,3,128,256]{2,0,3,1:T(2,128)(2,1)}, u32[]{:S(2)}) copy-start(bf16[1,3,128,256]{2,0,3,1:T(2,128)(2,1)} %copy.78) | copy-start | bytes 589828
  110.8 3.3 %copy-start.8 = (pred[512,512]{0,1:T(8,128)(4,1)S(1)}, pred[512,512]{0,1:T(8,128)(4,1)}, u32[]{:S(2)}) copy-start(pred[512,512]{0,1:T(8,128)(4,1)} %iota_compare_fusion.1) | copy-start | bytes 786436
  111.9 2.2 %copy-start.9 = (bf16[512,2,128]{0,2,1:T(8,128)(2,1)}, bf16[512,2,128]{0,2,1:T(8,128)(2,1)S(1)}, u32[]{:S(2)}) copy-start(bf16[512,2,128]{0,2,1:T(8,128)(2,1)S(1)} %reshape.144) | copy-start | bytes 786436
  112.7 1.4 copy-start.10
  114.1 1.0 copy-start.11
  115.1 2.3 %copy-start.5 = (pred[512,1024]{1,0:T(8,128)(4,1)S(1)}, pred[512,1024]{1,0:T(8,128)(4,1)}, u32[]{:S(2)}) copy-start(pred[512,1024]{1,0:T(8,128)(4,1)} %iota_compare_fusion) | copy-start | bytes 1572868
  124.5 2.2 %copy-start.3 = (bf16[1,64,1024]{2,1,0:T(8,128)(2,1)S(1)}, bf16[1,64,1024]{2,1,0:T(8,128)(2,1)}, u32[]{:S(2)}) copy-start(bf16[1,64,1024]{2,1,0:T(8,128)(2,1)} %copy-done.2) | copy-start | bytes 393220
  124.5 2.2 %copy-start.7 = (bf16[1,64,1024]{2,1,0:T(8,128)(2,1)S(1)}, bf16[1,64,1024]{2,1,0:T(8,128)(2,1)}, u32[]{:S(2)}) copy-start(bf16[1,64,1024]{2,1,0:T(8,128)(2,1)} %copy-done.6) | copy-start | bytes 393220
  126.6 2.9 %collective-permute-start.9 = (bf16[4,128,256]{2,1,0:T(8,128)(2,1)S(1)}, bf16[4,128,256]{2,1,0:T(8,128)(2,1)S(1)}, u32[]{:S(2)}, u32[]{:S(2)}) collective-permute-start(bf16[4,128,256]{2,1,0:T(8,128)(2,1)S(1)} %bitcast.90), channel_id=1, source_target_pairs={{0,4},{4,0},{8,12},{12,8},{16,20},{20,16},{24,28},{28,24},{1,5},{5... | collective-permute-start | bytes 786440 | tf_op jit(solution)/shard_map/ppermute | solution.py:52
  128.5 2.1 %collective-permute-start.10 = (bf16[256,1024]{1,0:T(8,128)(2,1)S(1)}, bf16[256,1024]{1,0:T(8,128)(2,1)S(1)}, u32[]{:S(2)}, u32[]{:S(2)}) collective-permute-start(bf16[256,1024]{1,0:T(8,128)(2,1)S(1)} %bitcast_select_fusion), channel_id=1, source_target_pairs={{0,4},{4,0},{8,12},{12,8},{16,20},{20,16},{24,28},{28,24},{1,5},{5... | collective-permute-start | bytes 1572872 | tf_op jit(solution)/shard_map/ppermute | solution.py:52
  131.1 9.2 %collective-permute-start.11 = (bf16[128,1024]{1,0:T(8,128)(2,1)S(1)}, bf16[128,1024]{1,0:T(8,128)(2,1)S(1)}, u32[]{:S(2)}, u32[]{:S(2)}) collective-permute-start(bf16[128,1024]{1,0:T(8,128)(2,1)S(1)} %get-tuple-element.4), channel_id=1, source_target_pairs={{0,8},{4,12},{8,0},{12,4},{16,24},{20,28},{24,16},{28,20},{1,9},{5... | collective-permute-start | bytes 786440 | tf_op jit(solution)/shard_map/ppermute | solution.py:52
  132.7 13.9 %collective-permute-start.12 = (bf16[128,1024]{1,0:T(8,128)(2,1)S(1)}, bf16[128,1024]{1,0:T(8,128)(2,1)S(1)}, u32[]{:S(2)}, u32[]{:S(2)}) collective-permute-start(bf16[128,1024]{1,0:T(8,128)(2,1)S(1)} %get-tuple-element.6), channel_id=1, source_target_pairs={{0,16},{4,20},{8,24},{12,28},{16,0},{20,4},{24,8},{28,12},{1,17},{... | collective-permute-start | bytes 786440 | tf_op jit(solution)/shard_map/ppermute | solution.py:52
  133.2 13.3 %collective-permute-start.13 = (bf16[128,1024]{1,0:T(8,128)(2,1)S(1)}, bf16[128,1024]{1,0:T(8,128)(2,1)}, u32[]{:S(2)}, u32[]{:S(2)}) collective-permute-start(bf16[128,1024]{1,0:T(8,128)(2,1)S(1)} %get-tuple-element.5), channel_id=1, source_target_pairs={{0,24},{4,28},{8,16},{12,20},{16,8},{20,12},{24,0},{28,4},{1,25},{... | collective-permute-start | bytes 786440 | tf_op jit(solution)/shard_map/ppermute | solution.py:52

commit v2 on v1

v2 whole, which is shorter than its diff:
```python
import functools
import math

import jax
import jax.numpy as jnp
from jax import lax
from jax.experimental import pallas as pl
from jax.experimental.pallas import tpu as pltpu
from jax.sharding import PartitionSpec as P

HEAD_DIM = 128
LANES = 128


beta_first = 0.9
beta_second = 0.999
learning_rate = 0.1
weight_decay = 0.1
epsilon = 1e-08
step_count = 10.0


def adamw(master, moment, second, gradient):
    moment_new = beta_first * moment + (1.0 - beta_first) * gradient
    second_new = beta_second * second + (1.0 - beta_second) * gradient * gradient
    moment_hat = moment_new / (1.0 - beta_first**step_count)
    second_hat = second_new / (1.0 - beta_second**step_count)
    return master - learning_rate * (
        moment_hat / (jnp.sqrt(second_hat) + epsilon) + weight_decay * master
    )


def swap(array, axis, count, distance):
    return lax.ppermute(array, axis, [(i, i ^ distance) for i in range(count)])


SMEM = pl.BlockSpec(memory_space=pltpu.SMEM)
VMEM = pl.BlockSpec(memory_space=pltpu.VMEM)
PARAMS = pltpu.CompilerParams(vmem_limit_bytes=32 * 1024 * 1024)


def pack_kernel(me_ref, *refs):
    arrays, parts = refs[:3], refs[3:]
    width = parts[0].shape[2]
    for distance, part in enumerate(parts):
        first = pl.multiple_of((me_ref[0] ^ distance) * width, width)
        for which, array in enumerate(arrays):
            part[which] = array[0, :, pl.ds(first, width)]


def pack(me, arrays, count):
    _, rows, features = arrays[0].shape
    part = jax.ShapeDtypeStruct((3, rows, features // count), arrays[0].dtype)
    size = 2 * 3 * rows * features * 2
    return pl.pallas_call(
        pack_kernel,
        out_shape=[part] * count,
        in_specs=[SMEM] + [VMEM] * 3,
        out_specs=[VMEM] * count,
        compiler_params=PARAMS,
        cost_estimate=pl.CostEstimate(flops=0, bytes_accessed=size, transcendentals=0),
        name="pack",
    )(me, *arrays)


def attend_kernel(count, block, me_ref, *refs):
    parts = refs[:count]
    kept, given, queries, keys, values, attended = refs[count:]
    rows = parts[0].shape[1]
    heads = values.shape[0]
    length = queries.shape[0]
    me = me_ref[0]
    for head in range(heads):
        values[head, :, HEAD_DIM:] = jnp.ones((length, LANES), values.dtype)
    for distance, part in enumerate(parts):
        at = pl.ds(pl.multiple_of((me ^ distance) * rows, rows), rows)
        queries[at, :] = part[0]
        keys[at, :] = part[1]
        for head in range(heads):
            values[head, at, :HEAD_DIM] = part[2, :, head * HEAD_DIM : (head + 1) * HEAD_DIM]
    scale = HEAD_DIM ** (-0.5) * math.log2(math.e)
    for first in range(0, length, block):
        last = first + block
        causal = lax.broadcasted_iota(jnp.int32, (block, block), 0) >= lax.broadcasted_iota(
            jnp.int32, (block, block), 1
        )
        for head in range(heads):
            columns = slice(head * HEAD_DIM, (head + 1) * HEAD_DIM)
            scores = lax.dot_general(
                queries[first:last, columns],
                keys[:last, columns],
                (((1,), (1,)), ((), ())),
                preferred_element_type=jnp.float32,
            )
            near = jnp.where(causal, scores[:, first:], -jnp.inf)
            highest = jnp.max(near, axis=1, keepdims=True)
            if first:
                far = scores[:, :first]
                highest = jnp.maximum(highest, jnp.max(far, axis=1, keepdims=True))
            expons = jnp.exp2((near - highest) * scale).astype(jnp.bfloat16)
            total = jnp.dot(expons, values[head, first:last], preferred_element_type=jnp.float32)
            if first:
                expons = jnp.exp2((far - highest) * scale).astype(jnp.bfloat16)
                total = total + jnp.dot(
                    expons, values[head, :first], preferred_element_type=jnp.float32
                )
            attended[first:last, columns] = (total[:, :HEAD_DIM] / total[:, HEAD_DIM:]).astype(
                attended.dtype
            )
    for distance in range(count // 2):
        pair = ((me // 2) ^ distance) * 2
        here, there = pair + me % 2, pair + 1 - me % 2
        at = slice(distance * rows, (distance + 1) * rows)
        kept[at, :] = attended[pl.ds(pl.multiple_of(here * rows, rows), rows), :]
        given[at, :] = attended[pl.ds(pl.multiple_of(there * rows, rows), rows), :]


def attend(me, parts):
    count = len(parts)
    _, rows, features = parts[0].shape
    length = count * rows
    heads = features // HEAD_DIM
    kind = parts[0].dtype
    half = jax.ShapeDtypeStruct((length // 2, features), kind)
    return pl.pallas_call(
        functools.partial(attend_kernel, count, min(256, length)),
        out_shape=[half, half],
        in_specs=[SMEM] + [VMEM] * count,
        out_specs=[VMEM] * 2,
        scratch_shapes=[
            pltpu.VMEM((length, features), kind),
            pltpu.VMEM((length, features), kind),
            pltpu.VMEM((heads, length, HEAD_DIM + LANES), kind),
            pltpu.VMEM((length, features), kind),
        ],
        compiler_params=PARAMS,
        cost_estimate=pl.CostEstimate(
            flops=4 * length * length * features,
            bytes_accessed=8 * length * features,
            transcendentals=length * length * heads // 2,
        ),
        name="attend",
    )(me, *parts)


def project_kernel(kept, taken, own_weight, their_weight, here, *sent):
    rows = here.shape[0]
    product = jnp.dot(kept[...], own_weight[...], preferred_element_type=jnp.float32)
    product += jnp.dot(taken[...], their_weight[...], preferred_element_type=jnp.float32)
    here[...] = product[:rows]
    for distance, block in enumerate(sent, 1):
        block[...] = product[distance * rows : (distance + 1) * rows].astype(block.dtype)


def project(kept, taken, own_weight, their_weight, rows):
    total, features = kept.shape
    outs = own_weight.shape[1]
    return pl.pallas_call(
        project_kernel,
        out_shape=[jax.ShapeDtypeStruct((rows, outs), jnp.float32)]
        + [jax.ShapeDtypeStruct((rows, outs), kept.dtype)] * (total // rows - 1),
        in_specs=[VMEM] * 4,
        out_specs=[VMEM] * (total // rows),
        compiler_params=PARAMS,
        cost_estimate=pl.CostEstimate(
            flops=4 * total * features * outs,
            bytes_accessed=4 * total * features + 4 * features * outs + 2 * total * outs,
            transcendentals=0,
        ),
        name="project",
    )(kept, taken, own_weight, their_weight)


def make_body(seq_count, dp_count):
    def body(queries, keys, values, master, moment, second, gradient):
        tok_rows = queries.shape[1]
        own_features = queries.shape[2] // seq_count
        out_features = master.shape[1]
        me = lax.axis_index("seq")
        place = lax.axis_index("dp")
        me_array = me.astype(jnp.int32).reshape(1)

        parts = pack(me_array, (queries, keys, values), seq_count)
        parts = [
            swap(part, "seq", seq_count, distance) if distance else part
            for distance, part in enumerate(parts)
        ]

        new_master = adamw(master, moment, second, gradient)
        rows = new_master.astype(jnp.bfloat16)[None]
        distance = 1
        while distance < dp_count:
            rows = jnp.concatenate([rows, swap(rows, "dp", dp_count, distance)], axis=0)
            distance *= 2
        rows = jnp.take(rows, place ^ jnp.arange(dp_count), axis=0)
        own_weight = rows.reshape(own_features, out_features)
        their_weight = swap(own_weight, "seq", seq_count, 1)

        kept, given = attend(me_array, parts)
        taken = swap(given, "seq", seq_count, 1)
        here, *sent = project(kept, taken, own_weight, their_weight, tok_rows)
        projected = here
        for distance, block in enumerate(sent, 1):
            projected += swap(block, "seq", seq_count, 2 * distance).astype(jnp.float32)
        return (projected.astype(jnp.bfloat16)[None], new_master)

    return body


def solution(mesh):
    tokens = P("dp", "seq", None)
    rows = P(("seq", "dp"), None)
    return jax.shard_map(
        make_body(mesh.shape["seq"], mesh.shape["dp"]),
        mesh=mesh,
        in_specs=(tokens,) * 3 + (rows,) * 4,
        out_specs=(tokens, rows),
        check_vma=False,
    )
```

time: 149 us -> 63.1 us (0.42)
  local copies, waits for them, and re-layouts: 95.6 us -> 2.58 us
  waiting for transfers between devices: 17.4 us -> 33.6 us
  matrix products: 10.8 us -> 0 us
  Pallas kernels: 0 us -> 3.64 us
    dynamic_update_slice x8 -> x0, local copies, waits for them, and re-layouts: 70.5 us -> none  [body(): lax.dynamic_update_index_in_dim(whole, parts[distance], me ^ distance, 0)]
    ppermute x14, waiting for transfers between devices: 17.4 us -> 33.6 us  [swap(): return lax.ppermute(array, axis, [(i, i ^ distance) for i in range(count)])]
    broadcast_in_dim x8 -> x0, local copies, waits for them, and re-layouts: 10.3 us -> none  [the longest x7 10.1 us: body(): lax.dynamic_update_index_in_dim(whole, parts[distance], me ^ distance, 0)]
    dot_general x4 -> x0, matrix products: 6.3 us -> none  [the longest x2 5.42 us: causal_attention(): jnp.einsum('hqk,khd->qhd', probs, head_values[:last_key], preferred_eleme...]
    sub x2 -> x0, matrix products: 4.55 us -> none  [causal_attention(): expons = jnp.exp(scores - highest)]
    another operation x8 -> x0, local copies, waits for them, and re-layouts: 3.92 us -> none
    slice x6 -> x0, local copies, waits for them, and re-layouts: 3.88 us -> none  [the longest x2 1.8 us: causal_attention(): head_keys[:last_key]]
    pallas_call x0 -> x3, Pallas kernels: none -> 3.64 us  [the longest x1 2.73 us: attend(): pl.pallas_call(functools.partial(attend_kernel, count, min(256, length)),...]
  transfers between devices with their start and end apart: 14 -> 14, of which waited for: 4 -> 5; matrix products, arithmetic and copies ran while one was open for 72% -> 7% of each run, Pallas kernels for 0% -> 5%
where the time goes in v2:
time: 63.1 us; the launch traced here: 62.8 us
  waiting for transfers between devices  33.6 us (53%)
  starting transfers between devices  16.2 us (26%)
  other arithmetic  6.1 us (10%)
  Pallas kernels  3.64 us (6%)
  local copies, waits for them, and re-layouts  2.58 us (4%)
  between operations  0.72 us (1%)
    ppermute x14, waiting for transfers between devices, swap(): return lax.ppermute(array, axis, [(i, i ^ distance) for i in range(count)])  33.6 us
    ppermute x14, starting transfers between devices, swap(): return lax.ppermute(array, axis, [(i, i ^ distance) for i in range(count)])  16.2 us
    pallas_call x1, Pallas kernels, attend(): pl.pallas_call(functools.partial(attend_kernel, count, min(256, length)),...  2.73 us
    broadcast_in_dim x1, other arithmetic, body(): rows = new_master.astype(jnp.bfloat16)[None]  2.19 us
    concatenate x2, other arithmetic, body(): rows = jnp.concatenate([rows, swap(rows, 'dp', dp_count, distance)], axis=0)  1.89 us
    gather x1, local copies, waits for them, and re-layouts, body(): rows = jnp.take(rows, place ^ jnp.arange(dp_count), axis=0)  1.37 us
  transfers between devices with their start and end apart: 14, of which 5 were waited for; matrix products, arithmetic and copies ran while one was open for 7% of the time, Pallas kernels for 5%

profile of v2, /device:TPU:0, one launch (start us, length us, event | category | flops | bytes accessed | tf_op | source)
XLA Modules:
  0.0 62.8 jit_solution(13923567239920876867)
XLA Ops:
  0.6 0.0 copy-start
  0.6 0.0 copy-start.1
  0.7 2.2 %convert_bitcast_fusion = (bf16[1,64,1024]{2,1,0:T(8,128)(2,1)S(1)}, f32[64,1024]{1,0:T(8,128)}) fusion(f32[64,1024]{1,0:T(8,128)} %param.10, f32[64,1024]{1,0:T(8,128)} %param.13, f32[64,1024]{1,0:T(8,128)} %param.12, f32[64,1024]{1,0:T(8,128)} %param.11), kind=kLoop, calls=%fused_computation.14 | loop fusion | flops 1048576 | bytes 1441792 | tf_op jit(solution)/shard_map/broadcast_in_dim | solution.py:190
  2.8 3.0 %collective-permute-start.8 = (bf16[1,64,1024]{2,1,0:T(8,128)(2,1)S(1)}, bf16[1,64,1024]{2,1,0:T(8,128)(2,1)}, u32[]{:S(2)}, u32[]{:S(2)}) collective-permute-start(bf16[1,64,1024]{2,1,0:T(8,128)(2,1)S(1)} %get-tuple-element.30), channel_id=1, source_target_pairs={{0,1},{1,0},{2,3},{3,2},{4,5},{5,4},{6,7},{7,6},{8,9},{9,8},{10,11... | collective-permute-start | bytes 393224 | tf_op jit(solution)/shard_map/ppermute | solution.py:34
  5.9 0.0 copy-done
  5.9 0.0 copy-done.1
  5.9 0.0 copy-start.2
  5.9 1.0 %copy-done.2 = bf16[1,128,2048]{2,1,0:T(8,128)(2,1)S(1)} copy-done((bf16[1,128,2048]{2,1,0:T(8,128)(2,1)S(1)}, bf16[1,128,2048]{2,1,0:T(8,128)(2,1)}, u32[]{:S(2)}) %copy-start.2) | copy-done | bytes 524312
  6.9 0.2 pack.1
  7.1 0.1 collective-permute-start
  7.2 1.6 %collective-permute-start.1 = (bf16[3,128,256]{2,1,0:T(8,128)(2,1)S(1)}, bf16[3,128,256]{2,1,0:T(8,128)(2,1)S(1)}, u32[]{:S(2)}, u32[]{:S(2)}) collective-permute-start(bf16[3,128,256]{2,1,0:T(8,128)(2,1)S(1)} %get-tuple-element.18), channel_id=1, source_target_pairs={{0,8},{4,12},{8,0},{12,4},{16,24},{20,28},{24,16},{28,20},{1,9},{5... | collective-permute-start | bytes 589832 | tf_op jit(solution)/shard_map/ppermute | solution.py:34
  8.8 0.3 collective-permute-start.2
  9.1 1.5 %collective-permute-start.3 = (bf16[3,128,256]{2,1,0:T(8,128)(2,1)S(1)}, bf16[3,128,256]{2,1,0:T(8,128)(2,1)S(1)}, u32[]{:S(2)}, u32[]{:S(2)}) collective-permute-start(bf16[3,128,256]{2,1,0:T(8,128)(2,1)S(1)} %get-tuple-element.20), channel_id=1, source_target_pairs={{0,16},{4,20},{8,24},{12,28},{16,0},{20,4},{24,8},{28,12},{1,17},{... | collective-permute-start | bytes 589832 | tf_op jit(solution)/shard_map/ppermute | solution.py:34
  10.6 0.0 collective-permute-done.8
  10.6 0.9 %pad_maximum_fusion.1 = bf16[2,64,1024]{2,1,0:T(8,128)(2,1)S(1)} fusion(bf16[1,64,1024]{2,1,0:T(8,128)(2,1)} %collective-permute-done.8, bf16[1,64,1024]{2,1,0:T(8,128)(2,1)S(1)} %get-tuple-element.30), kind=kLoop, calls=%fused_computation.12 | loop fusion | flops 131072 | bytes 524288 | tf_op jit(solution)/shard_map/concatenate | solution.py:193
  11.5 2.7 %collective-permute-start.9 = (bf16[2,64,1024]{2,1,0:T(8,128)(2,1)S(1)}, bf16[2,64,1024]{2,1,0:T(8,128)(2,1)S(1)}, u32[]{:S(2)}, u32[]{:S(2)}) collective-permute-start(bf16[2,64,1024]{2,1,0:T(8,128)(2,1)S(1)} %pad_maximum_fusion.1), channel_id=1, source_target_pairs={{0,2},{1,3},{2,0},{3,1},{4,6},{5,7},{6,4},{7,5},{8,10},{9,11},{10,... | collective-permute-start | bytes 786440 | tf_op jit(solution)/shard_map/ppermute | solution.py:34
  14.2 0.1 broadcast_in_dim.20
  14.3 0.1 broadcast_in_dim.21
  14.4 11.9 %collective-permute-done.9 = bf16[2,64,1024]{2,1,0:T(8,128)(2,1)S(1)} collective-permute-done((bf16[2,64,1024]{2,1,0:T(8,128)(2,1)S(1)}, bf16[2,64,1024]{2,1,0:T(8,128)(2,1)S(1)}, u32[]{:S(2)}, u32[]{:S(2)}) %collective-permute-start.9) | collective-permute-done | bytes 262176 | tf_op jit(solution)/shard_map/ppermute | solution.py:34
  26.3 0.2 collective-permute-start.4
  26.5 1.0 %pad_maximum_fusion = bf16[4,64,1024]{2,1,0:T(8,128)(2,1)S(1)} fusion(bf16[2,64,1024]{2,1,0:T(8,128)(2,1)S(1)} %collective-permute-done.9, bf16[1,64,1024]{2,1,0:T(8,128)(2,1)} %collective-permute-done.8, bf16[1,64,1024]{2,1,0:T(8,128)(2,1)S(1)} %get-tuple-element.30), kind=kLoop, calls=%fused_computation.1 | loop fusion | flops 524288 | bytes 1048576 | tf_op jit(solution)/shard_map/concatenate | solution.py:193
  27.4 1.4 %gather_fusion = bf16[4,64,1024]{2,1,0:T(8,128)(2,1)} fusion(bf16[4,64,1024]{2,1,0:T(8,128)(2,1)S(1)} %pad_maximum_fusion, s32[1024]{0:T(1024)S(1)} %pad_clamp_fusion), kind=kCustom, calls=%fused_computation | custom fusion | bytes 1048592 | tf_op jit(solution)/shard_map/jit(_take)/gather | solution.py:195
  28.8 0.0 collective-permute-done.refs_1_
  28.8 2.4 %collective-permute-start.5 = (bf16[3,128,256]{2,1,0:T(8,128)(2,1)S(1)}, bf16[3,128,256]{2,1,0:T(8,128)(2,1)S(1)}, u32[]{:S(2)}, u32[]{:S(2)}) collective-permute-start(bf16[3,128,256]{2,1,0:T(8,128)(2,1)S(1)} %get-tuple-element.22), channel_id=1, source_target_pairs={{0,24},{4,28},{8,16},{12,20},{16,8},{20,12},{24,0},{28,4},{1,25},{... | collective-permute-start | bytes 589832 | tf_op jit(solution)/shard_map/ppermute | solution.py:34
  31.2 0.0 collective-permute-done.1.refs_2_
  31.2 0.4 collective-permute-start.6
  31.6 1.2 %bitcast_select_fusion.own_weight = bf16[256,1024]{1,0:T(8,128)(2,1)S(1)} fusion(bf16[4,64,1024]{2,1,0:T(8,128)(2,1)} %gather_fusion, pred[256]{0:T(512)(128)(4,1)S(1)} %broadcast_in_dim.21), kind=kLoop, calls=%fused_computation.2 | loop fusion | flops 262144 | bytes 1048832 | tf_op jit(solution)/shard_map/jit(_take)/select_n | solution.py:195
  32.7 0.0 collective-permute-done.2.refs_3_
  32.7 0.4 collective-permute-start.10
  33.1 0.0 collective-permute-done.3.refs_4_
  33.1 8.6 %collective-permute-done.4.refs_5_ = bf16[3,128,256]{2,1,0:T(8,128)(2,1)S(1)} collective-permute-done((bf16[3,128,256]{2,1,0:T(8,128)(2,1)S(1)}, bf16[3,128,256]{2,1,0:T(8,128)(2,1)S(1)}, u32[]{:S(2)}, u32[]{:S(2)}) %collective-permute-start.4) | collective-permute-done | bytes 196640 | tf_op jit(solution)/shard_map/ppermute | solution.py:34
  41.7 0.0 collective-permute-done.5.refs_6_
  41.7 0.0 collective-permute-done.6.refs_7_
  41.7 2.7 %attend.1 = (bf16[512,256]{1,0:T(8,128)(2,1)S(1)}, bf16[512,256]{1,0:T(8,128)(2,1)S(1)}) custom-call(s32[1]{0:T(128)} %bitcast.me_ref, bf16[3,128,256]{2,1,0:T(8,128)(2,1)S(1)} %get-tuple-element.16.refs_0_, bf16[3,128,256]{2,1,0:T(8,128)(2,1)S(1)} %collective-permute-done.refs_1_, bf16[3,128,256]{2,1,0:T(8,128)(2,1)S(1)} %collective-permute-done.1.refs_2_, ...), custom_call_target="tpu_custom_call" | custom-call | flops 1073741824 | bytes 2097152 | tf_op jit(solution)/shard_map/attend/pallas_call | solution.py:125
  44.4 0.2 collective-permute-start.7
  44.6 1.4 %collective-permute-done.7.taken = bf16[512,256]{1,0:T(8,128)(2,1)S(1)} collective-permute-done((bf16[512,256]{1,0:T(8,128)(2,1)S(1)}, bf16[512,256]{1,0:T(8,128)(2,1)S(1)}, u32[]{:S(2)}, u32[]{:S(2)}) %collective-permute-start.7) | collective-permute-done | bytes 262176 | tf_op jit(solution)/shard_map/ppermute | solution.py:34
  46.0 0.0 collective-permute-done.10.their_weight
  46.0 0.7 %project.1 = (f32[128,1024]{1,0:T(8,128)S(1)}, bf16[128,1024]{1,0:T(8,128)(2,1)S(1)}, bf16[128,1024]{1,0:T(8,128)(2,1)S(1)}, bf16[128,1024]{1,0:T(8,128)(2,1)S(1)}) custom-call(bf16[512,256]{1,0:T(8,128)(2,1)S(1)} %get-tuple-element.24.kept, bf16[512,256]{1,0:T(8,128)(2,1)S(1)} %collective-permute-done.7.taken, ...), custom_call_target="tpu_custom_call" | custom-call | flops 536870912 | bytes 2621440 | tf_op jit(solution)/shard_map/project/pallas_call | solution.py:158
  46.7 1.6 %collective-permute-start.11 = (bf16[128,1024]{1,0:T(8,128)(2,1)S(1)}, bf16[128,1024]{1,0:T(8,128)(2,1)S(1)}, u32[]{:S(2)}, u32[]{:S(2)}) collective-permute-start(bf16[128,1024]{1,0:T(8,128)(2,1)S(1)} %get-tuple-element.27), channel_id=1, source_target_pairs={{0,8},{4,12},{8,0},{12,4},{16,24},{20,28},{24,16},{28,20},{1,9},{5... | collective-permute-start | bytes 786440 | tf_op jit(solution)/shard_map/ppermute | solution.py:34
  48.3 0.6 collective-permute-start.12
  48.9 1.4 %collective-permute-start.13 = (bf16[128,1024]{1,0:T(8,128)(2,1)S(1)}, bf16[128,1024]{1,0:T(8,128)(2,1)S(1)}, u32[]{:S(2)}, u32[]{:S(2)}) collective-permute-start(bf16[128,1024]{1,0:T(8,128)(2,1)S(1)} %get-tuple-element.29), channel_id=1, source_target_pairs={{0,24},{4,28},{8,16},{12,20},{16,8},{20,12},{24,0},{28,4},{1,25},{... | collective-permute-start | bytes 786440 | tf_op jit(solution)/shard_map/ppermute | solution.py:34
  50.3 5.7 %collective-permute-done.11 = bf16[128,1024]{1,0:T(8,128)(2,1)S(1)} collective-permute-done((bf16[128,1024]{1,0:T(8,128)(2,1)S(1)}, bf16[128,1024]{1,0:T(8,128)(2,1)S(1)}, u32[]{:S(2)}, u32[]{:S(2)}) %collective-permute-start.11) | collective-permute-done | bytes 262176 | tf_op jit(solution)/shard_map/ppermute | solution.py:34
  56.0 6.0 %collective-permute-done.12 = bf16[128,1024]{1,0:T(8,128)(2,1)S(1)} collective-permute-done((bf16[128,1024]{1,0:T(8,128)(2,1)S(1)}, bf16[128,1024]{1,0:T(8,128)(2,1)S(1)}, u32[]{:S(2)}, u32[]{:S(2)}) %collective-permute-start.12) | collective-permute-done | bytes 262176 | tf_op jit(solution)/shard_map/ppermute | solution.py:34
  62.0 0.0 collective-permute-done.13
  62.0 0.8 %fusion.6 = bf16[1,128,1024]{2,1,0:T(8,128)(2,1)} fusion(bf16[128,1024]{1,0:T(8,128)(2,1)S(1)} %collective-permute-done.13, bf16[128,1024]{1,0:T(8,128)(2,1)S(1)} %collective-permute-done.12, f32[128,1024]{1,0:T(8,128)S(1)} %get-tuple-element.26, bf16[128,1024]{1,0:T(8,128)(2,1)S(1)} %collective-permute-done.11), kind=kLoop, calls=%fused_computation.11 | loop fusion | flops 917504 | bytes 1572864 | tf_op jit(solution)/shard_map/broadcast_in_dim | solution.py:205
  (3 shorter events, 0.0 us)
Async XLA Ops:
  0.6 5.2 %copy-start = (bf16[1,128,2048]{2,1,0:T(8,128)(2,1)S(1)}, bf16[1,128,2048]{2,1,0:T(8,128)(2,1)}, u32[]{:S(2)}) copy-start(bf16[1,128,2048]{2,1,0:T(8,128)(2,1)} %refs_0_.1) | copy-start | bytes 1572868
  0.6 5.2 %copy-start.1 = (bf16[1,128,2048]{2,1,0:T(8,128)(2,1)S(1)}, bf16[1,128,2048]{2,1,0:T(8,128)(2,1)}, u32[]{:S(2)}) copy-start(bf16[1,128,2048]{2,1,0:T(8,128)(2,1)} %refs_1_.1) | copy-start | bytes 1572868
  2.8 7.8 %collective-permute-start.8 = (bf16[1,64,1024]{2,1,0:T(8,128)(2,1)S(1)}, bf16[1,64,1024]{2,1,0:T(8,128)(2,1)}, u32[]{:S(2)}, u32[]{:S(2)}) collective-permute-start(bf16[1,64,1024]{2,1,0:T(8,128)(2,1)S(1)} %get-tuple-element.30), channel_id=1, source_target_pairs={{0,1},{1,0},{2,3},{3,2},{4,5},{5,4},{6,7},{7,6},{8,9},{9,8},{10,11... | collective-permute-start | bytes 393224 | tf_op jit(solution)/shard_map/ppermute | solution.py:34
  5.9 1.0 %copy-start.2 = (bf16[1,128,2048]{2,1,0:T(8,128)(2,1)S(1)}, bf16[1,128,2048]{2,1,0:T(8,128)(2,1)}, u32[]{:S(2)}) copy-start(bf16[1,128,2048]{2,1,0:T(8,128)(2,1)} %refs_2_.1) | copy-start | bytes 1572868
  7.1 21.7 %collective-permute-start = (bf16[3,128,256]{2,1,0:T(8,128)(2,1)S(1)}, bf16[3,128,256]{2,1,0:T(8,128)(2,1)S(1)}, u32[]{:S(2)}, u32[]{:S(2)}) collective-permute-start(bf16[3,128,256]{2,1,0:T(8,128)(2,1)S(1)} %get-tuple-element.17), channel_id=1, source_target_pairs={{0,4},{4,0},{8,12},{12,8},{16,20},{20,16},{24,28},{28,24},{1,5},{5... | collective-permute-start | bytes 589832 | tf_op jit(solution)/shard_map/ppermute | solution.py:34
  7.2 24.0 %collective-permute-start.1 = (bf16[3,128,256]{2,1,0:T(8,128)(2,1)S(1)}, bf16[3,128,256]{2,1,0:T(8,128)(2,1)S(1)}, u32[]{:S(2)}, u32[]{:S(2)}) collective-permute-start(bf16[3,128,256]{2,1,0:T(8,128)(2,1)S(1)} %get-tuple-element.18), channel_id=1, source_target_pairs={{0,8},{4,12},{8,0},{12,4},{16,24},{20,28},{24,16},{28,20},{1,9},{5... | collective-permute-start | bytes 589832 | tf_op jit(solution)/shard_map/ppermute | solution.py:34
  8.8 24.0 %collective-permute-start.2 = (bf16[3,128,256]{2,1,0:T(8,128)(2,1)S(1)}, bf16[3,128,256]{2,1,0:T(8,128)(2,1)S(1)}, u32[]{:S(2)}, u32[]{:S(2)}) collective-permute-start(bf16[3,128,256]{2,1,0:T(8,128)(2,1)S(1)} %get-tuple-element.19), channel_id=1, source_target_pairs={{0,12},{4,8},{8,4},{12,0},{16,28},{20,24},{24,20},{28,16},{1,13},{... | collective-permute-start | bytes 589832 | tf_op jit(solution)/shard_map/ppermute | solution.py:34
  9.1 24.0 %collective-permute-start.3 = (bf16[3,128,256]{2,1,0:T(8,128)(2,1)S(1)}, bf16[3,128,256]{2,1,0:T(8,128)(2,1)S(1)}, u32[]{:S(2)}, u32[]{:S(2)}) collective-permute-start(bf16[3,128,256]{2,1,0:T(8,128)(2,1)S(1)} %get-tuple-element.20), channel_id=1, source_target_pairs={{0,16},{4,20},{8,24},{12,28},{16,0},{20,4},{24,8},{28,12},{1,17},{... | collective-permute-start | bytes 589832 | tf_op jit(solution)/shard_map/ppermute | solution.py:34
  11.5 14.7 %collective-permute-start.9 = (bf16[2,64,1024]{2,1,0:T(8,128)(2,1)S(1)}, bf16[2,64,1024]{2,1,0:T(8,128)(2,1)S(1)}, u32[]{:S(2)}, u32[]{:S(2)}) collective-permute-start(bf16[2,64,1024]{2,1,0:T(8,128)(2,1)S(1)} %pad_maximum_fusion.1), channel_id=1, source_target_pairs={{0,2},{1,3},{2,0},{3,1},{4,6},{5,7},{6,4},{7,5},{8,10},{9,11},{10,... | collective-permute-start | bytes 786440 | tf_op jit(solution)/shard_map/ppermute | solution.py:34
  26.3 15.4 %collective-permute-start.4 = (bf16[3,128,256]{2,1,0:T(8,128)(2,1)S(1)}, bf16[3,128,256]{2,1,0:T(8,128)(2,1)S(1)}, u32[]{:S(2)}, u32[]{:S(2)}) collective-permute-start(bf16[3,128,256]{2,1,0:T(8,128)(2,1)S(1)} %get-tuple-element.21), channel_id=1, source_target_pairs={{0,20},{4,16},{8,28},{12,24},{16,4},{20,0},{24,12},{28,8},{1,21},{... | collective-permute-start | bytes 589832 | tf_op jit(solution)/shard_map/ppermute | solution.py:34
  28.8 12.9 %collective-permute-start.5 = (bf16[3,128,256]{2,1,0:T(8,128)(2,1)S(1)}, bf16[3,128,256]{2,1,0:T(8,128)(2,1)S(1)}, u32[]{:S(2)}, u32[]{:S(2)}) collective-permute-start(bf16[3,128,256]{2,1,0:T(8,128)(2,1)S(1)} %get-tuple-element.22), channel_id=1, source_target_pairs={{0,24},{4,28},{8,16},{12,20},{16,8},{20,12},{24,0},{28,4},{1,25},{... | collective-permute-start | bytes 589832 | tf_op jit(solution)/shard_map/ppermute | solution.py:34
  31.2 10.5 %collective-permute-start.6 = (bf16[3,128,256]{2,1,0:T(8,128)(2,1)S(1)}, bf16[3,128,256]{2,1,0:T(8,128)(2,1)S(1)}, u32[]{:S(2)}, u32[]{:S(2)}) collective-permute-start(bf16[3,128,256]{2,1,0:T(8,128)(2,1)S(1)} %get-tuple-element.23), channel_id=1, source_target_pairs={{0,28},{4,24},{8,20},{12,16},{16,12},{20,8},{24,4},{28,0},{1,29},{... | collective-permute-start | bytes 589832 | tf_op jit(solution)/shard_map/ppermute | solution.py:34
  32.7 13.3 %collective-permute-start.10 = (bf16[256,1024]{1,0:T(8,128)(2,1)S(1)}, bf16[256,1024]{1,0:T(8,128)(2,1)S(1)}, u32[]{:S(2)}, u32[]{:S(2)}) collective-permute-start(bf16[256,1024]{1,0:T(8,128)(2,1)S(1)} %bitcast_select_fusion.own_weight), channel_id=1, source_target_pairs={{0,4},{4,0},{8,12},{12,8},{16,20},{20,16},{24,28},{28,24},{1,5},{5... | collective-permute-start | bytes 1572872 | tf_op jit(solution)/shard_map/ppermute | solution.py:34
  44.4 1.6 %collective-permute-start.7 = (bf16[512,256]{1,0:T(8,128)(2,1)S(1)}, bf16[512,256]{1,0:T(8,128)(2,1)S(1)}, u32[]{:S(2)}, u32[]{:S(2)}) collective-permute-start(bf16[512,256]{1,0:T(8,128)(2,1)S(1)} %get-tuple-element.25), channel_id=1, source_target_pairs={{0,4},{4,0},{8,12},{12,8},{16,20},{20,16},{24,28},{28,24},{1,5},{5... | collective-permute-start | bytes 786440 | tf_op jit(solution)/shard_map/ppermute | solution.py:34
  46.7 9.2 %collective-permute-start.11 = (bf16[128,1024]{1,0:T(8,128)(2,1)S(1)}, bf16[128,1024]{1,0:T(8,128)(2,1)S(1)}, u32[]{:S(2)}, u32[]{:S(2)}) collective-permute-start(bf16[128,1024]{1,0:T(8,128)(2,1)S(1)} %get-tuple-element.27), channel_id=1, source_target_pairs={{0,8},{4,12},{8,0},{12,4},{16,24},{20,28},{24,16},{28,20},{1,9},{5... | collective-permute-start | bytes 786440 | tf_op jit(solution)/shard_map/ppermute | solution.py:34
  48.3 13.7 %collective-permute-start.12 = (bf16[128,1024]{1,0:T(8,128)(2,1)S(1)}, bf16[128,1024]{1,0:T(8,128)(2,1)S(1)}, u32[]{:S(2)}, u32[]{:S(2)}) collective-permute-start(bf16[128,1024]{1,0:T(8,128)(2,1)S(1)} %get-tuple-element.28), channel_id=1, source_target_pairs={{0,16},{4,20},{8,24},{12,28},{16,0},{20,4},{24,8},{28,12},{1,17},{... | collective-permute-start | bytes 786440 | tf_op jit(solution)/shard_map/ppermute | solution.py:34
  48.9 13.1 %collective-permute-start.13 = (bf16[128,1024]{1,0:T(8,128)(2,1)S(1)}, bf16[128,1024]{1,0:T(8,128)(2,1)S(1)}, u32[]{:S(2)}, u32[]{:S(2)}) collective-permute-start(bf16[128,1024]{1,0:T(8,128)(2,1)S(1)} %get-tuple-element.29), channel_id=1, source_target_pairs={{0,24},{4,28},{8,16},{12,20},{16,8},{20,12},{24,0},{28,4},{1,25},{... | collective-permute-start | bytes 786440 | tf_op jit(solution)/shard_map/ppermute | solution.py:34

commit v3 on v1

v3 whole, which is shorter than its diff:
```python
import functools
import math

import jax
import jax.numpy as jnp
from jax import lax
from jax.experimental import pallas as pl
from jax.experimental.pallas import tpu as pltpu
from jax.sharding import PartitionSpec as P

HEAD_DIM = 128
LANES = 128


beta_first = 0.9
beta_second = 0.999
learning_rate = 0.1
weight_decay = 0.1
epsilon = 1e-08
step_count = 10.0


def adamw(master, moment, second, gradient):
    moment_new = beta_first * moment + (1.0 - beta_first) * gradient
    second_new = beta_second * second + (1.0 - beta_second) * gradient * gradient
    moment_hat = moment_new / (1.0 - beta_first**step_count)
    second_hat = second_new / (1.0 - beta_second**step_count)
    return master - learning_rate * (
        moment_hat / (jnp.sqrt(second_hat) + epsilon) + weight_decay * master
    )


def swap(array, axis, count, distance):
    return lax.ppermute(array, axis, [(i, i ^ distance) for i in range(count)])


SMEM = pl.BlockSpec(memory_space=pltpu.SMEM)
VMEM = pl.BlockSpec(memory_space=pltpu.VMEM)
HBM = pl.BlockSpec(memory_space=pltpu.HBM)
PARAMS = pltpu.CompilerParams(vmem_limit_bytes=32 * 1024 * 1024)


def in_hbm(array):
    return pltpu.with_memory_space_constraint(array, pltpu.HBM)


def like(shape, array):
    return jax.ShapeDtypeStruct(shape, array.dtype)


def cost(moved, flops=0, transcendentals=0):
    return pl.CostEstimate(
        flops=flops, bytes_accessed=moved, transcendentals=transcendentals
    )


def pack_kernel(me_ref, queries, keys, values, *refs):
    parts, sems = refs[:-1], refs[-1]
    chips = len(parts) // 2
    width = parts[0].shape[1]
    copies = []
    for which, array in enumerate((keys, values, queries)):
        for distance in range(chips):
            chip = (me_ref[0] // 2) ^ distance
            at = pl.ds(pl.multiple_of(chip * width, width), width)
            part = parts[distance] if which == 2 else parts[chips + distance].at[which]
            sem = sems.at[which * chips + distance]
            copies.append(pltpu.make_async_copy(array.at[0, :, at], part, sem))
    for copy in copies:
        copy.start()
    for copy in copies:
        copy.wait()


def pack(me, queries, keys, values, chips):
    _, rows, features = queries.shape
    width = features // chips
    parts = pl.pallas_call(
        pack_kernel,
        out_shape=[like((rows, width), queries)] * chips
        + [like((2, rows, width), queries)] * chips,
        in_specs=[SMEM] + [HBM] * 3,
        out_specs=[VMEM] * (2 * chips),
        scratch_shapes=[pltpu.SemaphoreType.DMA((3 * chips,))],
        compiler_params=PARAMS,
        cost_estimate=cost(12 * rows * features),
        name="pack",
    )(me, *map(in_hbm, (queries, keys, values)))
    return parts[:chips], parts[chips:]


def update_kernel(*refs):
    arrays, (new_master, weight), held, sems = refs[:4], refs[4:6], refs[6], refs[7]
    copies = [
        pltpu.make_async_copy(array, held.at[index], sems.at[index])
        for index, array in enumerate(arrays)
    ]
    for copy in copies:
        copy.start()
    for copy in copies:
        copy.wait()
    result = adamw(held[0], held[1], held[2], held[3])
    new_master[...] = result
    weight[...] = result.astype(weight.dtype)


def update(*arrays):
    shape, kind = arrays[0].shape, arrays[0].dtype
    return pl.pallas_call(
        update_kernel,
        out_shape=[like(shape, arrays[0]), jax.ShapeDtypeStruct(shape, jnp.bfloat16)],
        in_specs=[HBM] * 4,
        out_specs=[VMEM] * 2,
        scratch_shapes=[pltpu.VMEM((4, *shape), kind), pltpu.SemaphoreType.DMA((4,))],
        compiler_params=PARAMS,
        cost_estimate=cost(22 * arrays[0].size),
        name="update",
    )(*map(in_hbm, arrays))


def merge_kernel(index_ref, *refs):
    pieces, whole = refs[:-1], refs[-1]
    for distance, piece in enumerate(pieces):
        whole[:, index_ref[0] ^ distance] = piece[...]


def merge(index, pieces):
    shape = (pieces[0].shape[0], len(pieces)) + pieces[0].shape[1:]
    return pl.pallas_call(
        merge_kernel,
        out_shape=like(shape, pieces[0]),
        in_specs=[SMEM] + [VMEM] * len(pieces),
        out_specs=VMEM,
        compiler_params=PARAMS,
        cost_estimate=cost(4 * len(pieces) * pieces[0].size),
        name="merge",
    )(index, *pieces)


def stack_kernel(*refs):
    pieces, stacked = refs[:-1], refs[-1]
    for index, piece in enumerate(pieces):
        stacked[index] = piece[...]


def stack(pieces):
    return pl.pallas_call(
        stack_kernel,
        out_shape=like((len(pieces), *pieces[0].shape), pieces[0]),
        in_specs=[VMEM] * len(pieces),
        out_specs=VMEM,
        compiler_params=PARAMS,
        cost_estimate=cost(4 * len(pieces) * pieces[0].size),
        name="stack",
    )(*pieces)


def gather_kernel(me_ref, own, other, keys, values):
    chips, _, rows, _ = own.shape
    heads, length, _ = values.shape
    for head in range(heads):
        values[head, :, HEAD_DIM:] = jnp.ones((length, LANES), values.dtype)
    for distance in range(chips):
        for core, pair in enumerate((own, other)):
            block = me_ref[0] ^ (2 * distance + core)
            at = pl.ds(pl.multiple_of(block * rows, rows), rows)
            keys[at, :] = pair[distance, 0]
            for head in range(heads):
                values[head, at, :HEAD_DIM] = pair[
                    distance, 1, :, head * HEAD_DIM : (head + 1) * HEAD_DIM
                ]


def gather(me, own, other):
    chips, _, rows, width = own.shape
    length = 2 * chips * rows
    return pl.pallas_call(
        gather_kernel,
        out_shape=[
            like((length, width), own),
            like((width // HEAD_DIM, length, HEAD_DIM + LANES), own),
        ],
        in_specs=[SMEM] + [VMEM] * 2,
        out_specs=[VMEM] * 2,
        compiler_params=PARAMS,
        cost_estimate=cost(10 * length * width),
        name="gather",
    )(me, own, other)


def attend_kernel(chips, me_ref, *refs):
    parts, (keys, values, attended, queries, result) = refs[:chips], refs[chips:]
    rows, width = parts[0].shape
    near = 2 * rows
    chip, core = me_ref[0] // 2, me_ref[0] % 2
    for distance, part in enumerate(parts):
        at = pl.ds(pl.multiple_of((chip ^ distance) * rows, rows), rows)
        queries[at, :] = part[...]
    causal = core * rows + lax.broadcasted_iota(
        jnp.int32, (rows, near), 0
    ) >= lax.broadcasted_iota(jnp.int32, (rows, near), 1)
    scale = HEAD_DIM ** (-0.5) * math.log2(math.e)
    for head in range(width // HEAD_DIM):
        columns = slice(head * HEAD_DIM, (head + 1) * HEAD_DIM)
        scores = []
        for c in range(chips):
            score = lax.dot_general(
                queries[c * rows :, columns],
                keys[c * near : (c + 1) * near, columns],
                (((1,), (1,)), ((), ())),
                preferred_element_type=jnp.float32,
            )
            masked = jnp.where(causal, score[:rows], -jnp.inf)
            scores.append(jnp.concatenate([masked, score[rows:]], axis=0) if c < chips - 1 else masked)
        highest = []
        for block in range(chips):
            best = scores[0][block * rows : (block + 1) * rows]
            for c in range(1, block + 1):
                best = jnp.maximum(best, scores[c][(block - c) * rows : (block - c + 1) * rows])
            highest.append(jnp.max(best, axis=1, keepdims=True))
        highest = jnp.concatenate(highest, axis=0)
        totals = None
        for c in range(chips):
            expons = jnp.exp2((scores[c] - highest[c * rows :]) * scale).astype(jnp.bfloat16)
            total = jnp.dot(
                expons, values[head, c * near : (c + 1) * near], preferred_element_type=jnp.float32
            )
            if c:
                total += totals[rows:]
            totals = total
            result[c * rows : (c + 1) * rows, columns] = (
                totals[:rows, :HEAD_DIM] / totals[:rows, HEAD_DIM:]
            ).astype(result.dtype)
    half = width // 2
    for distance in range(chips):
        at = pl.ds(pl.multiple_of((chip ^ distance) * rows, rows), rows)
        for part in range(2):
            attended[part, distance * rows : (distance + 1) * rows, :] = result[
                at, part * half : (part + 1) * half
            ]


def attend(me, parts, keys, values):
    chips = len(parts)
    rows, width = parts[0].shape
    length = keys.shape[0]
    total = chips * rows
    return pl.pallas_call(
        functools.partial(attend_kernel, chips),
        out_shape=like((2, total, width // 2), keys),
        in_specs=[SMEM] + [VMEM] * (chips + 2),
        out_specs=VMEM,
        scratch_shapes=[pltpu.VMEM((total, width), keys.dtype)] * 2,
        compiler_params=PARAMS,
        cost_estimate=cost(
            6 * length * width + 4 * total * width,
            4 * total * length * width,
            total * length * (width // HEAD_DIM),
        ),
        name="attend",
    )(me, *parts, keys, values)


def project_kernel(me_ref, attended, own_weight, their_weight, here, *sent):
    rows = here.shape[0]
    core = me_ref[0] % 2
    product = jnp.dot(attended[core], own_weight[...], preferred_element_type=jnp.float32)
    product += jnp.dot(attended[1 - core], their_weight[...], preferred_element_type=jnp.float32)
    here[...] = product[:rows]
    for distance, block in enumerate(sent, 1):
        block[...] = product[distance * rows : (distance + 1) * rows].astype(block.dtype)


def project(me, attended, own_weight, their_weight, rows):
    _, total, features = attended.shape
    outs = own_weight.shape[1]
    return pl.pallas_call(
        project_kernel,
        out_shape=[jax.ShapeDtypeStruct((rows, outs), jnp.float32)]
        + [like((rows, outs), attended)] * (total // rows - 1),
        in_specs=[SMEM] + [VMEM] * 3,
        out_specs=[VMEM] * (total // rows),
        compiler_params=PARAMS,
        cost_estimate=cost(
            4 * total * features + 4 * features * outs + 2 * total * outs,
            4 * total * features * outs,
        ),
        name="project",
    )(me, attended, own_weight, their_weight)


def make_body(seq_count, dp_count):
    chips = seq_count // 2

    def body(queries, keys, values, master, moment, second, gradient):
        own_features = queries.shape[2] // seq_count
        out_features = master.shape[1]
        me = lax.axis_index("seq").astype(jnp.int32).reshape(1)
        place = lax.axis_index("dp").astype(jnp.int32)

        query_parts, pair_parts = pack(me, queries, keys, values, chips)
        pairs = [pair_parts[0]]
        pairs += [swap(pair_parts[d], "seq", seq_count, 2 * d) for d in range(1, chips)]

        state, _ = lax.optimization_barrier(((master, moment, second, gradient), pair_parts))
        new_master, weight = update(*state)
        weight = weight[None]
        distance = dp_count // 2
        while distance > 1:
            theirs = swap(weight, "dp", dp_count, distance)
            pairs, theirs = lax.optimization_barrier((pairs, theirs))
            weight = merge((place // distance % 2).reshape(1), [weight, theirs])
            weight = weight.reshape(-1, *weight.shape[2:])
            distance //= 2
        theirs = swap(weight, "dp", dp_count, 1)
        own_pairs = stack(pairs)
        other_pairs = swap(own_pairs, "seq", seq_count, 1)
        sent, _ = lax.optimization_barrier((query_parts[1:], pairs))
        own_queries = [query_parts[0]]
        own_queries += [swap(part, "seq", seq_count, 2 * d) for d, part in enumerate(sent, 1)]
        own_queries, other_pairs, theirs = lax.optimization_barrier(
            (own_queries, other_pairs, theirs)
        )
        weight = merge((place % 2).reshape(1), [weight, theirs])
        own_weight = weight.reshape(own_features, out_features)
        their_weight = swap(own_weight, "seq", seq_count, 1)

        all_keys, all_values = gather(me, own_pairs, other_pairs)
        attended = attend(me, own_queries, all_keys, all_values)
        here, *sent = project(me, attended, own_weight, their_weight, queries.shape[1])
        projected = here
        for d, block in enumerate(sent, 1):
            projected += swap(block, "seq", seq_count, 2 * d).astype(jnp.float32)
        return (projected.astype(jnp.bfloat16)[None], new_master)

    return body


def solution(mesh):
    tokens = P("dp", "seq", None)
    rows = P(("seq", "dp"), None)
    return jax.shard_map(
        make_body(mesh.shape["seq"], mesh.shape["dp"]),
        mesh=mesh,
        in_specs=(tokens,) * 3 + (rows,) * 4,
        out_specs=(tokens, rows),
        check_vma=False,
    )
```

time: 149 us -> 49.8 us (0.33)
  local copies, waits for them, and re-layouts: 95.6 us -> 0 us
  matrix products: 10.8 us -> 0 us
  Pallas kernels: 0 us -> 7.3 us
  waiting for transfers between devices: 17.4 us -> 24.2 us
  other arithmetic: 6.89 us -> 0.86 us
    dynamic_update_slice x8 -> x0, local copies, waits for them, and re-layouts: 70.5 us -> none  [body(): lax.dynamic_update_index_in_dim(whole, parts[distance], me ^ distance, 0)]
    broadcast_in_dim x10 -> x0, local copies, waits for them, and re-layouts: 10.5 us -> none  [the longest x7 10.1 us: body(): lax.dynamic_update_index_in_dim(whole, parts[distance], me ^ distance, 0)]
    pallas_call x0 -> x8, Pallas kernels: none -> 7.3 us  [the longest x1 2.4 us: attend(): pl.pallas_call(functools.partial(attend_kernel, chips), out_shape=like((2...]
    ppermute x14 -> x13, waiting for transfers between devices: 17.4 us -> 24.2 us  [swap(): return lax.ppermute(array, axis, [(i, i ^ distance) for i in range(count)])]
    dot_general x4 -> x0, matrix products: 6.3 us -> none  [the longest x2 5.42 us: causal_attention(): jnp.einsum('hqk,khd->qhd', probs, head_values[:last_key], preferred_eleme...]
    sub x2 -> x0, matrix products: 4.55 us -> none  [causal_attention(): expons = jnp.exp(scores - highest)]
    another operation x8 -> x0, local copies, waits for them, and re-layouts: 3.92 us -> none
    slice x6 -> x0, local copies, waits for them, and re-layouts: 3.88 us -> none  [the longest x2 1.8 us: causal_attention(): head_keys[:last_key]]
  transfers between devices with their start and end apart: 14 -> 13, of which waited for: 4 -> 7; matrix products, arithmetic and copies ran while one was open for 72% -> 0% of each run, Pallas kernels for 0% -> 10%
where the time goes in v3:
time: 49.8 us; the launch traced here: 49.6 us
  waiting for transfers between devices  24.2 us (49%)
  starting transfers between devices  16.5 us (33%)
  Pallas kernels  7.3 us (15%)
  other arithmetic  0.86 us (2%)
  between operations  0.76 us (2%)
    ppermute x13, waiting for transfers between devices, swap(): return lax.ppermute(array, axis, [(i, i ^ distance) for i in range(count)])  24.2 us
    ppermute x13, starting transfers between devices, swap(): return lax.ppermute(array, axis, [(i, i ^ distance) for i in range(count)])  16.5 us
    pallas_call x1, Pallas kernels, attend(): pl.pallas_call(functools.partial(attend_kernel, chips), out_shape=like((2...  2.4 us
    pallas_call x1, Pallas kernels, update(): pl.pallas_call(update_kernel, out_shape=[like(shape, arrays[0]), jax.Shap...  2.13 us
    pallas_call x1, Pallas kernels, pack(): pl.pallas_call(pack_kernel, out_shape=[like((rows, width), queries)] * ch...  1.57 us
  transfers between devices with their start and end apart: 13, of which 7 were waited for; matrix products, arithmetic and copies ran while one was open for 0% of the time, Pallas kernels for 10%

profile of v3, /device:TPU:0, one launch (start us, length us, event | category | flops | bytes accessed | tf_op | source)
XLA Modules:
  0.0 49.6 jit_solution(2221863082377026973)
XLA Ops:
  0.6 1.6 %pack.1 = (bf16[128,512]{1,0:T(8,128)(2,1)S(1)}, bf16[128,512]{1,0:T(8,128)(2,1)S(1)}, bf16[128,512]{1,0:T(8,128)(2,1)S(1)}, bf16[128,512]{1,0:T(8,128)(2,1)S(1)...) custom-call(s32[1]{0:T(128)} %bitcast.me_ref, ...), custom_call_target="tpu_custom_call" | custom-call | bytes 3145728 | tf_op jit(solution)/shard_map/pack/pallas_call | solution.py:78
  2.2 3.0 %collective-permute-start = (bf16[2,128,512]{2,1,0:T(8,128)(2,1)S(1)}, bf16[2,128,512]{2,1,0:T(8,128)(2,1)S(1)}, u32[]{:S(2)}, u32[]{:S(2)}) collective-permute-start(bf16[2,128,512]{2,1,0:T(8,128)(2,1)S(1)} %get-tuple-element.41), channel_id=1, source_target_pairs={{0,8},{4,12},{8,0},{12,4},{16,24},{20,28},{24,16},{28,20},{1,9},{5... | collective-permute-start | bytes 786440 | tf_op jit(solution)/shard_map/ppermute | solution.py:34
  5.2 1.5 %collective-permute-start.1 = (bf16[2,128,512]{2,1,0:T(8,128)(2,1)S(1)}, bf16[2,128,512]{2,1,0:T(8,128)(2,1)S(1)}, u32[]{:S(2)}, u32[]{:S(2)}) collective-permute-start(bf16[2,128,512]{2,1,0:T(8,128)(2,1)S(1)} %get-tuple-element.42), channel_id=1, source_target_pairs={{0,16},{4,20},{8,24},{12,28},{16,0},{20,4},{24,8},{28,12},{1,17},{... | collective-permute-start | bytes 786440 | tf_op jit(solution)/shard_map/ppermute | solution.py:34
  6.7 0.0 collective-permute-start.2
  6.8 2.1 %update.1 = (f32[64,1024]{1,0:T(8,128)}, bf16[64,1024]{1,0:T(8,128)(2,1)S(1)}) custom-call(f32[64,1024]{1,0:T(8,128)} %refs_0_, f32[64,1024]{1,0:T(8,128)} %refs_1_, f32[64,1024]{1,0:T(8,128)} %refs_2_, f32[64,1024]{1,0:T(8,128)} %refs_3_), custom_call_target="tpu_custom_call" | custom-call | bytes 1441792 | tf_op jit(solution)/shard_map/update/pallas_call | solution.py:109
  8.9 3.1 %collective-permute-start.3 = (bf16[1,64,1024]{2,1,0:T(8,128)(2,1)S(1)}, bf16[1,64,1024]{2,1,0:T(8,128)(2,1)S(1)}, u32[]{:S(2)}, u32[]{:S(2)}) collective-permute-start(bf16[1,64,1024]{2,1,0:T(8,128)(2,1)S(1)} %bitcast.12), channel_id=1, source_target_pairs={{0,2},{1,3},{2,0},{3,1},{4,6},{5,7},{6,4},{7,5},{8,10},{9,11},{10,... | collective-permute-start | bytes 393224 | tf_op jit(solution)/shard_map/ppermute | solution.py:34
  12.0 5.5 %collective-permute-done.3.refs_1_ = bf16[1,64,1024]{2,1,0:T(8,128)(2,1)S(1)} collective-permute-done((bf16[1,64,1024]{2,1,0:T(8,128)(2,1)S(1)}, bf16[1,64,1024]{2,1,0:T(8,128)(2,1)S(1)}, u32[]{:S(2)}, u32[]{:S(2)}) %collective-permute-start.3) | collective-permute-done | bytes 131104 | tf_op jit(solution)/shard_map/ppermute | solution.py:34
  17.5 0.0 collective-permute-done.refs_1_
  17.5 1.1 %collective-permute-done.1.refs_2_ = bf16[2,128,512]{2,1,0:T(8,128)(2,1)S(1)} collective-permute-done((bf16[2,128,512]{2,1,0:T(8,128)(2,1)S(1)}, bf16[2,128,512]{2,1,0:T(8,128)(2,1)S(1)}, u32[]{:S(2)}, u32[]{:S(2)}) %collective-permute-start.1) | collective-permute-done | bytes 262176 | tf_op jit(solution)/shard_map/ppermute | solution.py:34
  18.6 0.0 collective-permute-done.2.refs_3_
  18.6 0.1 stack.1.own
  18.7 0.1 collective-permute-start.7
  18.8 1.6 %collective-permute-start.8 = (bf16[2,64,1024]{2,1,0:T(8,128)(2,1)S(1)}, bf16[2,64,1024]{2,1,0:T(8,128)(2,1)S(1)}, u32[]{:S(2)}, u32[]{:S(2)}) collective-permute-start(bf16[2,64,1024]{2,1,0:T(8,128)(2,1)S(1)} %bitcast.8), channel_id=1, source_target_pairs={{0,1},{1,0},{2,3},{3,2},{4,5},{5,4},{6,7},{7,6},{8,9},{9,8},{10,11... | collective-permute-start | bytes 786440 | tf_op jit(solution)/shard_map/ppermute | solution.py:34
  20.5 1.2 %collective-permute-start.4 = (bf16[128,512]{1,0:T(8,128)(2,1)S(1)}, bf16[128,512]{1,0:T(8,128)(2,1)S(1)}, u32[]{:S(2)}, u32[]{:S(2)}) collective-permute-start(bf16[128,512]{1,0:T(8,128)(2,1)S(1)} %get-tuple-element.53), channel_id=1, source_target_pairs={{0,8},{4,12},{8,0},{12,4},{16,24},{20,28},{24,16},{28,20},{1,9},{5... | collective-permute-start | bytes 393224 | tf_op jit(solution)/shard_map/ppermute | solution.py:34
  21.7 0.8 %collective-permute-start.5 = (bf16[128,512]{1,0:T(8,128)(2,1)S(1)}, bf16[128,512]{1,0:T(8,128)(2,1)S(1)}, u32[]{:S(2)}, u32[]{:S(2)}) collective-permute-start(bf16[128,512]{1,0:T(8,128)(2,1)S(1)} %get-tuple-element.54), channel_id=1, source_target_pairs={{0,16},{4,20},{8,24},{12,28},{16,0},{20,4},{24,8},{28,12},{1,17},{... | collective-permute-start | bytes 393224 | tf_op jit(solution)/shard_map/ppermute | solution.py:34
  22.5 1.4 %collective-permute-start.6 = (bf16[128,512]{1,0:T(8,128)(2,1)S(1)}, bf16[128,512]{1,0:T(8,128)(2,1)S(1)}, u32[]{:S(2)}, u32[]{:S(2)}) collective-permute-start(bf16[128,512]{1,0:T(8,128)(2,1)S(1)} %get-tuple-element.55), channel_id=1, source_target_pairs={{0,24},{4,28},{8,16},{12,20},{16,8},{20,12},{24,0},{28,4},{1,25},{... | collective-permute-start | bytes 393224 | tf_op jit(solution)/shard_map/ppermute | solution.py:34
  23.9 2.7 %collective-permute-done.4.refs_1_ = bf16[128,512]{1,0:T(8,128)(2,1)S(1)} collective-permute-done((bf16[128,512]{1,0:T(8,128)(2,1)S(1)}, bf16[128,512]{1,0:T(8,128)(2,1)S(1)}, u32[]{:S(2)}, u32[]{:S(2)}) %collective-permute-start.4) | collective-permute-done | bytes 131104 | tf_op jit(solution)/shard_map/ppermute | solution.py:34
  26.7 1.5 %collective-permute-done.5.refs_2_ = bf16[128,512]{1,0:T(8,128)(2,1)S(1)} collective-permute-done((bf16[128,512]{1,0:T(8,128)(2,1)S(1)}, bf16[128,512]{1,0:T(8,128)(2,1)S(1)}, u32[]{:S(2)}, u32[]{:S(2)}) %collective-permute-start.5) | collective-permute-done | bytes 131104 | tf_op jit(solution)/shard_map/ppermute | solution.py:34
  28.2 1.6 %collective-permute-done.6.refs_3_ = bf16[128,512]{1,0:T(8,128)(2,1)S(1)} collective-permute-done((bf16[128,512]{1,0:T(8,128)(2,1)S(1)}, bf16[128,512]{1,0:T(8,128)(2,1)S(1)}, u32[]{:S(2)}, u32[]{:S(2)}) %collective-permute-start.6) | collective-permute-done | bytes 131104 | tf_op jit(solution)/shard_map/ppermute | solution.py:34
  29.8 0.0 collective-permute-done.8.refs_1_
  29.8 0.0 collective-permute-done.7.other
  29.8 0.1 collective-permute-start.9
  29.9 0.4 gather.1
  30.3 2.4 %attend.1.attended = bf16[2,512,256]{2,1,0:T(8,128)(2,1)S(1)} custom-call(s32[1]{0:T(128)} %bitcast.me_ref, bf16[128,512]{1,0:T(8,128)(2,1)S(1)} %get-tuple-element.57.refs_0_, bf16[128,512]{1,0:T(8,128)(2,1)S(1)} %collective-permute-done.4.refs_1_, bf16[128,512]{1,0:T(8,128)(2,1)S(1)} %collective-permute-done.5.refs_2_, ...), custom_call_target="tpu_custom_call" | custom-call | flops 1073741824 | bytes 4194304 | tf_op jit(solution)/shard_map/attend/pallas_call | solution.py:248
  32.7 0.0 collective-permute-done.9.their_weight
  32.7 0.7 %project.1 = (f32[128,1024]{1,0:T(8,128)S(1)}, bf16[128,1024]{1,0:T(8,128)(2,1)S(1)}, bf16[128,1024]{1,0:T(8,128)(2,1)S(1)}, bf16[128,1024]{1,0:T(8,128)(2,1)S(1)}) custom-call(s32[1]{0:T(128)} %bitcast.me_ref, bf16[2,512,256]{2,1,0:T(8,128)(2,1)S(1)} %attend.1.attended, bf16[256,1024]{1,0:T(8,128)(2,1)S(1)} %bitcast.11, ...), custom_call_target="tpu_custom_call" | custom-call | flops 536870912 | bytes 2621440 | tf_op jit(solution)/shard_map/project/pallas_call | solution.py:277
  33.4 1.8 %collective-permute-start.12 = (bf16[128,1024]{1,0:T(8,128)(2,1)S(1)}, bf16[128,1024]{1,0:T(8,128)(2,1)S(1)}, u32[]{:S(2)}, u32[]{:S(2)}) collective-permute-start(bf16[128,1024]{1,0:T(8,128)(2,1)S(1)} %get-tuple-element.68), channel_id=1, source_target_pairs={{0,24},{4,28},{8,16},{12,20},{16,8},{20,12},{24,0},{28,4},{1,25},{... | collective-permute-start | bytes 786440 | tf_op jit(solution)/shard_map/ppermute | solution.py:34
  35.3 0.5 %collective-permute-start.11 = (bf16[128,1024]{1,0:T(8,128)(2,1)S(1)}, bf16[128,1024]{1,0:T(8,128)(2,1)S(1)}, u32[]{:S(2)}, u32[]{:S(2)}) collective-permute-start(bf16[128,1024]{1,0:T(8,128)(2,1)S(1)} %get-tuple-element.67), channel_id=1, source_target_pairs={{0,16},{4,20},{8,24},{12,28},{16,0},{20,4},{24,8},{28,12},{1,17},{... | collective-permute-start | bytes 786440 | tf_op jit(solution)/shard_map/ppermute | solution.py:34
  35.8 1.2 %collective-permute-start.10 = (bf16[128,1024]{1,0:T(8,128)(2,1)S(1)}, bf16[128,1024]{1,0:T(8,128)(2,1)S(1)}, u32[]{:S(2)}, u32[]{:S(2)}) collective-permute-start(bf16[128,1024]{1,0:T(8,128)(2,1)S(1)} %get-tuple-element.66), channel_id=1, source_target_pairs={{0,8},{4,12},{8,0},{12,4},{16,24},{20,28},{24,16},{28,20},{1,9},{5... | collective-permute-start | bytes 786440 | tf_op jit(solution)/shard_map/ppermute | solution.py:34
  37.0 6.6 %collective-permute-done.12 = bf16[128,1024]{1,0:T(8,128)(2,1)S(1)} collective-permute-done((bf16[128,1024]{1,0:T(8,128)(2,1)S(1)}, bf16[128,1024]{1,0:T(8,128)(2,1)S(1)}, u32[]{:S(2)}, u32[]{:S(2)}) %collective-permute-start.12) | collective-permute-done | bytes 262176 | tf_op jit(solution)/shard_map/ppermute | solution.py:34
  43.6 5.2 %collective-permute-done.11 = bf16[128,1024]{1,0:T(8,128)(2,1)S(1)} collective-permute-done((bf16[128,1024]{1,0:T(8,128)(2,1)S(1)}, bf16[128,1024]{1,0:T(8,128)(2,1)S(1)}, u32[]{:S(2)}, u32[]{:S(2)}) %collective-permute-start.11) | collective-permute-done | bytes 262176 | tf_op jit(solution)/shard_map/ppermute | solution.py:34
  48.7 0.0 collective-permute-done.10
  48.7 0.9 %fusion = bf16[1,128,1024]{2,1,0:T(8,128)(2,1)} fusion(bf16[128,1024]{1,0:T(8,128)(2,1)S(1)} %collective-permute-done.12, bf16[128,1024]{1,0:T(8,128)(2,1)S(1)} %collective-permute-done.11, f32[128,1024]{1,0:T(8,128)S(1)} %get-tuple-element.65, bf16[128,1024]{1,0:T(8,128)(2,1)S(1)} %collective-permute-done.10), kind=kLoop, calls=%fused_computation.1 | loop fusion | flops 917504 | bytes 1572864 | tf_op jit(solution)/shard_map/broadcast_in_dim | solution.py:334
  (2 shorter events, 0.1 us)
Async XLA Ops:
  2.2 15.3 %collective-permute-start = (bf16[2,128,512]{2,1,0:T(8,128)(2,1)S(1)}, bf16[2,128,512]{2,1,0:T(8,128)(2,1)S(1)}, u32[]{:S(2)}, u32[]{:S(2)}) collective-permute-start(bf16[2,128,512]{2,1,0:T(8,128)(2,1)S(1)} %get-tuple-element.41), channel_id=1, source_target_pairs={{0,8},{4,12},{8,0},{12,4},{16,24},{20,28},{24,16},{28,20},{1,9},{5... | collective-permute-start | bytes 786440 | tf_op jit(solution)/shard_map/ppermute | solution.py:34
  5.2 13.4 %collective-permute-start.1 = (bf16[2,128,512]{2,1,0:T(8,128)(2,1)S(1)}, bf16[2,128,512]{2,1,0:T(8,128)(2,1)S(1)}, u32[]{:S(2)}, u32[]{:S(2)}) collective-permute-start(bf16[2,128,512]{2,1,0:T(8,128)(2,1)S(1)} %get-tuple-element.42), channel_id=1, source_target_pairs={{0,16},{4,20},{8,24},{12,28},{16,0},{20,4},{24,8},{28,12},{1,17},{... | collective-permute-start | bytes 786440 | tf_op jit(solution)/shard_map/ppermute | solution.py:34
  6.7 11.9 %collective-permute-start.2 = (bf16[2,128,512]{2,1,0:T(8,128)(2,1)S(1)}, bf16[2,128,512]{2,1,0:T(8,128)(2,1)S(1)}, u32[]{:S(2)}, u32[]{:S(2)}) collective-permute-start(bf16[2,128,512]{2,1,0:T(8,128)(2,1)S(1)} %get-tuple-element.43), channel_id=1, source_target_pairs={{0,24},{4,28},{8,16},{12,20},{16,8},{20,12},{24,0},{28,4},{1,25},{... | collective-permute-start | bytes 786440 | tf_op jit(solution)/shard_map/ppermute | solution.py:34
  8.9 8.6 %collective-permute-start.3 = (bf16[1,64,1024]{2,1,0:T(8,128)(2,1)S(1)}, bf16[1,64,1024]{2,1,0:T(8,128)(2,1)S(1)}, u32[]{:S(2)}, u32[]{:S(2)}) collective-permute-start(bf16[1,64,1024]{2,1,0:T(8,128)(2,1)S(1)} %bitcast.12), channel_id=1, source_target_pairs={{0,2},{1,3},{2,0},{3,1},{4,6},{5,7},{6,4},{7,5},{8,10},{9,11},{10,... | collective-permute-start | bytes 393224 | tf_op jit(solution)/shard_map/ppermute | solution.py:34
  18.7 11.1 %collective-permute-start.7 = (bf16[4,2,128,512]{3,2,1,0:T(8,128)(2,1)S(1)}, bf16[4,2,128,512]{3,2,1,0:T(8,128)(2,1)S(1)}, u32[]{:S(2)}, u32[]{:S(2)}) collective-permute-start(bf16[4,2,128,512]{3,2,1,0:T(8,128)(2,1)S(1)} %stack.1.own), channel_id=1, source_target_pairs={{0,4},{4,0},{8,12},{12,8},{16,20},{20,16},{24,28},{28,24},{1,5},{5... | collective-permute-start | bytes 3145736 | tf_op jit(solution)/shard_map/ppermute | solution.py:34
  18.8 11.0 %collective-permute-start.8 = (bf16[2,64,1024]{2,1,0:T(8,128)(2,1)S(1)}, bf16[2,64,1024]{2,1,0:T(8,128)(2,1)S(1)}, u32[]{:S(2)}, u32[]{:S(2)}) collective-permute-start(bf16[2,64,1024]{2,1,0:T(8,128)(2,1)S(1)} %bitcast.8), channel_id=1, source_target_pairs={{0,1},{1,0},{2,3},{3,2},{4,5},{5,4},{6,7},{7,6},{8,9},{9,8},{10,11... | collective-permute-start | bytes 786440 | tf_op jit(solution)/shard_map/ppermute | solution.py:34
  20.5 6.2 %collective-permute-start.4 = (bf16[128,512]{1,0:T(8,128)(2,1)S(1)}, bf16[128,512]{1,0:T(8,128)(2,1)S(1)}, u32[]{:S(2)}, u32[]{:S(2)}) collective-permute-start(bf16[128,512]{1,0:T(8,128)(2,1)S(1)} %get-tuple-element.53), channel_id=1, source_target_pairs={{0,8},{4,12},{8,0},{12,4},{16,24},{20,28},{24,16},{28,20},{1,9},{5... | collective-permute-start | bytes 393224 | tf_op jit(solution)/shard_map/ppermute | solution.py:34
  21.7 6.5 %collective-permute-start.5 = (bf16[128,512]{1,0:T(8,128)(2,1)S(1)}, bf16[128,512]{1,0:T(8,128)(2,1)S(1)}, u32[]{:S(2)}, u32[]{:S(2)}) collective-permute-start(bf16[128,512]{1,0:T(8,128)(2,1)S(1)} %get-tuple-element.54), channel_id=1, source_target_pairs={{0,16},{4,20},{8,24},{12,28},{16,0},{20,4},{24,8},{28,12},{1,17},{... | collective-permute-start | bytes 393224 | tf_op jit(solution)/shard_map/ppermute | solution.py:34
  22.5 7.3 %collective-permute-start.6 = (bf16[128,512]{1,0:T(8,128)(2,1)S(1)}, bf16[128,512]{1,0:T(8,128)(2,1)S(1)}, u32[]{:S(2)}, u32[]{:S(2)}) collective-permute-start(bf16[128,512]{1,0:T(8,128)(2,1)S(1)} %get-tuple-element.55), channel_id=1, source_target_pairs={{0,24},{4,28},{8,16},{12,20},{16,8},{20,12},{24,0},{28,4},{1,25},{... | collective-permute-start | bytes 393224 | tf_op jit(solution)/shard_map/ppermute | solution.py:34
  29.8 2.9 %collective-permute-start.9 = (bf16[256,1024]{1,0:T(8,128)(2,1)S(1)}, bf16[256,1024]{1,0:T(8,128)(2,1)S(1)}, u32[]{:S(2)}, u32[]{:S(2)}) collective-permute-start(bf16[256,1024]{1,0:T(8,128)(2,1)S(1)} %bitcast.10), channel_id=1, source_target_pairs={{0,4},{4,0},{8,12},{12,8},{16,20},{20,16},{24,28},{28,24},{1,5},{5... | collective-permute-start | bytes 1572872 | tf_op jit(solution)/shard_map/ppermute | solution.py:34
  33.4 10.1 %collective-permute-start.12 = (bf16[128,1024]{1,0:T(8,128)(2,1)S(1)}, bf16[128,1024]{1,0:T(8,128)(2,1)S(1)}, u32[]{:S(2)}, u32[]{:S(2)}) collective-permute-start(bf16[128,1024]{1,0:T(8,128)(2,1)S(1)} %get-tuple-element.68), channel_id=1, source_target_pairs={{0,24},{4,28},{8,16},{12,20},{16,8},{20,12},{24,0},{28,4},{1,25},{... | collective-permute-start | bytes 786440 | tf_op jit(solution)/shard_map/ppermute | solution.py:34
  35.3 13.5 %collective-permute-start.11 = (bf16[128,1024]{1,0:T(8,128)(2,1)S(1)}, bf16[128,1024]{1,0:T(8,128)(2,1)S(1)}, u32[]{:S(2)}, u32[]{:S(2)}) collective-permute-start(bf16[128,1024]{1,0:T(8,128)(2,1)S(1)} %get-tuple-element.67), channel_id=1, source_target_pairs={{0,16},{4,20},{8,24},{12,28},{16,0},{20,4},{24,8},{28,12},{1,17},{... | collective-permute-start | bytes 786440 | tf_op jit(solution)/shard_map/ppermute | solution.py:34
  35.8 13.0 %collective-permute-start.10 = (bf16[128,1024]{1,0:T(8,128)(2,1)S(1)}, bf16[128,1024]{1,0:T(8,128)(2,1)S(1)}, u32[]{:S(2)}, u32[]{:S(2)}) collective-permute-start(bf16[128,1024]{1,0:T(8,128)(2,1)S(1)} %get-tuple-element.66), channel_id=1, source_target_pairs={{0,8},{4,12},{8,0},{12,4},{16,24},{20,28},{24,16},{28,20},{1,9},{5... | collective-permute-start | bytes 786440 | tf_op jit(solution)/shard_map/ppermute | solution.py:34

commit v4 on v3

--- a/solution.py
+++ b/solution.py
@@ -188,67 +188,83 @@
     )(me, own, other)
 
 
-def attend_kernel(chips, me_ref, *refs):
-    parts, (keys, values, attended, queries, result) = refs[:chips], refs[chips:]
+def attend_kernel(distances, me_ref, *refs):
+    many = len(distances)
+    parts, (keys, values, attended, queries, result) = refs[:many], refs[many:]
     rows, width = parts[0].shape
     near = 2 * rows
+    half = width // 2
     chip, core = me_ref[0] // 2, me_ref[0] % 2
-    for distance, part in enumerate(parts):
-        at = pl.ds(pl.multiple_of((chip ^ distance) * rows, rows), rows)
-        queries[at, :] = part[...]
-    causal = core * rows + lax.broadcasted_iota(
-        jnp.int32, (rows, near), 0
-    ) >= lax.broadcasted_iota(jnp.int32, (rows, near), 1)
     scale = HEAD_DIM ** (-0.5) * math.log2(math.e)
-    for head in range(width // HEAD_DIM):
-        columns = slice(head * HEAD_DIM, (head + 1) * HEAD_DIM)
-        scores = []
-        for c in range(chips):
-            score = lax.dot_general(
-                queries[c * rows :, columns],
-                keys[c * near : (c + 1) * near, columns],
-                (((1,), (1,)), ((), ())),
-                preferred_element_type=jnp.float32,
-            )
-            masked = jnp.where(causal, score[:rows], -jnp.inf)
-            scores.append(jnp.concatenate([masked, score[rows:]], axis=0) if c < chips - 1 else masked)
-        highest = []
-        for block in range(chips):
-            best = scores[0][block * rows : (block + 1) * rows]
-            for c in range(1, block + 1):
-                best = jnp.maximum(best, scores[c][(block - c) * rows : (block - c + 1) * rows])
-            highest.append(jnp.max(best, axis=1, keepdims=True))
-        highest = jnp.concatenate(highest, axis=0)
-        totals = None
-        for c in range(chips):
-            expons = jnp.exp2((scores[c] - highest[c * rows :]) * scale).astype(jnp.bfloat16)
-            total = jnp.dot(
-                expons, values[head, c * near : (c + 1) * near], preferred_element_type=jnp.float32
-            )
-            if c:
-                total += totals[rows:]
-            totals = total
-            result[c * rows : (c + 1) * rows, columns] = (
-                totals[:rows, :HEAD_DIM] / totals[:rows, HEAD_DIM:]
-            ).astype(result.dtype)
-    half = width // 2
-    for distance in range(chips):
-        at = pl.ds(pl.multiple_of((chip ^ distance) * rows, rows), rows)
-        for part in range(2):
-            attended[part, distance * rows : (distance + 1) * rows, :] = result[
-                at, part * half : (part + 1) * half
-            ]
-
-
-def attend(me, parts, keys, values):
-    chips = len(parts)
+
+    def attend_from(here):
+        chips = sorted(here ^ distance for distance in distances)
+        place = {chip: index * rows for index, chip in enumerate(chips)}
+        for distance, part in zip(distances, parts):
+            at = place[here ^ distance]
+            queries[at : at + rows, :] = part[...]
+        causal = core * rows + lax.broadcasted_iota(
+            jnp.int32, (rows, near), 0
+        ) >= lax.broadcasted_iota(jnp.int32, (rows, near), 1)
+        for head in range(width // HEAD_DIM):
+            columns = slice(head * HEAD_DIM, (head + 1) * HEAD_DIM)
+            tiles = []
+            for c in range(chips[-1] + 1):
+                first = min(place[chip] for chip in chips if chip >= c)
+                score = lax.dot_general(
+                    queries[first : many * rows, columns],
+                    keys[c * near : (c + 1) * near, columns],
+                    (((1,), (1,)), ((), ())),
+                    preferred_element_type=jnp.float32,
+                )
+                if c in place:
+                    masked = jnp.where(causal, score[:rows], -jnp.inf)
+                    later = [score[rows:]] if first + rows < many * rows else []
+                    score = jnp.concatenate([masked, *later], axis=0)
+                tiles.append((c, first, score))
+            highest = []
+            for chip in chips:
+                best = None
+                for c, first, score in tiles:
+                    if c <= chip:
+                        at = place[chip] - first
+                        block = score[at : at + rows]
+                        best = block if best is None else jnp.maximum(best, block)
+                highest.append(jnp.max(best, axis=1, keepdims=True))
+            highest = jnp.concatenate(highest, axis=0)
+            totals, start = None, 0
+            for c, first, score in tiles:
+                expons = jnp.exp2((score - highest[first:]) * scale).astype(jnp.bfloat16)
+                total = jnp.dot(
+                    expons,
+                    values[head, c * near : (c + 1) * near],
+                    preferred_element_type=jnp.float32,
+                )
+                totals = total if totals is None else totals[first - start :] + total
+                start = first
+                if c in place:
+                    result[first : first + rows, columns] = (
+                        totals[:rows, :HEAD_DIM] / totals[:rows, HEAD_DIM:]
+                    ).astype(result.dtype)
+        for index, distance in enumerate(distances):
+            at = place[here ^ distance]
+            for part in range(2):
+                attended[part, index * rows : (index + 1) * rows, :] = result[
+                    at : at + rows, part * half : (part + 1) * half
+                ]
+
+    for here in range(keys.shape[0] // near):
+        pl.when(chip == here)(functools.partial(attend_from, here))
+
+
+def attend(me, distances, parts, keys, values):
     rows, width = parts[0].shape
     length = keys.shape[0]
-    total = chips * rows
-    return pl.pallas_call(
-        functools.partial(attend_kernel, chips),
+    total = len(parts) * rows
+    return pl.pallas_call(
+        functools.partial(attend_kernel, distances),
         out_shape=like((2, total, width // 2), keys),
-        in_specs=[SMEM] + [VMEM] * (chips + 2),
+        in_specs=[SMEM] + [VMEM] * (len(parts) + 2),
         out_specs=VMEM,
         scratch_shapes=[pltpu.VMEM((total, width), keys.dtype)] * 2,
         compiler_params=PARAMS,
@@ -261,32 +277,56 @@
     )(me, *parts, keys, values)
 
 
-def project_kernel(me_ref, attended, own_weight, their_weight, here, *sent):
-    rows = here.shape[0]
+def project_kernel(me_ref, attended, own_weight, their_weight, *outs):
     core = me_ref[0] % 2
     product = jnp.dot(attended[core], own_weight[...], preferred_element_type=jnp.float32)
     product += jnp.dot(attended[1 - core], their_weight[...], preferred_element_type=jnp.float32)
-    here[...] = product[:rows]
-    for distance, block in enumerate(sent, 1):
-        block[...] = product[distance * rows : (distance + 1) * rows].astype(block.dtype)
-
-
-def project(me, attended, own_weight, their_weight, rows):
+    rows, columns = outs[0].shape
+    across = product.shape[1] // columns
+    for index, out in enumerate(outs):
+        down, right = index // across * rows, index % across * columns
+        out[...] = product[down : down + rows, right : right + columns].astype(out.dtype)
+
+
+def project(me, attended, own_weight, their_weight, shape, kind):
     _, total, features = attended.shape
-    outs = own_weight.shape[1]
+    width = own_weight.shape[1]
+    many = total * width // math.prod(shape)
     return pl.pallas_call(
         project_kernel,
-        out_shape=[jax.ShapeDtypeStruct((rows, outs), jnp.float32)]
-        + [like((rows, outs), attended)] * (total // rows - 1),
+        out_shape=[jax.ShapeDtypeStruct(shape, kind)] * many,
         in_specs=[SMEM] + [VMEM] * 3,
-        out_specs=[VMEM] * (total // rows),
+        out_specs=[VMEM] * many,
         compiler_params=PARAMS,
         cost_estimate=cost(
-            4 * total * features + 4 * features * outs + 2 * total * outs,
-            4 * total * features * outs,
+            4 * total * features + 4 * features * width + 4 * total * width,
+            4 * total * features * width,
         ),
         name="project",
     )(me, attended, own_weight, their_weight)
+
+
+def add_kernel(marks, *refs):
+    products, (left, right), outs = refs[: len(marks)], refs[len(marks) : -len(marks)], refs[-len(marks) :]
+    half = left.shape[1]
+    for mark, product, out in zip(marks, products, outs):
+        out[...] = product[...].astype(out.dtype)
+        if mark == 1:
+            out[:, :half] = (product[:, :half] + left[...].astype(jnp.float32)).astype(out.dtype)
+        if mark == 2:
+            out[:, half:] = (product[:, half:] + right[...].astype(jnp.float32)).astype(out.dtype)
+
+
+def add(marks, products, left, right):
+    return pl.pallas_call(
+        functools.partial(add_kernel, marks),
+        out_shape=[like(product.shape, left) for product in products],
+        in_specs=[VMEM] * (len(products) + 2),
+        out_specs=[VMEM] * len(products),
+        compiler_params=PARAMS,
+        cost_estimate=cost(8 * len(products) * products[0].size),
+        name="add",
+    )(*products, left, right)
 
 
 def make_body(seq_count, dp_count):
@@ -305,33 +345,51 @@
         state, _ = lax.optimization_barrier(((master, moment, second, gradient), pair_parts))
         new_master, weight = update(*state)
         weight = weight[None]
-        distance = dp_count // 2
-        while distance > 1:
-            theirs = swap(weight, "dp", dp_count, distance)
-            pairs, theirs = lax.optimization_barrier((pairs, theirs))
-            weight = merge((place // distance % 2).reshape(1), [weight, theirs])
-            weight = weight.reshape(-1, *weight.shape[2:])
-            distance //= 2
-        theirs = swap(weight, "dp", dp_count, 1)
+        span = dp_count
+        while span > 1:
+            many = 4 if span % 4 == 0 else 2
+            span //= many
+            pieces = [weight, swap(weight, "dp", dp_count, span)]
+            if many == 4:
+                pieces.append(swap(weight, "dp", dp_count, 2 * span))
+            if span == 1:
+                pairs, pieces = lax.optimization_barrier((pairs, pieces))
+            if many == 4:
+                pieces.append(swap(pieces[2], "dp", dp_count, span))
+            if span > 1:
+                weight = merge((place // span % many).reshape(1), pieces)
+                weight = weight.reshape(-1, *weight.shape[2:])
         own_pairs = stack(pairs)
         other_pairs = swap(own_pairs, "seq", seq_count, 1)
         sent, _ = lax.optimization_barrier((query_parts[1:], pairs))
         own_queries = [query_parts[0]]
         own_queries += [swap(part, "seq", seq_count, 2 * d) for d, part in enumerate(sent, 1)]
-        own_queries, other_pairs, theirs = lax.optimization_barrier(
-            (own_queries, other_pairs, theirs)
-        )
-        weight = merge((place % 2).reshape(1), [weight, theirs])
+        own_queries, other_pairs = lax.optimization_barrier((own_queries, other_pairs))
+        all_keys, all_values = gather(me, own_pairs, other_pairs)
+        pieces, all_keys = lax.optimization_barrier((pieces, all_keys))
+        weight = merge((place % len(pieces)).reshape(1), pieces)
         own_weight = weight.reshape(own_features, out_features)
         their_weight = swap(own_weight, "seq", seq_count, 1)
 
-        all_keys, all_values = gather(me, own_pairs, other_pairs)
-        attended = attend(me, own_queries, all_keys, all_values)
-        here, *sent = project(me, attended, own_weight, their_weight, queries.shape[1])
-        projected = here
-        for d, block in enumerate(sent, 1):
+        rows = queries.shape[1]
+        far = chips - 1
+        attended = attend(me, (far,), [own_queries[far]], all_keys, all_values)
+        halves = project(
+            me, attended, own_weight, their_weight, (rows, out_features // 2), attended.dtype
+        )
+        left = swap(halves[0], "seq", seq_count, 2)
+        right = swap(halves[1], "seq", seq_count, 4)
+        near = tuple(range(far))
+        attended = attend(me, near, own_queries[:far], all_keys, all_values)
+        projected, *products = project(
+            me, attended, own_weight, their_weight, (rows, out_features), jnp.float32
+        )
+        marks = [{far ^ 1: 1, far ^ 2: 2}.get(d, 0) for d in near[1:]]
+        sent = add(marks, products, left, right)
+        for d, block in zip(near[1:], sent):
             projected += swap(block, "seq", seq_count, 2 * d).astype(jnp.float32)
-        return (projected.astype(jnp.bfloat16)[None], new_master)
+        projected = projected.astype(jnp.bfloat16)[None]
+        return (projected, new_master)
 
     return body
 

time: 49.8 us -> 47.1 us (0.946)
  waiting for transfers between devices: 24.2 us -> 18.3 us
  starting transfers between devices: 16.5 us -> 18.7 us
  Pallas kernels: 7.3 us -> 8.37 us
    ppermute x13 -> x15, waiting for transfers between devices: 24.2 us -> 18.3 us  [swap(): return lax.ppermute(array, axis, [(i, i ^ distance) for i in range(count)])]
    ppermute x13 -> x15, starting transfers between devices: 16.5 us -> 18.7 us  [swap(): return lax.ppermute(array, axis, [(i, i ^ distance) for i in range(count)])]
    pallas_call x2 -> x5, Pallas kernels: 3.11 us -> 4.2 us  [the longest x2 3.25 us: attend(): pl.pallas_call(functools.partial(attend_kernel, distances), out_shape=lik...]
  transfers between devices with their start and end apart: 13 -> 15, of which waited for: 7 -> 9; matrix products, arithmetic and copies ran while one was open for 0% -> 0% of each run, Pallas kernels for 10% -> 13%
where the time goes in v4:
time: 47.1 us; the launch traced here: 46.9 us
  starting transfers between devices  18.7 us (40%)
  waiting for transfers between devices  18.3 us (39%)
  Pallas kernels  8.37 us (18%)
  other arithmetic  0.8 us (2%)
  between operations  0.74 us (2%)
    ppermute x15, starting transfers between devices, swap(): return lax.ppermute(array, axis, [(i, i ^ distance) for i in range(count)])  18.7 us
    ppermute x15, waiting for transfers between devices, swap(): return lax.ppermute(array, axis, [(i, i ^ distance) for i in range(count)])  18.3 us
    pallas_call x2, Pallas kernels, attend(): pl.pallas_call(functools.partial(attend_kernel, distances), out_shape=lik...  3.25 us
    pallas_call x1, Pallas kernels, update(): pl.pallas_call(update_kernel, out_shape=[like(shape, arrays[0]), jax.Shap...  2.13 us
    pallas_call x1, Pallas kernels, pack(): pl.pallas_call(pack_kernel, out_shape=[like((rows, width), queries)] * ch...  1.57 us
  transfers between devices with their start and end apart: 15, of which 9 were waited for; matrix products, arithmetic and copies ran while one was open for 0% of the time, Pallas kernels for 13%

profile of v4, /device:TPU:0, one launch (start us, length us, event | category | flops | bytes accessed | tf_op | source)
XLA Modules:
  0.0 46.9 jit_solution(2979687540744609370)
XLA Ops:
  0.6 1.6 %pack.1 = (bf16[128,512]{1,0:T(8,128)(2,1)S(1)}, bf16[128,512]{1,0:T(8,128)(2,1)S(1)}, bf16[128,512]{1,0:T(8,128)(2,1)S(1)}, bf16[128,512]{1,0:T(8,128)(2,1)S(1)...) custom-call(s32[1]{0:T(128)} %bitcast.me_ref, ...), custom_call_target="tpu_custom_call" | custom-call | bytes 3145728 | tf_op jit(solution)/shard_map/pack/pallas_call | solution.py:78
  2.2 3.0 %collective-permute-start = (bf16[2,128,512]{2,1,0:T(8,128)(2,1)S(1)}, bf16[2,128,512]{2,1,0:T(8,128)(2,1)S(1)}, u32[]{:S(2)}, u32[]{:S(2)}) collective-permute-start(bf16[2,128,512]{2,1,0:T(8,128)(2,1)S(1)} %get-tuple-element.50), channel_id=1, source_target_pairs={{0,8},{4,12},{8,0},{12,4},{16,24},{20,28},{24,16},{28,20},{1,9},{5... | collective-permute-start | bytes 786440 | tf_op jit(solution)/shard_map/ppermute | solution.py:34
  5.2 1.5 %collective-permute-start.1 = (bf16[2,128,512]{2,1,0:T(8,128)(2,1)S(1)}, bf16[2,128,512]{2,1,0:T(8,128)(2,1)S(1)}, u32[]{:S(2)}, u32[]{:S(2)}) collective-permute-start(bf16[2,128,512]{2,1,0:T(8,128)(2,1)S(1)} %get-tuple-element.51), channel_id=1, source_target_pairs={{0,16},{4,20},{8,24},{12,28},{16,0},{20,4},{24,8},{28,12},{1,17},{... | collective-permute-start | bytes 786440 | tf_op jit(solution)/shard_map/ppermute | solution.py:34
  6.7 0.0 collective-permute-start.2
  6.8 2.1 %update.1 = (f32[64,1024]{1,0:T(8,128)}, bf16[64,1024]{1,0:T(8,128)(2,1)S(1)}) custom-call(f32[64,1024]{1,0:T(8,128)} %refs_0_, f32[64,1024]{1,0:T(8,128)} %refs_1_, f32[64,1024]{1,0:T(8,128)} %refs_2_, f32[64,1024]{1,0:T(8,128)} %refs_3_), custom_call_target="tpu_custom_call" | custom-call | bytes 1441792 | tf_op jit(solution)/shard_map/update/pallas_call | solution.py:109
  8.9 2.1 %collective-permute-start.3 = (bf16[1,64,1024]{2,1,0:T(8,128)(2,1)S(1)}, bf16[1,64,1024]{2,1,0:T(8,128)(2,1)S(1)}, u32[]{:S(2)}, u32[]{:S(2)}) collective-permute-start(bf16[1,64,1024]{2,1,0:T(8,128)(2,1)S(1)} %bitcast.9), channel_id=1, source_target_pairs={{0,1},{1,0},{2,3},{3,2},{4,5},{5,4},{6,7},{7,6},{8,9},{9,8},{10,11... | collective-permute-start | bytes 393224 | tf_op jit(solution)/shard_map/ppermute | solution.py:34
  11.0 2.6 %collective-permute-start.4 = (bf16[1,64,1024]{2,1,0:T(8,128)(2,1)S(1)}, bf16[1,64,1024]{2,1,0:T(8,128)(2,1)S(1)}, u32[]{:S(2)}, u32[]{:S(2)}) collective-permute-start(bf16[1,64,1024]{2,1,0:T(8,128)(2,1)S(1)} %bitcast.10), channel_id=1, source_target_pairs={{0,2},{1,3},{2,0},{3,1},{4,6},{5,7},{6,4},{7,5},{8,10},{9,11},{10,... | collective-permute-start | bytes 393224 | tf_op jit(solution)/shard_map/ppermute | solution.py:34
  13.6 1.6 %collective-permute-done.3.refs_1_ = bf16[1,64,1024]{2,1,0:T(8,128)(2,1)S(1)} collective-permute-done((bf16[1,64,1024]{2,1,0:T(8,128)(2,1)S(1)}, bf16[1,64,1024]{2,1,0:T(8,128)(2,1)S(1)}, u32[]{:S(2)}, u32[]{:S(2)}) %collective-permute-start.3) | collective-permute-done | bytes 131104 | tf_op jit(solution)/shard_map/ppermute | solution.py:34
  15.2 3.6 %collective-permute-done.4.refs_2_ = bf16[1,64,1024]{2,1,0:T(8,128)(2,1)S(1)} collective-permute-done((bf16[1,64,1024]{2,1,0:T(8,128)(2,1)S(1)}, bf16[1,64,1024]{2,1,0:T(8,128)(2,1)S(1)}, u32[]{:S(2)}, u32[]{:S(2)}) %collective-permute-start.4) | collective-permute-done | bytes 131104 | tf_op jit(solution)/shard_map/ppermute | solution.py:34
  18.9 0.0 collective-permute-done.refs_1_
  18.9 0.0 collective-permute-done.1.refs_2_
  18.9 0.0 collective-permute-done.2.refs_3_
  18.9 0.1 stack.1.own
  19.0 0.1 collective-permute-start.8
  19.0 1.6 %collective-permute-start.5 = (bf16[128,512]{1,0:T(8,128)(2,1)S(1)}, bf16[128,512]{1,0:T(8,128)(2,1)S(1)}, u32[]{:S(2)}, u32[]{:S(2)}) collective-permute-start(bf16[128,512]{1,0:T(8,128)(2,1)S(1)} %get-tuple-element.62), channel_id=1, source_target_pairs={{0,8},{4,12},{8,0},{12,4},{16,24},{20,28},{24,16},{28,20},{1,9},{5... | collective-permute-start | bytes 393224 | tf_op jit(solution)/shard_map/ppermute | solution.py:34
  20.6 1.5 %collective-permute-start.6 = (bf16[128,512]{1,0:T(8,128)(2,1)S(1)}, bf16[128,512]{1,0:T(8,128)(2,1)S(1)}, u32[]{:S(2)}, u32[]{:S(2)}) collective-permute-start(bf16[128,512]{1,0:T(8,128)(2,1)S(1)} %get-tuple-element.63), channel_id=1, source_target_pairs={{0,16},{4,20},{8,24},{12,28},{16,0},{20,4},{24,8},{28,12},{1,17},{... | collective-permute-start | bytes 393224 | tf_op jit(solution)/shard_map/ppermute | solution.py:34
  22.1 0.5 %collective-permute-start.7 = (bf16[128,512]{1,0:T(8,128)(2,1)S(1)}, bf16[128,512]{1,0:T(8,128)(2,1)S(1)}, u32[]{:S(2)}, u32[]{:S(2)}) collective-permute-start(bf16[128,512]{1,0:T(8,128)(2,1)S(1)} %get-tuple-element.64), channel_id=1, source_target_pairs={{0,24},{4,28},{8,16},{12,20},{16,8},{20,12},{24,0},{28,4},{1,25},{... | collective-permute-start | bytes 393224 | tf_op jit(solution)/shard_map/ppermute | solution.py:34
  22.6 1.3 %collective-permute-start.9 = (bf16[1,64,1024]{2,1,0:T(8,128)(2,1)S(1)}, bf16[1,64,1024]{2,1,0:T(8,128)(2,1)S(1)}, u32[]{:S(2)}, u32[]{:S(2)}) collective-permute-start(bf16[1,64,1024]{2,1,0:T(8,128)(2,1)S(1)} %collective-permute-done.4.refs_2_), channel_id=1, source_target_pairs={{0,1},{1,0},{2,3},{3,2},{4,5},{5,4},{6,7},{7,6},{8,9},{9,8},{10,11... | collective-permute-start | bytes 393224 | tf_op jit(solution)/shard_map/ppermute | solution.py:34
  23.9 1.4 %collective-permute-done.5.refs_1_ = bf16[128,512]{1,0:T(8,128)(2,1)S(1)} collective-permute-done((bf16[128,512]{1,0:T(8,128)(2,1)S(1)}, bf16[128,512]{1,0:T(8,128)(2,1)S(1)}, u32[]{:S(2)}, u32[]{:S(2)}) %collective-permute-start.5) | collective-permute-done | bytes 131104 | tf_op jit(solution)/shard_map/ppermute | solution.py:34
  25.3 3.7 %collective-permute-done.6.refs_2_ = bf16[128,512]{1,0:T(8,128)(2,1)S(1)} collective-permute-done((bf16[128,512]{1,0:T(8,128)(2,1)S(1)}, bf16[128,512]{1,0:T(8,128)(2,1)S(1)}, u32[]{:S(2)}, u32[]{:S(2)}) %collective-permute-start.6) | collective-permute-done | bytes 131104 | tf_op jit(solution)/shard_map/ppermute | solution.py:34
  29.0 0.0 collective-permute-done.7.refs_0_
  29.0 0.0 collective-permute-done.8.other
  29.0 0.4 gather.1
  29.3 0.0 collective-permute-done.9.refs_3_
  29.4 0.1 collective-permute-start.10
  29.5 1.2 %attend.3.attended = bf16[2,128,256]{2,1,0:T(8,128)(2,1)S(1)} custom-call(s32[1]{0:T(128)} %bitcast.me_ref, bf16[128,512]{1,0:T(8,128)(2,1)S(1)} %collective-permute-done.7.refs_0_, bf16[1024,512]{1,0:T(8,128)(2,1)S(1)} %get-tuple-element.73.refs_3_.refs_1_, bf16[4,1024,256]{2,1,0:T(8,128)(2,1)S(1)} %get-tuple-element.74.refs_4_.refs_2_), custom_call_target="tpu_custom_call" | custom-call | flops 268435456 | bytes 3407872 | tf_op jit(solution)/shard_map/attend/pallas_call | solution.py:264
  30.6 0.7 %collective-permute-done.10.their_weight = bf16[256,1024]{1,0:T(8,128)(2,1)S(1)} collective-permute-done((bf16[256,1024]{1,0:T(8,128)(2,1)S(1)}, bf16[256,1024]{1,0:T(8,128)(2,1)S(1)}, u32[]{:S(2)}, u32[]{:S(2)}) %collective-permute-start.10) | collective-permute-done | bytes 524320 | tf_op jit(solution)/shard_map/ppermute | solution.py:34
  31.4 0.3 project.3
  31.7 1.3 %collective-permute-start.11 = (bf16[128,512]{1,0:T(8,128)(2,1)S(1)}, bf16[128,512]{1,0:T(8,128)(2,1)S(1)}, u32[]{:S(2)}, u32[]{:S(2)}) collective-permute-start(bf16[128,512]{1,0:T(8,128)(2,1)S(1)} %get-tuple-element.83), channel_id=1, source_target_pairs={{0,8},{4,12},{8,0},{12,4},{16,24},{20,28},{24,16},{28,20},{1,9},{5... | collective-permute-start | bytes 393224 | tf_op jit(solution)/shard_map/ppermute | solution.py:34
  33.0 0.8 %collective-permute-start.12 = (bf16[128,512]{1,0:T(8,128)(2,1)S(1)}, bf16[128,512]{1,0:T(8,128)(2,1)S(1)}, u32[]{:S(2)}, u32[]{:S(2)}) collective-permute-start(bf16[128,512]{1,0:T(8,128)(2,1)S(1)} %get-tuple-element.84), channel_id=1, source_target_pairs={{0,16},{4,20},{8,24},{12,28},{16,0},{20,4},{24,8},{28,12},{1,17},{... | collective-permute-start | bytes 393224 | tf_op jit(solution)/shard_map/ppermute | solution.py:34
  33.8 2.1 %attend.2.attended = bf16[2,384,256]{2,1,0:T(8,128)(2,1)S(1)} custom-call(s32[1]{0:T(128)} %bitcast.me_ref, bf16[128,512]{1,0:T(8,128)(2,1)S(1)} %get-tuple-element.65.refs_0_, bf16[128,512]{1,0:T(8,128)(2,1)S(1)} %collective-permute-done.5.refs_1_, bf16[128,512]{1,0:T(8,128)(2,1)S(1)} %collective-permute-done.6.refs_2_, ...), custom_call_target="tpu_custom_call" | custom-call | flops 805306368 | bytes 3932160 | tf_op jit(solution)/shard_map/attend/pallas_call | solution.py:264
  35.9 0.6 %project.2 = (f32[128,1024]{1,0:T(8,128)S(1)}, f32[128,1024]{1,0:T(8,128)S(1)}, f32[128,1024]{1,0:T(8,128)S(1)}) custom-call(s32[1]{0:T(128)} %bitcast.me_ref, bf16[2,384,256]{2,1,0:T(8,128)(2,1)S(1)} %attend.2.attended, bf16[256,1024]{1,0:T(8,128)(2,1)S(1)} %bitcast.8, bf16[256,1024]{1,0:T(8,128)(2,1)S(1)} %collective-permute-done.10.their_weight), custom_call_target="tpu_custom_call" | custom-call | flops 402653184 | bytes 3014656 | tf_op jit(solution)/shard_map/project/pallas_call | solution.py:295
  36.5 0.8 %collective-permute-done.11.refs_2_ = bf16[128,512]{1,0:T(8,128)(2,1)S(1)} collective-permute-done((bf16[128,512]{1,0:T(8,128)(2,1)S(1)}, bf16[128,512]{1,0:T(8,128)(2,1)S(1)}, u32[]{:S(2)}, u32[]{:S(2)}) %collective-permute-start.11) | collective-permute-done | bytes 131104 | tf_op jit(solution)/shard_map/ppermute | solution.py:34
  37.3 1.0 %collective-permute-done.12.refs_3_ = bf16[128,512]{1,0:T(8,128)(2,1)S(1)} collective-permute-done((bf16[128,512]{1,0:T(8,128)(2,1)S(1)}, bf16[128,512]{1,0:T(8,128)(2,1)S(1)}, u32[]{:S(2)}, u32[]{:S(2)}) %collective-permute-start.12) | collective-permute-done | bytes 131104 | tf_op jit(solution)/shard_map/ppermute | solution.py:34
  38.3 0.1 add.20
  38.3 0.9 %collective-permute-start.13 = (bf16[128,1024]{1,0:T(8,128)(2,1)S(1)}, bf16[128,1024]{1,0:T(8,128)(2,1)S(1)}, u32[]{:S(2)}, u32[]{:S(2)}) collective-permute-start(bf16[128,1024]{1,0:T(8,128)(2,1)S(1)} %get-tuple-element.85), channel_id=1, source_target_pairs={{0,8},{4,12},{8,0},{12,4},{16,24},{20,28},{24,16},{28,20},{1,9},{5... | collective-permute-start | bytes 786440 | tf_op jit(solution)/shard_map/ppermute | solution.py:34
  39.2 1.5 %collective-permute-start.14 = (bf16[128,1024]{1,0:T(8,128)(2,1)S(1)}, bf16[128,1024]{1,0:T(8,128)(2,1)S(1)}, u32[]{:S(2)}, u32[]{:S(2)}) collective-permute-start(bf16[128,1024]{1,0:T(8,128)(2,1)S(1)} %get-tuple-element.86), channel_id=1, source_target_pairs={{0,16},{4,20},{8,24},{12,28},{16,0},{20,4},{24,8},{28,12},{1,17},{... | collective-permute-start | bytes 786440 | tf_op jit(solution)/shard_map/ppermute | solution.py:34
  40.7 4.9 %collective-permute-done.13 = bf16[128,1024]{1,0:T(8,128)(2,1)S(1)} collective-permute-done((bf16[128,1024]{1,0:T(8,128)(2,1)S(1)}, bf16[128,1024]{1,0:T(8,128)(2,1)S(1)}, u32[]{:S(2)}, u32[]{:S(2)}) %collective-permute-start.13) | collective-permute-done | bytes 262176 | tf_op jit(solution)/shard_map/ppermute | solution.py:34
  45.6 0.5 %collective-permute-done.14 = bf16[128,1024]{1,0:T(8,128)(2,1)S(1)} collective-permute-done((bf16[128,1024]{1,0:T(8,128)(2,1)S(1)}, bf16[128,1024]{1,0:T(8,128)(2,1)S(1)}, u32[]{:S(2)}, u32[]{:S(2)}) %collective-permute-start.14) | collective-permute-done | bytes 262176 | tf_op jit(solution)/shard_map/ppermute | solution.py:34
  46.1 0.8 %fusion = bf16[1,128,1024]{2,1,0:T(8,128)(2,1)} fusion(bf16[128,1024]{1,0:T(8,128)(2,1)S(1)} %collective-permute-done.14, f32[128,1024]{1,0:T(8,128)S(1)} %get-tuple-element.79, bf16[128,1024]{1,0:T(8,128)(2,1)S(1)} %collective-permute-done.13), kind=kLoop, calls=%fused_computation.1 | loop fusion | flops 655360 | bytes 1310720 | tf_op jit(solution)/shard_map/broadcast_in_dim | solution.py:391
  (1 shorter events, 0.0 us)
Async XLA Ops:
  2.2 16.7 %collective-permute-start = (bf16[2,128,512]{2,1,0:T(8,128)(2,1)S(1)}, bf16[2,128,512]{2,1,0:T(8,128)(2,1)S(1)}, u32[]{:S(2)}, u32[]{:S(2)}) collective-permute-start(bf16[2,128,512]{2,1,0:T(8,128)(2,1)S(1)} %get-tuple-element.50), channel_id=1, source_target_pairs={{0,8},{4,12},{8,0},{12,4},{16,24},{20,28},{24,16},{28,20},{1,9},{5... | collective-permute-start | bytes 786440 | tf_op jit(solution)/shard_map/ppermute | solution.py:34
  5.2 13.7 %collective-permute-start.1 = (bf16[2,128,512]{2,1,0:T(8,128)(2,1)S(1)}, bf16[2,128,512]{2,1,0:T(8,128)(2,1)S(1)}, u32[]{:S(2)}, u32[]{:S(2)}) collective-permute-start(bf16[2,128,512]{2,1,0:T(8,128)(2,1)S(1)} %get-tuple-element.51), channel_id=1, source_target_pairs={{0,16},{4,20},{8,24},{12,28},{16,0},{20,4},{24,8},{28,12},{1,17},{... | collective-permute-start | bytes 786440 | tf_op jit(solution)/shard_map/ppermute | solution.py:34
  6.7 12.1 %collective-permute-start.2 = (bf16[2,128,512]{2,1,0:T(8,128)(2,1)S(1)}, bf16[2,128,512]{2,1,0:T(8,128)(2,1)S(1)}, u32[]{:S(2)}, u32[]{:S(2)}) collective-permute-start(bf16[2,128,512]{2,1,0:T(8,128)(2,1)S(1)} %get-tuple-element.52), channel_id=1, source_target_pairs={{0,24},{4,28},{8,16},{12,20},{16,8},{20,12},{24,0},{28,4},{1,25},{... | collective-permute-start | bytes 786440 | tf_op jit(solution)/shard_map/ppermute | solution.py:34
  8.9 6.3 %collective-permute-start.3 = (bf16[1,64,1024]{2,1,0:T(8,128)(2,1)S(1)}, bf16[1,64,1024]{2,1,0:T(8,128)(2,1)S(1)}, u32[]{:S(2)}, u32[]{:S(2)}) collective-permute-start(bf16[1,64,1024]{2,1,0:T(8,128)(2,1)S(1)} %bitcast.9), channel_id=1, source_target_pairs={{0,1},{1,0},{2,3},{3,2},{4,5},{5,4},{6,7},{7,6},{8,9},{9,8},{10,11... | collective-permute-start | bytes 393224 | tf_op jit(solution)/shard_map/ppermute | solution.py:34
  11.0 7.9 %collective-permute-start.4 = (bf16[1,64,1024]{2,1,0:T(8,128)(2,1)S(1)}, bf16[1,64,1024]{2,1,0:T(8,128)(2,1)S(1)}, u32[]{:S(2)}, u32[]{:S(2)}) collective-permute-start(bf16[1,64,1024]{2,1,0:T(8,128)(2,1)S(1)} %bitcast.10), channel_id=1, source_target_pairs={{0,2},{1,3},{2,0},{3,1},{4,6},{5,7},{6,4},{7,5},{8,10},{9,11},{10,... | collective-permute-start | bytes 393224 | tf_op jit(solution)/shard_map/ppermute | solution.py:34
  19.0 10.0 %collective-permute-start.8 = (bf16[4,2,128,512]{3,2,1,0:T(8,128)(2,1)S(1)}, bf16[4,2,128,512]{3,2,1,0:T(8,128)(2,1)S(1)}, u32[]{:S(2)}, u32[]{:S(2)}) collective-permute-start(bf16[4,2,128,512]{3,2,1,0:T(8,128)(2,1)S(1)} %stack.1.own), channel_id=1, source_target_pairs={{0,4},{4,0},{8,12},{12,8},{16,20},{20,16},{24,28},{28,24},{1,5},{5... | collective-permute-start | bytes 3145736 | tf_op jit(solution)/shard_map/ppermute | solution.py:34
  19.0 6.3 %collective-permute-start.5 = (bf16[128,512]{1,0:T(8,128)(2,1)S(1)}, bf16[128,512]{1,0:T(8,128)(2,1)S(1)}, u32[]{:S(2)}, u32[]{:S(2)}) collective-permute-start(bf16[128,512]{1,0:T(8,128)(2,1)S(1)} %get-tuple-element.62), channel_id=1, source_target_pairs={{0,8},{4,12},{8,0},{12,4},{16,24},{20,28},{24,16},{28,20},{1,9},{5... | collective-permute-start | bytes 393224 | tf_op jit(solution)/shard_map/ppermute | solution.py:34
  20.6 8.4 %collective-permute-start.6 = (bf16[128,512]{1,0:T(8,128)(2,1)S(1)}, bf16[128,512]{1,0:T(8,128)(2,1)S(1)}, u32[]{:S(2)}, u32[]{:S(2)}) collective-permute-start(bf16[128,512]{1,0:T(8,128)(2,1)S(1)} %get-tuple-element.63), channel_id=1, source_target_pairs={{0,16},{4,20},{8,24},{12,28},{16,0},{20,4},{24,8},{28,12},{1,17},{... | collective-permute-start | bytes 393224 | tf_op jit(solution)/shard_map/ppermute | solution.py:34
  22.1 6.9 %collective-permute-start.7 = (bf16[128,512]{1,0:T(8,128)(2,1)S(1)}, bf16[128,512]{1,0:T(8,128)(2,1)S(1)}, u32[]{:S(2)}, u32[]{:S(2)}) collective-permute-start(bf16[128,512]{1,0:T(8,128)(2,1)S(1)} %get-tuple-element.64), channel_id=1, source_target_pairs={{0,24},{4,28},{8,16},{12,20},{16,8},{20,12},{24,0},{28,4},{1,25},{... | collective-permute-start | bytes 393224 | tf_op jit(solution)/shard_map/ppermute | solution.py:34
  22.6 6.8 %collective-permute-start.9 = (bf16[1,64,1024]{2,1,0:T(8,128)(2,1)S(1)}, bf16[1,64,1024]{2,1,0:T(8,128)(2,1)S(1)}, u32[]{:S(2)}, u32[]{:S(2)}) collective-permute-start(bf16[1,64,1024]{2,1,0:T(8,128)(2,1)S(1)} %collective-permute-done.4.refs_2_), channel_id=1, source_target_pairs={{0,1},{1,0},{2,3},{3,2},{4,5},{5,4},{6,7},{7,6},{8,9},{9,8},{10,11... | collective-permute-start | bytes 393224 | tf_op jit(solution)/shard_map/ppermute | solution.py:34
  29.4 2.0 %collective-permute-start.10 = (bf16[256,1024]{1,0:T(8,128)(2,1)S(1)}, bf16[256,1024]{1,0:T(8,128)(2,1)S(1)}, u32[]{:S(2)}, u32[]{:S(2)}) collective-permute-start(bf16[256,1024]{1,0:T(8,128)(2,1)S(1)} %bitcast.6), channel_id=1, source_target_pairs={{0,4},{4,0},{8,12},{12,8},{16,20},{20,16},{24,28},{28,24},{1,5},{5... | collective-permute-start | bytes 1572872 | tf_op jit(solution)/shard_map/ppermute | solution.py:34
  31.7 5.6 %collective-permute-start.11 = (bf16[128,512]{1,0:T(8,128)(2,1)S(1)}, bf16[128,512]{1,0:T(8,128)(2,1)S(1)}, u32[]{:S(2)}, u32[]{:S(2)}) collective-permute-start(bf16[128,512]{1,0:T(8,128)(2,1)S(1)} %get-tuple-element.83), channel_id=1, source_target_pairs={{0,8},{4,12},{8,0},{12,4},{16,24},{20,28},{24,16},{28,20},{1,9},{5... | collective-permute-start | bytes 393224 | tf_op jit(solution)/shard_map/ppermute | solution.py:34
  33.0 5.3 %collective-permute-start.12 = (bf16[128,512]{1,0:T(8,128)(2,1)S(1)}, bf16[128,512]{1,0:T(8,128)(2,1)S(1)}, u32[]{:S(2)}, u32[]{:S(2)}) collective-permute-start(bf16[128,512]{1,0:T(8,128)(2,1)S(1)} %get-tuple-element.84), channel_id=1, source_target_pairs={{0,16},{4,20},{8,24},{12,28},{16,0},{20,4},{24,8},{28,12},{1,17},{... | collective-permute-start | bytes 393224 | tf_op jit(solution)/shard_map/ppermute | solution.py:34
  38.3 7.3 %collective-permute-start.13 = (bf16[128,1024]{1,0:T(8,128)(2,1)S(1)}, bf16[128,1024]{1,0:T(8,128)(2,1)S(1)}, u32[]{:S(2)}, u32[]{:S(2)}) collective-permute-start(bf16[128,1024]{1,0:T(8,128)(2,1)S(1)} %get-tuple-element.85), channel_id=1, source_target_pairs={{0,8},{4,12},{8,0},{12,4},{16,24},{20,28},{24,16},{28,20},{1,9},{5... | collective-permute-start | bytes 786440 | tf_op jit(solution)/shard_map/ppermute | solution.py:34
  39.2 6.9 %collective-permute-start.14 = (bf16[128,1024]{1,0:T(8,128)(2,1)S(1)}, bf16[128,1024]{1,0:T(8,128)(2,1)S(1)}, u32[]{:S(2)}, u32[]{:S(2)}) collective-permute-start(bf16[128,1024]{1,0:T(8,128)(2,1)S(1)} %get-tuple-element.86), channel_id=1, source_target_pairs={{0,16},{4,20},{8,24},{12,28},{16,0},{20,4},{24,8},{28,12},{1,17},{... | collective-permute-start | bytes 786440 | tf_op jit(solution)/shard_map/ppermute | solution.py:34

commit v5 on v4

v5 whole, which is shorter than its diff:
```python
import functools
import math

import jax
import jax.numpy as jnp
from jax import lax
from jax.experimental import pallas as pl
from jax.experimental.pallas import tpu as pltpu
from jax.sharding import PartitionSpec as P

HEAD_DIM = 128
LANES = 128


beta_first = 0.9
beta_second = 0.999
learning_rate = 0.1
weight_decay = 0.1
epsilon = 1e-08
step_count = 10.0


def adamw(master, moment, second, gradient):
    moment_new = beta_first * moment + (1.0 - beta_first) * gradient
    second_new = beta_second * second + (1.0 - beta_second) * gradient * gradient
    moment_hat = moment_new / (1.0 - beta_first**step_count)
    second_hat = second_new / (1.0 - beta_second**step_count)
    return master - learning_rate * (
        moment_hat / (jnp.sqrt(second_hat) + epsilon) + weight_decay * master
    )


def swap(array, axis, count, distance):
    return lax.ppermute(array, axis, [(i, i ^ distance) for i in range(count)])


SMEM = pl.BlockSpec(memory_space=pltpu.SMEM)
VMEM = pl.BlockSpec(memory_space=pltpu.VMEM)
HBM = pl.BlockSpec(memory_space=pltpu.HBM)
PARAMS = pltpu.CompilerParams(vmem_limit_bytes=14 * 1024 * 1024)


def in_hbm(array):
    return pltpu.with_memory_space_constraint(array, pltpu.HBM)


def like(shape, array):
    return jax.ShapeDtypeStruct(shape, array.dtype)


def cost(moved, flops=0, transcendentals=0):
    return pl.CostEstimate(
        flops=flops, bytes_accessed=moved, transcendentals=transcendentals
    )


def chip_columns(me_ref, distance, width):
    return pl.ds(pl.multiple_of(((me_ref[0] // 2) ^ distance) * width, width), width)


def pack_kernel(me_ref, keys, values, queries, *refs):
    pairs, (here, sems) = refs[:-2], refs[-2:]
    width = here.shape[1]
    copies = []

    def copy(array, distance, part):
        at = chip_columns(me_ref, distance, width)
        copies.append(pltpu.make_async_copy(array.at[0, :, at], part, sems.at[len(copies)]))
        copies[-1].start()

    for distance, pair in enumerate(pairs):
        copy(keys, distance, pair.at[0])
        copy(values, distance, pair.at[1])
    copy(queries, 0, here)
    for each in copies:
        each.wait()


def pack(me, keys, values, queries, chips):
    _, rows, features = queries.shape
    width = features // chips
    *pairs, here = pl.pallas_call(
        pack_kernel,
        out_shape=[like((2, rows, width), queries)] * chips + [like((rows, width), queries)],
        in_specs=[SMEM] + [HBM] * 3,
        out_specs=[VMEM] * (chips + 1),
        scratch_shapes=[pltpu.SemaphoreType.DMA((2 * chips + 1,))],
        compiler_params=PARAMS,
        cost_estimate=cost(8 * rows * features),
        name="pack",
    )(me, *map(in_hbm, (keys, values, queries)))
    return pairs, here


def pack_queries_kernel(me_ref, queries, *refs):
    many = len(refs) - 2
    parts, (held, sems) = refs[:-2], refs[-2:]
    width = held.shape[2]
    arrive = [
        pltpu.make_async_copy(
            queries.at[0, :, chip_columns(me_ref, index + 1, width)],
            held.at[index],
            sems.at[index],
        )
        for index in range(many)
    ]
    leave = [
        pltpu.make_async_copy(held.at[index], part, sems.at[index])
        for index, part in enumerate(parts)
    ]
    for copy in arrive:
        copy.start()
    for first, second in zip(arrive, leave):
        first.wait()
        second.start()
    for copy in leave:
        copy.wait()


def pack_queries(me, queries, chips):
    _, rows, features = queries.shape
    width, many = features // chips, chips - 1
    return pl.pallas_call(
        pack_queries_kernel,
        out_shape=[pltpu.HBM((rows, width), queries.dtype)] * many,
        in_specs=[SMEM, HBM],
        out_specs=[HBM] * many,
        scratch_shapes=[
            pltpu.VMEM((many, rows, width), queries.dtype),
            pltpu.SemaphoreType.DMA((many,)),
        ],
        compiler_params=PARAMS,
        cost_estimate=cost(4 * rows * features),
        name="pack_queries",
    )(me, in_hbm(queries))


def weigh_kernel(*refs):
    arrays, weight, held, sems = refs[:4], refs[4], refs[5], refs[6]
    pieces = sems.shape[1]
    rows = weight.shape[0] // pieces
    copies = []
    for piece in range(pieces):
        at = pl.ds(piece * rows, rows)
        copies.append(
            [
                pltpu.make_async_copy(array.at[at], held.at[index, at], sems.at[index, piece])
                for index, array in enumerate(arrays)
            ]
        )
        for copy in copies[-1]:
            copy.start()
    for piece in range(pieces):
        for copy in copies[piece]:
            copy.wait()
        at = pl.ds(piece * rows, rows)
        result = adamw(held[0, at], held[1, at], held[2, at], held[3, at])
        weight[at, :] = result.astype(weight.dtype)


def weigh(*arrays):
    shape, kind = arrays[0].shape, arrays[0].dtype
    pieces = math.gcd(shape[0] // 16, 4) if shape[0] % 16 == 0 else 1
    return pl.pallas_call(
        weigh_kernel,
        out_shape=jax.ShapeDtypeStruct(shape, jnp.bfloat16),
        in_specs=[HBM] * 4,
        out_specs=VMEM,
        scratch_shapes=[pltpu.VMEM((4, *shape), kind), pltpu.SemaphoreType.DMA((4, pieces))],
        compiler_params=PARAMS,
        cost_estimate=cost(18 * arrays[0].size),
        name="weigh",
    )(*map(in_hbm, arrays))


def merge_kernel(index_ref, *refs):
    pieces, whole = refs[:-1], refs[-1]
    for distance, piece in enumerate(pieces):
        whole[index_ref[0] ^ distance] = piece[...]


def merge(index, pieces):
    return pl.pallas_call(
        merge_kernel,
        out_shape=like((len(pieces), *pieces[0].shape), pieces[0]),
        in_specs=[SMEM] + [VMEM] * len(pieces),
        out_specs=VMEM,
        compiler_params=PARAMS,
        cost_estimate=cost(4 * len(pieces) * pieces[0].size),
        name="merge",
    )(index, *pieces)


def places(chips, rows, pieces, width):
    tokens = [slice(index * rows, (index + 1) * rows) for index in range(2 * chips)]
    down, out_features = pieces.shape
    first, across = 2 * chips * rows, out_features // width
    weights = [
        slice(first + index * down, first + (index + 1) * down) for index in range(3 * across)
    ]
    return tokens, [weights[index * across : (index + 1) * across] for index in range(3)]


def stack_kernel(chips, *refs):
    pairs, pieces, stacked = refs[:chips], refs[chips:-1], refs[-1]
    rows, width = pairs[0].shape[1:]
    tokens, weights = places(chips, rows, pieces[0], width)
    for distance, pair in enumerate(pairs):
        stacked[tokens[2 * distance], :] = pair[0]
        stacked[tokens[2 * distance + 1], :] = pair[1]
    for piece, blocks in zip(pieces, weights):
        for index, block in enumerate(blocks):
            stacked[block, :] = piece[:, index * width : (index + 1) * width]


def stack(pairs, pieces):
    chips = len(pairs)
    _, rows, width = pairs[0].shape
    total = 2 * chips * rows + len(pieces) * pieces[0].size // width
    return pl.pallas_call(
        functools.partial(stack_kernel, chips),
        out_shape=like((total, width), pairs[0]),
        in_specs=[VMEM] * (chips + len(pieces)),
        out_specs=VMEM,
        compiler_params=PARAMS,
        cost_estimate=cost(4 * total * width),
        name="stack",
    )(*pairs, *pieces)


def weights_kernel(chips, rows, index_ref, own, own_last, other, other_last, weights):
    down, out_features = own_last.shape
    width = own.shape[1]
    _, blocks = places(chips, rows, own_last, width)
    for which, (stacked, last) in enumerate(((own, own_last), (other, other_last))):
        for distance in range(4):
            at = pl.ds(pl.multiple_of((index_ref[0] ^ distance) * down, down), down)
            if distance == 3:
                weights[which, at, :] = last[...]
            else:
                for index, block in enumerate(blocks[distance]):
                    weights[which, at, index * width : (index + 1) * width] = stacked[block, :]


def collect(index, chips, rows, own, own_last, other, other_last):
    down, out_features = own_last.shape
    shape = (2, 4 * down, out_features)
    return pl.pallas_call(
        functools.partial(weights_kernel, chips, rows),
        out_shape=like(shape, own),
        in_specs=[SMEM] + [VMEM] * 4,
        out_specs=VMEM,
        compiler_params=PARAMS,
        cost_estimate=cost(4 * math.prod(shape)),
        name="collect",
    )(index, own, own_last, other, other_last)


def attend_kernel(distances, chips, me_ref, *refs):
    many = len(distances)
    parts, (own, other, attended, queries, result) = refs[:many], refs[many:]
    total, width = queries.shape
    rows = total // many
    half = width // 2
    chip, core = me_ref[0] // 2, me_ref[0] % 2
    scale = HEAD_DIM ** (-0.5) * math.log2(math.e)

    def attend_from(here):
        order = sorted(here ^ distance for distance in distances)
        place = {chip: index * rows for index, chip in enumerate(order)}
        for distance, part in zip(distances, parts):
            at = place[here ^ distance]
            queries[at : at + rows, :] = part[...]
        row = lax.broadcasted_iota(jnp.int32, (rows, 2 * rows), 0)
        column = lax.broadcasted_iota(jnp.int32, (rows, 2 * rows), 1)
        causal = jnp.where(column < rows, row, 2 * rows * core - 1) >= column

        def both(index, columns):
            at = slice(index * rows, (index + 1) * rows)
            return jnp.concatenate([own[at, columns], other[at, columns]], axis=0)

        ones = jnp.ones((2 * rows, LANES), own.dtype)
        for head in range(width // HEAD_DIM):
            columns = slice(head * HEAD_DIM, (head + 1) * HEAD_DIM)
            tiles = []
            for c in range(order[-1] + 1):
                first = min(place[chip] for chip in order if chip >= c)
                score = lax.dot_general(
                    queries[first : many * rows, columns],
                    both(2 * (here ^ c), columns),
                    (((1,), (1,)), ((), ())),
                    preferred_element_type=jnp.float32,
                )
                if c in place:
                    masked = jnp.where(causal, score[:rows], -jnp.inf)
                    later = [score[rows:]] if first + rows < many * rows else []
                    score = jnp.concatenate([masked, *later], axis=0)
                tiles.append((c, first, score))
            highest = []
            for chip in order:
                best = None
                for c, first, score in tiles:
                    if c <= chip:
                        at = place[chip] - first
                        block = score[at : at + rows]
                        best = block if best is None else jnp.maximum(best, block)
                highest.append(jnp.max(best, axis=1, keepdims=True))
            highest = jnp.concatenate(highest, axis=0)
            totals, start = None, 0
            for c, first, score in tiles:
                expons = jnp.exp2((score - highest[first:]) * scale).astype(jnp.bfloat16)
                seen = jnp.concatenate([both(2 * (here ^ c) + 1, columns), ones], axis=1)
                total = jnp.dot(expons, seen, preferred_element_type=jnp.float32)
                totals = total if totals is None else totals[first - start :] + total
                start = first
                if c in place:
                    result[first : first + rows, columns] = (
                        totals[:rows, :HEAD_DIM] / totals[:rows, HEAD_DIM:]
                    ).astype(result.dtype)
        for index, distance in enumerate(distances):
            at = place[here ^ distance]
            for part in range(2):
                attended[part, index * rows : (index + 1) * rows, :] = result[
                    at : at + rows, part * half : (part + 1) * half
                ]

    for here in range(chips):
        pl.when(chip == here)(functools.partial(attend_from, here))


def attend(me, distances, parts, own, other, chips):
    rows, width = parts[0].shape[-2:]
    length = 2 * chips * rows
    total = len(parts) * rows
    return pl.pallas_call(
        functools.partial(attend_kernel, distances, chips),
        out_shape=like((2, total, width // 2), own),
        in_specs=[SMEM] + [VMEM] * (len(parts) + 2),
        out_specs=VMEM,
        scratch_shapes=[pltpu.VMEM((total, width), own.dtype)] * 2,
        compiler_params=PARAMS,
        cost_estimate=cost(
            4 * length * width + 4 * total * width,
            4 * total * length * width,
            total * length * (width // HEAD_DIM),
        ),
        name="attend",
    )(me, *parts, own, other)


def project_kernel(me_ref, attended, weights, *outs):
    core = me_ref[0] % 2
    product = jnp.dot(attended[core], weights[0], preferred_element_type=jnp.float32)
    product += jnp.dot(attended[1 - core], weights[1], preferred_element_type=jnp.float32)
    rows, columns = outs[0].shape
    across = product.shape[1] // columns
    for index, out in enumerate(outs):
        down, right = index // across * rows, index % across * columns
        out[...] = product[down : down + rows, right : right + columns].astype(out.dtype)


def project(me, attended, weights, shape, kind):
    _, total, features = attended.shape
    width = weights.shape[2]
    many = total * width // math.prod(shape)
    return pl.pallas_call(
        project_kernel,
        out_shape=[jax.ShapeDtypeStruct(shape, kind)] * many,
        in_specs=[SMEM] + [VMEM] * 2,
        out_specs=[VMEM] * many,
        compiler_params=PARAMS,
        cost_estimate=cost(
            4 * total * features + 4 * features * width + 4 * total * width,
            4 * total * features * width,
        ),
        name="project",
    )(me, attended, weights)


def add_kernel(marks, *refs):
    products, (left, right), outs = refs[: len(marks)], refs[len(marks) : -len(marks)], refs[-len(marks) :]
    half = left.shape[1]
    for mark, product, out in zip(marks, products, outs):
        out[...] = product[...].astype(out.dtype)
        if mark == 1:
            out[:, :half] = (product[:, :half] + left[...].astype(jnp.float32)).astype(out.dtype)
        if mark == 2:
            out[:, half:] = (product[:, half:] + right[...].astype(jnp.float32)).astype(out.dtype)


def add(marks, products, left, right):
    return pl.pallas_call(
        functools.partial(add_kernel, marks),
        out_shape=[like(product.shape, left) for product in products],
        in_specs=[VMEM] * (len(products) + 2),
        out_specs=[VMEM] * len(products),
        compiler_params=PARAMS,
        cost_estimate=cost(8 * len(products) * products[0].size),
        name="add",
    )(*products, left, right)


def make_body(seq_count, dp_count):
    chips = seq_count // 2
    far = chips - 1

    def to_chip(part, distance):
        return swap(part, "seq", seq_count, 2 * distance)

    def exchange(parts):
        got = [to_chip(part, d) if d else part for d, part in enumerate(parts)]
        return [*got[:-1], lax.optimization_barrier(got[-1])]

    def body(queries, keys, values, master, moment, second, gradient):
        rows = queries.shape[1]
        out_features = master.shape[1]
        me = lax.axis_index("seq").astype(jnp.int32).reshape(1)
        place = lax.axis_index("dp").astype(jnp.int32)

        sent_pairs, own_queries = pack(me, keys, values, queries, chips)
        pairs = exchange(sent_pairs)

        state, _ = lax.optimization_barrier(((master, moment, second, gradient), sent_pairs))
        weight = weigh(*state)[None]
        span = 1
        while 4 * span < dp_count:
            many = 4 if dp_count // span % 16 == 0 else 2
            pieces = [weight] + [swap(weight, "dp", dp_count, span * d) for d in range(1, many)]
            weight = merge((place // span % many).reshape(1), pieces)
            weight = weight.reshape(-1, *weight.shape[2:])
            span *= many
        weight = weight.reshape(-1, out_features)
        pieces = [weight] + [swap(weight, "dp", dp_count, span * d) for d in (1, 2)]
        queries, _ = lax.optimization_barrier((queries, weight))
        sent_queries = pack_queries(me, queries, chips)
        pairs, sent_queries = lax.optimization_barrier((pairs, sent_queries))
        own = stack(pairs, pieces)
        forwarded = swap(pieces[2], "dp", dp_count, span)

        other = swap(own, "seq", seq_count, 1)
        sent_queries, _ = lax.optimization_barrier((sent_queries, own))
        own_queries = exchange([own_queries, *sent_queries])

        attended = attend(me, (far,), own_queries[far:], own, other, chips)
        near_queries, others, attended = lax.optimization_barrier(
            (own_queries[:far], swap(forwarded, "seq", seq_count, 1), attended)
        )
        index = (place // span % 4).reshape(1)
        weights = collect(index, chips, rows, own, forwarded, other, others)
        halves = project(me, attended, weights, (rows, out_features // 2), attended.dtype)
        left, right = to_chip(halves[0], 1), to_chip(halves[1], 2)
        near = tuple(range(far))
        attended = attend(me, near, near_queries, own, other, chips)
        projected, *products = project(me, attended, weights, (rows, out_features), jnp.float32)
        marks = [{far ^ 1: 1, far ^ 2: 2}.get(d, 0) for d in near[1:]]
        sent = add(marks, products, left, right)
        for d, block in zip(near[1:], sent):
            projected += to_chip(block, d).astype(jnp.float32)
        projected = projected.astype(jnp.bfloat16)[None]
        return (projected, adamw(master, moment, second, gradient))

    return body


def solution(mesh):
    tokens = P("dp", "seq", None)
    rows = P(("seq", "dp"), None)
    return jax.shard_map(
        make_body(mesh.shape["seq"], mesh.shape["dp"]),
        mesh=mesh,
        in_specs=(tokens,) * 3 + (rows,) * 4,
        out_specs=(tokens, rows),
        check_vma=False,
    )
```

time: 47.1 us -> 46 us (0.977)
  waiting for transfers between devices: 18.3 us -> 14 us
  Pallas kernels: 8.37 us -> 9.71 us
  other arithmetic: 0.8 us -> 1.71 us
  starting transfers between devices: 18.7 us -> 19.5 us
    ppermute x15, waiting for transfers between devices: 18.3 us -> 14 us  [swap(): return lax.ppermute(array, axis, [(i, i ^ distance) for i in range(count)])]
    pallas_call x7, Pallas kernels: 7.42 us -> 8.75 us  [the longest x2 4.03 us: attend(): pl.pallas_call(functools.partial(attend_kernel, distances, chips), out_sh...]
    sub x0 -> x1, other arithmetic: none -> 0.91 us  [adamw(): master - learning_rate * (moment_hat / (jnp.sqrt(second_hat) + epsilon) +...]
    ppermute x15, starting transfers between devices: 18.7 us -> 19.5 us  [swap(): return lax.ppermute(array, axis, [(i, i ^ distance) for i in range(count)])]
  transfers between devices with their start and end apart: 15 -> 15, of which waited for: 9 -> 6; matrix products, arithmetic and copies ran while one was open for 0% -> 2% of each run, Pallas kernels for 13% -> 17%
where the time goes in v5:
time: 46 us; the launch traced here: 45.8 us
  starting transfers between devices  19.5 us (42%)
  waiting for transfers between devices  14 us (30%)
  Pallas kernels  9.71 us (21%)
  other arithmetic  1.71 us (4%)
  between operations  0.81 us (2%)
    ppermute x15, starting transfers between devices, swap(): return lax.ppermute(array, axis, [(i, i ^ distance) for i in range(count)])  19.5 us
    ppermute x15, waiting for transfers between devices, swap(): return lax.ppermute(array, axis, [(i, i ^ distance) for i in range(count)])  14 us
    pallas_call x2, Pallas kernels, attend(): pl.pallas_call(functools.partial(attend_kernel, distances, chips), out_sh...  4.03 us
    pallas_call x1, Pallas kernels, pack_queries(): pl.pallas_call(pack_queries_kernel, out_shape=[pltpu.HBM((rows, width), q...  1.71 us
    pallas_call x1, Pallas kernels, weigh(): pl.pallas_call(weigh_kernel, out_shape=jax.ShapeDtypeStruct(shape, jnp.bf...  1.43 us
    pallas_call x1, Pallas kernels, pack(): pl.pallas_call(pack_kernel, out_shape=[like((2, rows, width), queries)] *...  1.42 us
  transfers between devices with their start and end apart: 15, of which 6 were waited for; matrix products, arithmetic and copies ran while one was open for 2% of the time, Pallas kernels for 17%

profile of v5, /device:TPU:0, one launch (start us, length us, event | category | flops | bytes accessed | tf_op | source)
XLA Modules:
  0.0 45.8 jit_solution(10520680609318004086)
XLA Ops:
  0.6 1.4 %pack.1 = (bf16[2,128,512]{2,1,0:T(8,128)(2,1)S(1)}, bf16[2,128,512]{2,1,0:T(8,128)(2,1)S(1)}, bf16[2,128,512]{2,1,0:T(8,128)(2,1)S(1)}, bf16[2,128,512]{2,1,0:T(8,128)(2,1)S(1)}, bf16[128,512]{1,0:T(8,128)(2,1)S(1)}) custom-call(s32[1]{0:T(128)} %bitcast.me_ref, bf16[1,128,2048]{2,1,0:T(8,128)(2,1)} %keys.1, bf16[1,128,2048]{2,1,0:T(8,128)(2,1)} %values.1, ...), custom_call_target="tpu_custom_call" | custom-call | bytes 2097152 | tf_op jit(solution)/shard_map/pack/pallas_call | solution.py:82
  2.1 4.0 %collective-permute-start.2 = (bf16[2,128,512]{2,1,0:T(8,128)(2,1)S(1)}, bf16[2,128,512]{2,1,0:T(8,128)(2,1)S(1)}, u32[]{:S(2)}, u32[]{:S(2)}) collective-permute-start(bf16[2,128,512]{2,1,0:T(8,128)(2,1)S(1)} %get-tuple-element.41), channel_id=1, source_target_pairs={{0,24},{4,28},{8,16},{12,20},{16,8},{20,12},{24,0},{28,4},{1,25},{... | collective-permute-start | bytes 786440 | tf_op jit(solution)/shard_map/ppermute | solution.py:34
  6.0 0.5 %collective-permute-start = (bf16[2,128,512]{2,1,0:T(8,128)(2,1)S(1)}, bf16[2,128,512]{2,1,0:T(8,128)(2,1)S(1)}, u32[]{:S(2)}, u32[]{:S(2)}) collective-permute-start(bf16[2,128,512]{2,1,0:T(8,128)(2,1)S(1)} %get-tuple-element.39), channel_id=1, source_target_pairs={{0,8},{4,12},{8,0},{12,4},{16,24},{20,28},{24,16},{28,20},{1,9},{5... | collective-permute-start | bytes 786440 | tf_op jit(solution)/shard_map/ppermute | solution.py:34
  6.6 0.1 collective-permute-start.1
  6.7 1.4 %weigh.1.refs_4_ = bf16[64,1024]{1,0:T(8,128)(2,1)S(1)} custom-call(f32[64,1024]{1,0:T(8,128)} %refs_0_, f32[64,1024]{1,0:T(8,128)} %refs_1_, f32[64,1024]{1,0:T(8,128)} %refs_2_, f32[64,1024]{1,0:T(8,128)} %refs_3_), custom_call_target="tpu_custom_call" | custom-call | bytes 1179648 | tf_op jit(solution)/shard_map/weigh/pallas_call | solution.py:164
  8.1 2.0 %collective-permute-start.3 = (bf16[64,1024]{1,0:T(8,128)(2,1)S(1)}, bf16[64,1024]{1,0:T(8,128)(2,1)S(1)}, u32[]{:S(2)}, u32[]{:S(2)}) collective-permute-start(bf16[64,1024]{1,0:T(8,128)(2,1)S(1)} %weigh.1.refs_4_), channel_id=1, source_target_pairs={{0,1},{1,0},{2,3},{3,2},{4,5},{5,4},{6,7},{7,6},{8,9},{9,8},{10,11... | collective-permute-start | bytes 393224 | tf_op jit(solution)/shard_map/ppermute | solution.py:34
  10.1 2.6 %collective-permute-start.4 = (bf16[64,1024]{1,0:T(8,128)(2,1)S(1)}, bf16[64,1024]{1,0:T(8,128)(2,1)S(1)}, u32[]{:S(2)}, u32[]{:S(2)}) collective-permute-start(bf16[64,1024]{1,0:T(8,128)(2,1)S(1)} %weigh.1.refs_4_), channel_id=1, source_target_pairs={{0,2},{1,3},{2,0},{3,1},{4,6},{5,7},{6,4},{7,5},{8,10},{9,11},{10,... | collective-permute-start | bytes 393224 | tf_op jit(solution)/shard_map/ppermute | solution.py:34
  12.7 1.7 %pack_queries.1 = (bf16[128,512]{1,0:T(8,128)(2,1)}, bf16[128,512]{1,0:T(8,128)(2,1)}, bf16[128,512]{1,0:T(8,128)(2,1)}) custom-call(s32[1]{0:T(128)} %bitcast.me_ref, bf16[1,128,2048]{2,1,0:T(8,128)(2,1)} %queries.2), custom_call_target="tpu_custom_call" | custom-call | bytes 1048576 | tf_op jit(solution)/shard_map/pack_queries/pallas_call | solution.py:123
  14.4 0.0 collective-permute-done.2.refs_3_
  14.5 3.8 %collective-permute-done.refs_1_ = bf16[2,128,512]{2,1,0:T(8,128)(2,1)S(1)} collective-permute-done((bf16[2,128,512]{2,1,0:T(8,128)(2,1)S(1)}, bf16[2,128,512]{2,1,0:T(8,128)(2,1)S(1)}, u32[]{:S(2)}, u32[]{:S(2)}) %collective-permute-start) | collective-permute-done | bytes 262176 | tf_op jit(solution)/shard_map/ppermute | solution.py:34
  18.2 0.0 collective-permute-done.1.refs_2_
  18.2 0.0 collective-permute-done.3.refs_5_
  18.2 0.0 collective-permute-done.4.refs_6_
  18.2 0.1 stack.1.refs_1_.refs_3_.own
  18.4 0.1 collective-permute-start.10
  18.4 1.6 %collective-permute-start.7 = (bf16[64,1024]{1,0:T(8,128)(2,1)S(1)}, bf16[64,1024]{1,0:T(8,128)(2,1)S(1)}, u32[]{:S(2)}, u32[]{:S(2)}) collective-permute-start(bf16[64,1024]{1,0:T(8,128)(2,1)S(1)} %collective-permute-done.4.refs_6_), channel_id=1, source_target_pairs={{0,1},{1,0},{2,3},{3,2},{4,5},{5,4},{6,7},{7,6},{8,9},{9,8},{10,11... | collective-permute-start | bytes 393224 | tf_op jit(solution)/shard_map/ppermute | solution.py:34
  20.1 2.3 %collective-permute-start.9 = (bf16[128,512]{1,0:T(8,128)(2,1)}, bf16[128,512]{1,0:T(8,128)(2,1)}, u32[]{:S(2)}, u32[]{:S(2)}) collective-permute-start(bf16[128,512]{1,0:T(8,128)(2,1)} %get-tuple-element.59), channel_id=1, source_target_pairs={{0,24},{4,28},{8,16},{12,20},{16,8},{20,12},{24,0},{28,4},{1,25},{... | collective-permute-start | bytes 393224 | tf_op jit(solution)/shard_map/ppermute | solution.py:34
  22.4 0.5 %collective-permute-start.5 = (bf16[128,512]{1,0:T(8,128)(2,1)}, bf16[128,512]{1,0:T(8,128)(2,1)S(1)}, u32[]{:S(2)}, u32[]{:S(2)}) collective-permute-start(bf16[128,512]{1,0:T(8,128)(2,1)} %get-tuple-element.57), channel_id=1, source_target_pairs={{0,8},{4,12},{8,0},{12,4},{16,24},{20,28},{24,16},{28,20},{1,9},{5... | collective-permute-start | bytes 393224 | tf_op jit(solution)/shard_map/ppermute | solution.py:34
  22.9 0.6 %collective-permute-start.6 = (bf16[128,512]{1,0:T(8,128)(2,1)}, bf16[128,512]{1,0:T(8,128)(2,1)S(1)}, u32[]{:S(2)}, u32[]{:S(2)}) collective-permute-start(bf16[128,512]{1,0:T(8,128)(2,1)} %get-tuple-element.58), channel_id=1, source_target_pairs={{0,16},{4,20},{8,24},{12,28},{16,0},{20,4},{24,8},{28,12},{1,17},{... | collective-permute-start | bytes 393224 | tf_op jit(solution)/shard_map/ppermute | solution.py:34
  23.6 0.8 %collective-permute-done.7.own_last = bf16[64,1024]{1,0:T(8,128)(2,1)S(1)} collective-permute-done((bf16[64,1024]{1,0:T(8,128)(2,1)S(1)}, bf16[64,1024]{1,0:T(8,128)(2,1)S(1)}, u32[]{:S(2)}, u32[]{:S(2)}) %collective-permute-start.7) | collective-permute-done | bytes 131104 | tf_op jit(solution)/shard_map/ppermute | solution.py:34
  24.3 0.0 collective-permute-start.8
  24.3 3.3 %collective-permute-done.9.refs_0_ = bf16[128,512]{1,0:T(8,128)(2,1)} collective-permute-done((bf16[128,512]{1,0:T(8,128)(2,1)}, bf16[128,512]{1,0:T(8,128)(2,1)}, u32[]{:S(2)}, u32[]{:S(2)}) %collective-permute-start.9) | collective-permute-done | bytes 131104 | tf_op jit(solution)/shard_map/ppermute | solution.py:34
  27.6 0.0 collective-permute-done.10.refs_2_.refs_4_.other
  27.6 2.0 %attend.2.attended = bf16[2,128,256]{2,1,0:T(8,128)(2,1)S(1)} custom-call(s32[1]{0:T(128)} %bitcast.me_ref, bf16[128,512]{1,0:T(8,128)(2,1)} %collective-permute-done.9.refs_0_, bf16[1408,512]{1,0:T(8,128)(2,1)S(1)} %stack.1.refs_1_.refs_3_.own, bf16[1408,512]{1,0:T(8,128)(2,1)S(1)} %collective-permute-done.10.refs_2_.refs_4_.other), custom_call_target="tpu_custom_call" | custom-call | flops 268435456 | bytes 2359296 | tf_op jit(solution)/shard_map/attend/pallas_call | solution.py:335
  29.6 0.0 collective-permute-done.5.refs_1_
  29.6 0.0 collective-permute-done.6.refs_2_
  29.6 0.0 collective-permute-done.8.other_last
  29.6 0.1 collect.1.weights
  29.7 0.3 project.3
  30.0 1.5 %collective-permute-start.11 = (bf16[128,512]{1,0:T(8,128)(2,1)S(1)}, bf16[128,512]{1,0:T(8,128)(2,1)S(1)}, u32[]{:S(2)}, u32[]{:S(2)}) collective-permute-start(bf16[128,512]{1,0:T(8,128)(2,1)S(1)} %get-tuple-element.68), channel_id=1, source_target_pairs={{0,8},{4,12},{8,0},{12,4},{16,24},{20,28},{24,16},{28,20},{1,9},{5... | collective-permute-start | bytes 393224 | tf_op jit(solution)/shard_map/ppermute | solution.py:34
  31.5 1.4 %collective-permute-start.12 = (bf16[128,512]{1,0:T(8,128)(2,1)S(1)}, bf16[128,512]{1,0:T(8,128)(2,1)S(1)}, u32[]{:S(2)}, u32[]{:S(2)}) collective-permute-start(bf16[128,512]{1,0:T(8,128)(2,1)S(1)} %get-tuple-element.69), channel_id=1, source_target_pairs={{0,16},{4,20},{8,24},{12,28},{16,0},{20,4},{24,8},{28,12},{1,17},{... | collective-permute-start | bytes 393224 | tf_op jit(solution)/shard_map/ppermute | solution.py:34
  32.9 2.1 %attend.3.attended = bf16[2,384,256]{2,1,0:T(8,128)(2,1)S(1)} custom-call(s32[1]{0:T(128)} %bitcast.me_ref, bf16[128,512]{1,0:T(8,128)(2,1)S(1)} %get-tuple-element.60.refs_0_, bf16[128,512]{1,0:T(8,128)(2,1)S(1)} %collective-permute-done.5.refs_1_, bf16[128,512]{1,0:T(8,128)(2,1)S(1)} %collective-permute-done.6.refs_2_, ...), custom_call_target="tpu_custom_call" | custom-call | flops 805306368 | bytes 2883584 | tf_op jit(solution)/shard_map/attend/pallas_call | solution.py:335
  35.0 0.0 copy-start
  35.0 0.0 copy-start.1
  35.0 0.0 copy-start.2
  35.0 0.0 copy-start.3
  35.0 0.6 %project.2 = (f32[128,1024]{1,0:T(8,128)S(1)}, f32[128,1024]{1,0:T(8,128)S(1)}, f32[128,1024]{1,0:T(8,128)S(1)}) custom-call(s32[1]{0:T(128)} %bitcast.me_ref, bf16[2,384,256]{2,1,0:T(8,128)(2,1)S(1)} %attend.3.attended, bf16[2,256,1024]{2,1,0:T(8,128)(2,1)S(1)} %collect.1.weights), custom_call_target="tpu_custom_call" | custom-call | flops 402653184 | bytes 3014656 | tf_op jit(solution)/shard_map/project/pallas_call | solution.py:366
  35.6 0.0 collective-permute-done.11.refs_2_
  35.6 0.9 %collective-permute-done.12.refs_3_ = bf16[128,512]{1,0:T(8,128)(2,1)S(1)} collective-permute-done((bf16[128,512]{1,0:T(8,128)(2,1)S(1)}, bf16[128,512]{1,0:T(8,128)(2,1)S(1)}, u32[]{:S(2)}, u32[]{:S(2)}) %collective-permute-start.12) | collective-permute-done | bytes 131104 | tf_op jit(solution)/shard_map/ppermute | solution.py:34
  36.5 0.1 add.66
  36.6 1.6 %collective-permute-start.14 = (bf16[128,1024]{1,0:T(8,128)(2,1)S(1)}, bf16[128,1024]{1,0:T(8,128)(2,1)S(1)}, u32[]{:S(2)}, u32[]{:S(2)}) collective-permute-start(bf16[128,1024]{1,0:T(8,128)(2,1)S(1)} %get-tuple-element.71), channel_id=1, source_target_pairs={{0,16},{4,20},{8,24},{12,28},{16,0},{20,4},{24,8},{28,12},{1,17},{... | collective-permute-start | bytes 786440 | tf_op jit(solution)/shard_map/ppermute | solution.py:34
  38.2 0.5 %collective-permute-start.13 = (bf16[128,1024]{1,0:T(8,128)(2,1)S(1)}, bf16[128,1024]{1,0:T(8,128)(2,1)S(1)}, u32[]{:S(2)}, u32[]{:S(2)}) collective-permute-start(bf16[128,1024]{1,0:T(8,128)(2,1)S(1)} %get-tuple-element.70), channel_id=1, source_target_pairs={{0,8},{4,12},{8,0},{12,4},{16,24},{20,28},{24,16},{28,20},{1,9},{5... | collective-permute-start | bytes 786440 | tf_op jit(solution)/shard_map/ppermute | solution.py:34
  38.7 0.0 copy-done
  38.7 0.0 copy-done.1
  38.8 0.9 %multiply_subtract_fusion = f32[64,1024]{1,0:T(8,128)} fusion(f32[64,1024]{1,0:T(8,128)S(1)} %copy-done, f32[64,1024]{1,0:T(8,128)S(1)} %copy-done.3, f32[64,1024]{1,0:T(8,128)S(1)} %copy-done.2, f32[64,1024]{1,0:T(8,128)S(1)} %copy-done.1), kind=kLoop, calls=%fused_computation.9 | loop fusion | flops 983040 | bytes 1310720 | tf_op jit(solution)/shard_map/sub | solution.py:28
  39.7 3.9 %collective-permute-done.14 = bf16[128,1024]{1,0:T(8,128)(2,1)S(1)} collective-permute-done((bf16[128,1024]{1,0:T(8,128)(2,1)S(1)}, bf16[128,1024]{1,0:T(8,128)(2,1)S(1)}, u32[]{:S(2)}, u32[]{:S(2)}) %collective-permute-start.14) | collective-permute-done | bytes 262176 | tf_op jit(solution)/shard_map/ppermute | solution.py:34
  43.5 1.5 %collective-permute-done.13 = bf16[128,1024]{1,0:T(8,128)(2,1)S(1)} collective-permute-done((bf16[128,1024]{1,0:T(8,128)(2,1)S(1)}, bf16[128,1024]{1,0:T(8,128)(2,1)S(1)}, u32[]{:S(2)}, u32[]{:S(2)}) %collective-permute-start.13) | collective-permute-done | bytes 262176 | tf_op jit(solution)/shard_map/ppermute | solution.py:34
  45.0 0.8 %fusion.6 = bf16[1,128,1024]{2,1,0:T(8,128)(2,1)} fusion(bf16[128,1024]{1,0:T(8,128)(2,1)S(1)} %collective-permute-done.14, f32[128,1024]{1,0:T(8,128)S(1)} %get-tuple-element.64, bf16[128,1024]{1,0:T(8,128)(2,1)S(1)} %collective-permute-done.13), kind=kLoop, calls=%fused_computation.8 | loop fusion | flops 655360 | bytes 1310720 | tf_op jit(solution)/shard_map/broadcast_in_dim | solution.py:459
  (2 shorter events, 0.0 us)
Async XLA Ops:
  2.1 12.4 %collective-permute-start.2 = (bf16[2,128,512]{2,1,0:T(8,128)(2,1)S(1)}, bf16[2,128,512]{2,1,0:T(8,128)(2,1)S(1)}, u32[]{:S(2)}, u32[]{:S(2)}) collective-permute-start(bf16[2,128,512]{2,1,0:T(8,128)(2,1)S(1)} %get-tuple-element.41), channel_id=1, source_target_pairs={{0,24},{4,28},{8,16},{12,20},{16,8},{20,12},{24,0},{28,4},{1,25},{... | collective-permute-start | bytes 786440 | tf_op jit(solution)/shard_map/ppermute | solution.py:34
  6.0 12.2 %collective-permute-start = (bf16[2,128,512]{2,1,0:T(8,128)(2,1)S(1)}, bf16[2,128,512]{2,1,0:T(8,128)(2,1)S(1)}, u32[]{:S(2)}, u32[]{:S(2)}) collective-permute-start(bf16[2,128,512]{2,1,0:T(8,128)(2,1)S(1)} %get-tuple-element.39), channel_id=1, source_target_pairs={{0,8},{4,12},{8,0},{12,4},{16,24},{20,28},{24,16},{28,20},{1,9},{5... | collective-permute-start | bytes 786440 | tf_op jit(solution)/shard_map/ppermute | solution.py:34
  6.6 11.7 %collective-permute-start.1 = (bf16[2,128,512]{2,1,0:T(8,128)(2,1)S(1)}, bf16[2,128,512]{2,1,0:T(8,128)(2,1)S(1)}, u32[]{:S(2)}, u32[]{:S(2)}) collective-permute-start(bf16[2,128,512]{2,1,0:T(8,128)(2,1)S(1)} %get-tuple-element.40), channel_id=1, source_target_pairs={{0,16},{4,20},{8,24},{12,28},{16,0},{20,4},{24,8},{28,12},{1,17},{... | collective-permute-start | bytes 786440 | tf_op jit(solution)/shard_map/ppermute | solution.py:34
  8.1 10.1 %collective-permute-start.3 = (bf16[64,1024]{1,0:T(8,128)(2,1)S(1)}, bf16[64,1024]{1,0:T(8,128)(2,1)S(1)}, u32[]{:S(2)}, u32[]{:S(2)}) collective-permute-start(bf16[64,1024]{1,0:T(8,128)(2,1)S(1)} %weigh.1.refs_4_), channel_id=1, source_target_pairs={{0,1},{1,0},{2,3},{3,2},{4,5},{5,4},{6,7},{7,6},{8,9},{9,8},{10,11... | collective-permute-start | bytes 393224 | tf_op jit(solution)/shard_map/ppermute | solution.py:34
  10.1 8.1 %collective-permute-start.4 = (bf16[64,1024]{1,0:T(8,128)(2,1)S(1)}, bf16[64,1024]{1,0:T(8,128)(2,1)S(1)}, u32[]{:S(2)}, u32[]{:S(2)}) collective-permute-start(bf16[64,1024]{1,0:T(8,128)(2,1)S(1)} %weigh.1.refs_4_), channel_id=1, source_target_pairs={{0,2},{1,3},{2,0},{3,1},{4,6},{5,7},{6,4},{7,5},{8,10},{9,11},{10,... | collective-permute-start | bytes 393224 | tf_op jit(solution)/shard_map/ppermute | solution.py:34
  18.4 9.3 %collective-permute-start.10 = (bf16[1408,512]{1,0:T(8,128)(2,1)S(1)}, bf16[1408,512]{1,0:T(8,128)(2,1)S(1)}, u32[]{:S(2)}, u32[]{:S(2)}) collective-permute-start(bf16[1408,512]{1,0:T(8,128)(2,1)S(1)} %stack.1.refs_1_.refs_3_.own), channel_id=1, source_target_pairs={{0,4},{4,0},{8,12},{12,8},{16,20},{20,16},{24,28},{28,24},{1,5},{5... | collective-permute-start | bytes 4325384 | tf_op jit(solution)/shard_map/ppermute | solution.py:34
  18.4 5.9 %collective-permute-start.7 = (bf16[64,1024]{1,0:T(8,128)(2,1)S(1)}, bf16[64,1024]{1,0:T(8,128)(2,1)S(1)}, u32[]{:S(2)}, u32[]{:S(2)}) collective-permute-start(bf16[64,1024]{1,0:T(8,128)(2,1)S(1)} %collective-permute-done.4.refs_6_), channel_id=1, source_target_pairs={{0,1},{1,0},{2,3},{3,2},{4,5},{5,4},{6,7},{7,6},{8,9},{9,8},{10,11... | collective-permute-start | bytes 393224 | tf_op jit(solution)/shard_map/ppermute | solution.py:34
  20.1 7.6 %collective-permute-start.9 = (bf16[128,512]{1,0:T(8,128)(2,1)}, bf16[128,512]{1,0:T(8,128)(2,1)}, u32[]{:S(2)}, u32[]{:S(2)}) collective-permute-start(bf16[128,512]{1,0:T(8,128)(2,1)} %get-tuple-element.59), channel_id=1, source_target_pairs={{0,24},{4,28},{8,16},{12,20},{16,8},{20,12},{24,0},{28,4},{1,25},{... | collective-permute-start | bytes 393224 | tf_op jit(solution)/shard_map/ppermute | solution.py:34
  22.4 7.2 %collective-permute-start.5 = (bf16[128,512]{1,0:T(8,128)(2,1)}, bf16[128,512]{1,0:T(8,128)(2,1)S(1)}, u32[]{:S(2)}, u32[]{:S(2)}) collective-permute-start(bf16[128,512]{1,0:T(8,128)(2,1)} %get-tuple-element.57), channel_id=1, source_target_pairs={{0,8},{4,12},{8,0},{12,4},{16,24},{20,28},{24,16},{28,20},{1,9},{5... | collective-permute-start | bytes 393224 | tf_op jit(solution)/shard_map/ppermute | solution.py:34
  22.9 6.7 %collective-permute-start.6 = (bf16[128,512]{1,0:T(8,128)(2,1)}, bf16[128,512]{1,0:T(8,128)(2,1)S(1)}, u32[]{:S(2)}, u32[]{:S(2)}) collective-permute-start(bf16[128,512]{1,0:T(8,128)(2,1)} %get-tuple-element.58), channel_id=1, source_target_pairs={{0,16},{4,20},{8,24},{12,28},{16,0},{20,4},{24,8},{28,12},{1,17},{... | collective-permute-start | bytes 393224 | tf_op jit(solution)/shard_map/ppermute | solution.py:34
  24.3 5.3 %collective-permute-start.8 = (bf16[64,1024]{1,0:T(8,128)(2,1)S(1)}, bf16[64,1024]{1,0:T(8,128)(2,1)S(1)}, u32[]{:S(2)}, u32[]{:S(2)}) collective-permute-start(bf16[64,1024]{1,0:T(8,128)(2,1)S(1)} %collective-permute-done.7.own_last), channel_id=1, source_target_pairs={{0,4},{4,0},{8,12},{12,8},{16,20},{20,16},{24,28},{28,24},{1,5},{5... | collective-permute-start | bytes 393224 | tf_op jit(solution)/shard_map/ppermute | solution.py:34
  30.0 5.6 %collective-permute-start.11 = (bf16[128,512]{1,0:T(8,128)(2,1)S(1)}, bf16[128,512]{1,0:T(8,128)(2,1)S(1)}, u32[]{:S(2)}, u32[]{:S(2)}) collective-permute-start(bf16[128,512]{1,0:T(8,128)(2,1)S(1)} %get-tuple-element.68), channel_id=1, source_target_pairs={{0,8},{4,12},{8,0},{12,4},{16,24},{20,28},{24,16},{28,20},{1,9},{5... | collective-permute-start | bytes 393224 | tf_op jit(solution)/shard_map/ppermute | solution.py:34
  31.5 5.0 %collective-permute-start.12 = (bf16[128,512]{1,0:T(8,128)(2,1)S(1)}, bf16[128,512]{1,0:T(8,128)(2,1)S(1)}, u32[]{:S(2)}, u32[]{:S(2)}) collective-permute-start(bf16[128,512]{1,0:T(8,128)(2,1)S(1)} %get-tuple-element.69), channel_id=1, source_target_pairs={{0,16},{4,20},{8,24},{12,28},{16,0},{20,4},{24,8},{28,12},{1,17},{... | collective-permute-start | bytes 393224 | tf_op jit(solution)/shard_map/ppermute | solution.py:34
  35.0 3.8 %copy-start = (f32[64,1024]{1,0:T(8,128)S(1)}, f32[64,1024]{1,0:T(8,128)}, u32[]{:S(2)}) copy-start(f32[64,1024]{1,0:T(8,128)} %refs_0_) | copy-start | bytes 786436
  35.0 3.8 %copy-start.1 = (f32[64,1024]{1,0:T(8,128)S(1)}, f32[64,1024]{1,0:T(8,128)}, u32[]{:S(2)}) copy-start(f32[64,1024]{1,0:T(8,128)} %refs_1_) | copy-start | bytes 786436
  35.0 3.7 %copy-start.2 = (f32[64,1024]{1,0:T(8,128)S(1)}, f32[64,1024]{1,0:T(8,128)}, u32[]{:S(2)}) copy-start(f32[64,1024]{1,0:T(8,128)} %refs_2_) | copy-start | bytes 786436
  35.0 3.7 %copy-start.3 = (f32[64,1024]{1,0:T(8,128)S(1)}, f32[64,1024]{1,0:T(8,128)}, u32[]{:S(2)}) copy-start(f32[64,1024]{1,0:T(8,128)} %refs_3_) | copy-start | bytes 786436
  36.6 7.0 %collective-permute-start.14 = (bf16[128,1024]{1,0:T(8,128)(2,1)S(1)}, bf16[128,1024]{1,0:T(8,128)(2,1)S(1)}, u32[]{:S(2)}, u32[]{:S(2)}) collective-permute-start(bf16[128,1024]{1,0:T(8,128)(2,1)S(1)} %get-tuple-element.71), channel_id=1, source_target_pairs={{0,16},{4,20},{8,24},{12,28},{16,0},{20,4},{24,8},{28,12},{1,17},{... | collective-permute-start | bytes 786440 | tf_op jit(solution)/shard_map/ppermute | solution.py:34
  38.2 6.8 %collective-permute-start.13 = (bf16[128,1024]{1,0:T(8,128)(2,1)S(1)}, bf16[128,1024]{1,0:T(8,128)(2,1)S(1)}, u32[]{:S(2)}, u32[]{:S(2)}) collective-permute-start(bf16[128,1024]{1,0:T(8,128)(2,1)S(1)} %get-tuple-element.70), channel_id=1, source_target_pairs={{0,8},{4,12},{8,0},{12,4},{16,24},{20,28},{24,16},{28,20},{1,9},{5... | collective-permute-start | bytes 786440 | tf_op jit(solution)/shard_map/ppermute | solution.py:34

commit v6 on v5

--- a/solution.py
+++ b/solution.py
@@ -93,27 +93,17 @@
 
 
 def pack_queries_kernel(me_ref, queries, *refs):
-    many = len(refs) - 2
-    parts, (held, sems) = refs[:-2], refs[-2:]
-    width = held.shape[2]
-    arrive = [
+    parts, sems = refs[:-1], refs[-1]
+    width = parts[0].shape[1]
+    copies = [
         pltpu.make_async_copy(
-            queries.at[0, :, chip_columns(me_ref, index + 1, width)],
-            held.at[index],
-            sems.at[index],
+            queries.at[0, :, chip_columns(me_ref, distance, width)], part, sems.at[distance - 1]
         )
-        for index in range(many)
+        for distance, part in enumerate(parts, 1)
     ]
-    leave = [
-        pltpu.make_async_copy(held.at[index], part, sems.at[index])
-        for index, part in enumerate(parts)
-    ]
-    for copy in arrive:
+    for copy in copies:
         copy.start()
-    for first, second in zip(arrive, leave):
-        first.wait()
-        second.start()
-    for copy in leave:
+    for copy in copies:
         copy.wait()
 
 
@@ -122,13 +112,10 @@
     width, many = features // chips, chips - 1
     return pl.pallas_call(
         pack_queries_kernel,
-        out_shape=[pltpu.HBM((rows, width), queries.dtype)] * many,
+        out_shape=[like((rows, width), queries)] * many,
         in_specs=[SMEM, HBM],
-        out_specs=[HBM] * many,
-        scratch_shapes=[
-            pltpu.VMEM((many, rows, width), queries.dtype),
-            pltpu.SemaphoreType.DMA((many,)),
-        ],
+        out_specs=[VMEM] * many,
+        scratch_shapes=[pltpu.SemaphoreType.DMA((many,))],
         compiler_params=PARAMS,
         cost_estimate=cost(4 * rows * features),
         name="pack_queries",
@@ -228,32 +215,32 @@
     )(*pairs, *pieces)
 
 
-def weights_kernel(chips, rows, index_ref, own, own_last, other, other_last, weights):
-    down, out_features = own_last.shape
+def collect_kernel(chips, rows, index_ref, own, last, other, weights):
+    down, out_features = last.shape
     width = own.shape[1]
-    _, blocks = places(chips, rows, own_last, width)
-    for which, (stacked, last) in enumerate(((own, own_last), (other, other_last))):
-        for distance in range(4):
+    _, blocks = places(chips, rows, last, width)
+    for which, stacked in enumerate((own, other)):
+        for distance in range(3):
             at = pl.ds(pl.multiple_of((index_ref[0] ^ distance) * down, down), down)
-            if distance == 3:
-                weights[which, at, :] = last[...]
-            else:
-                for index, block in enumerate(blocks[distance]):
-                    weights[which, at, index * width : (index + 1) * width] = stacked[block, :]
-
-
-def collect(index, chips, rows, own, own_last, other, other_last):
-    down, out_features = own_last.shape
+            for index, block in enumerate(blocks[distance]):
+                weights[which, at, index * width : (index + 1) * width] = stacked[block, :]
+    at = pl.ds(pl.multiple_of((index_ref[0] ^ 3) * down, down), down)
+    weights[0, at, :] = last[...]
+    weights[1, at, :] = jnp.zeros_like(last)
+
+
+def collect(index, chips, rows, own, last, other):
+    down, out_features = last.shape
     shape = (2, 4 * down, out_features)
     return pl.pallas_call(
-        functools.partial(weights_kernel, chips, rows),
+        functools.partial(collect_kernel, chips, rows),
         out_shape=like(shape, own),
-        in_specs=[SMEM] + [VMEM] * 4,
+        in_specs=[SMEM] + [VMEM] * 3,
         out_specs=VMEM,
         compiler_params=PARAMS,
         cost_estimate=cost(4 * math.prod(shape)),
         name="collect",
-    )(index, own, own_last, other, other_last)
+    )(index, own, last, other)
 
 
 def attend_kernel(distances, chips, me_ref, *refs):
@@ -348,61 +335,90 @@
     )(me, *parts, own, other)
 
 
-def project_kernel(me_ref, attended, weights, *outs):
+def project_kernel(chips, me_ref, index_ref, attended, weights, last, *refs):
+    outs, other = refs[:-1], refs[-1]
+    down = last.shape[0]
     core = me_ref[0] % 2
+    other[...] = weights[1]
+    other[pl.ds(pl.multiple_of((index_ref[0] ^ 3) * down, down), down), :] = last[...]
     product = jnp.dot(attended[core], weights[0], preferred_element_type=jnp.float32)
-    product += jnp.dot(attended[1 - core], weights[1], preferred_element_type=jnp.float32)
-    rows, columns = outs[0].shape
-    across = product.shape[1] // columns
-    for index, out in enumerate(outs):
-        down, right = index // across * rows, index % across * columns
-        out[...] = product[down : down + rows, right : right + columns].astype(out.dtype)
-
-
-def project(me, attended, weights, shape, kind):
+    product += jnp.dot(attended[1 - core], other[...], preferred_element_type=jnp.float32)
+    rows = outs[0].shape[0]
+
+    def give(out, distance):
+        out[...] = product[distance * rows : (distance + 1) * rows].astype(out.dtype)
+
+    if len(outs) == 1:
+        give(outs[0], 0)
+        return
+    for out, distance in zip(outs[2:], (0, *straight(chips))):
+        give(out, distance)
+    for which in range(2):
+
+        @pl.when(core == which)
+        def _(which=which):
+            give(outs[0], early(chips, which))
+            give(outs[1], late(chips, which))
+
+
+def via(core):
+    return 1 + core
+
+
+def late(chips, core):
+    return chips - 1 ^ via(core)
+
+
+def early(chips, core):
+    return late(chips, 1 - core)
+
+
+def straight(chips):
+    return [d for d in range(1, chips - 1) if d not in (late(chips, 0), late(chips, 1))]
+
+
+def project(me, index, attended, weights, last, chips, kinds):
     _, total, features = attended.shape
     width = weights.shape[2]
-    many = total * width // math.prod(shape)
-    return pl.pallas_call(
-        project_kernel,
-        out_shape=[jax.ShapeDtypeStruct(shape, kind)] * many,
-        in_specs=[SMEM] + [VMEM] * 2,
-        out_specs=[VMEM] * many,
+    return pl.pallas_call(
+        functools.partial(project_kernel, chips),
+        out_shape=[jax.ShapeDtypeStruct((total // len(kinds), width), kind) for kind in kinds],
+        in_specs=[SMEM] * 2 + [VMEM] * 3,
+        out_specs=[VMEM] * len(kinds),
+        scratch_shapes=[pltpu.VMEM(weights.shape[1:], weights.dtype)],
         compiler_params=PARAMS,
         cost_estimate=cost(
-            4 * total * features + 4 * features * width + 4 * total * width,
+            4 * total * features + 6 * features * width + 4 * total * width,
             4 * total * features * width,
         ),
         name="project",
-    )(me, attended, weights)
-
-
-def add_kernel(marks, *refs):
-    products, (left, right), outs = refs[: len(marks)], refs[len(marks) : -len(marks)], refs[-len(marks) :]
-    half = left.shape[1]
-    for mark, product, out in zip(marks, products, outs):
-        out[...] = product[...].astype(out.dtype)
-        if mark == 1:
-            out[:, :half] = (product[:, :half] + left[...].astype(jnp.float32)).astype(out.dtype)
-        if mark == 2:
-            out[:, half:] = (product[:, half:] + right[...].astype(jnp.float32)).astype(out.dtype)
-
-
-def add(marks, products, left, right):
-    return pl.pallas_call(
-        functools.partial(add_kernel, marks),
-        out_shape=[like(product.shape, left) for product in products],
-        in_specs=[VMEM] * (len(products) + 2),
-        out_specs=[VMEM] * len(products),
-        compiler_params=PARAMS,
-        cost_estimate=cost(8 * len(products) * products[0].size),
+    )(me, index, attended, weights, last)
+
+
+def add_kernel(product, passed, out):
+    out[...] = (product[...] + passed[...].astype(jnp.float32)).astype(out.dtype)
+
+
+def add(product, passed):
+    return pl.pallas_call(
+        add_kernel,
+        out_shape=like(passed.shape, passed),
+        in_specs=[VMEM] * 2,
+        out_specs=VMEM,
+        compiler_params=PARAMS,
+        cost_estimate=cost(8 * product.size),
         name="add",
-    )(*products, left, right)
+    )(product, passed)
 
 
 def make_body(seq_count, dp_count):
     chips = seq_count // 2
     far = chips - 1
+
+    def by_core(part, distance):
+        return lax.ppermute(
+            part, "seq", [(i, i ^ 2 * distance(i % 2)) for i in range(seq_count)]
+        )
 
     def to_chip(part, distance):
         return swap(part, "seq", seq_count, 2 * distance)
@@ -442,20 +458,26 @@
         own_queries = exchange([own_queries, *sent_queries])
 
         attended = attend(me, (far,), own_queries[far:], own, other, chips)
-        near_queries, others, attended = lax.optimization_barrier(
-            (own_queries[:far], swap(forwarded, "seq", seq_count, 1), attended)
+        attended, forwarded = lax.optimization_barrier((attended, forwarded))
+        near_queries, others = lax.optimization_barrier(
+            (own_queries[:far], swap(forwarded, "seq", seq_count, 1))
         )
         index = (place // span % 4).reshape(1)
-        weights = collect(index, chips, rows, own, forwarded, other, others)
-        halves = project(me, attended, weights, (rows, out_features // 2), attended.dtype)
-        left, right = to_chip(halves[0], 1), to_chip(halves[1], 2)
-        near = tuple(range(far))
-        attended = attend(me, near, near_queries, own, other, chips)
-        projected, *products = project(me, attended, weights, (rows, out_features), jnp.float32)
-        marks = [{far ^ 1: 1, far ^ 2: 2}.get(d, 0) for d in near[1:]]
-        sent = add(marks, products, left, right)
-        for d, block in zip(near[1:], sent):
-            projected += to_chip(block, d).astype(jnp.float32)
+        weights = collect(index, chips, rows, own, forwarded, other)
+        (product,) = project(me, index, attended, weights, others, chips, [attended.dtype])
+        passed = by_core(product, via)
+        attended = attend(me, tuple(range(far)), near_queries, own, other, chips)
+        kinds = [attended.dtype, jnp.float32, jnp.float32] + [attended.dtype] * (chips - 4)
+        sent, waiting, projected, *rest = project(
+            me, index, attended, weights, others, chips, kinds
+        )
+        got = [by_core(sent, functools.partial(early, chips))]
+        got += [to_chip(product, d) for d, product in zip(straight(chips), rest)]
+        for product in got:
+            projected += product.astype(jnp.float32)
+        projected = lax.optimization_barrier(projected)
+        last = by_core(add(waiting, passed), functools.partial(late, chips))
+        projected += last.astype(jnp.float32)
         projected = projected.astype(jnp.bfloat16)[None]
         return (projected, adamw(master, moment, second, gradient))
 

time: 46 us -> 42.9 us (0.933)
  waiting for transfers between devices: 14 us -> 12.2 us
  starting transfers between devices: 19.5 us -> 18.2 us
    ppermute x15 -> x11, waiting for transfers between devices: 14 us -> 6.28 us  [swap(): return lax.ppermute(array, axis, [(i, i ^ distance) for i in range(count)])]
    ppermute x0 -> x3, waiting for transfers between devices: none -> 5.92 us  [by_core(): lax.ppermute(part, 'seq', [(i, i ^ 2 * distance(i % 2)) for i in range(se...]
    ppermute x15 -> x11, starting transfers between devices: 19.5 us -> 14.4 us  [swap(): return lax.ppermute(array, axis, [(i, i ^ distance) for i in range(count)])]
    ppermute x0 -> x3, starting transfers between devices: none -> 3.79 us  [by_core(): lax.ppermute(part, 'seq', [(i, i ^ 2 * distance(i % 2)) for i in range(se...]
    pallas_call x2, Pallas kernels: 4.03 us -> 2.95 us  [attend(): pl.pallas_call(functools.partial(attend_kernel, distances, chips), out_sh...]
    pallas_call x5, Pallas kernels: 2.74 us -> 3.81 us  [the longest x1 1.75 us: pack_queries(): pl.pallas_call(pack_queries_kernel, out_shape=[like((rows, width), querie...]
  transfers between devices with their start and end apart: 15 -> 14, of which waited for: 6 -> 7; matrix products, arithmetic and copies ran while one was open for 2% -> 2% of each run, Pallas kernels for 17% -> 18%
where the time goes in v6:
time: 42.9 us; the launch traced here: 42.7 us
  starting transfers between devices  18.2 us (42%)
  waiting for transfers between devices  12.2 us (28%)
  Pallas kernels  9.7 us (23%)
  other arithmetic  1.74 us (4%)
  between operations  0.79 us (2%)
    ppermute x11, starting transfers between devices, swap(): return lax.ppermute(array, axis, [(i, i ^ distance) for i in range(count)])  14.4 us
    ppermute x11, waiting for transfers between devices, swap(): return lax.ppermute(array, axis, [(i, i ^ distance) for i in range(count)])  6.28 us
    ppermute x3, waiting for transfers between devices, by_core(): lax.ppermute(part, 'seq', [(i, i ^ 2 * distance(i % 2)) for i in range(se...  5.92 us
    ppermute x3, starting transfers between devices, by_core(): lax.ppermute(part, 'seq', [(i, i ^ 2 * distance(i % 2)) for i in range(se...  3.79 us
    pallas_call x2, Pallas kernels, attend(): pl.pallas_call(functools.partial(attend_kernel, distances, chips), out_sh...  2.95 us
    pallas_call x1, Pallas kernels, pack_queries(): pl.pallas_call(pack_queries_kernel, out_shape=[like((rows, width), querie...  1.75 us
    pallas_call x1, Pallas kernels, weigh(): pl.pallas_call(weigh_kernel, out_shape=jax.ShapeDtypeStruct(shape, jnp.bf...  1.43 us
    pallas_call x1, Pallas kernels, pack(): pl.pallas_call(pack_kernel, out_shape=[like((2, rows, width), queries)] *...  1.42 us
  transfers between devices with their start and end apart: 14, of which 7 were waited for; matrix products, arithmetic and copies ran while one was open for 2% of the time, Pallas kernels for 18%

profile of v6, /device:TPU:0, one launch (start us, length us, event | category | flops | bytes accessed | tf_op | source)
XLA Modules:
  0.0 42.7 jit_solution(17074947447180884729)
XLA Ops:
  0.6 1.4 %pack.1 = (bf16[2,128,512]{2,1,0:T(8,128)(2,1)S(1)}, bf16[2,128,512]{2,1,0:T(8,128)(2,1)S(1)}, bf16[2,128,512]{2,1,0:T(8,128)(2,1)S(1)}, bf16[2,128,512]{2,1,0:T(8,128)(2,1)S(1)}, bf16[128,512]{1,0:T(8,128)(2,1)S(1)}) custom-call(s32[1]{0:T(128)} %bitcast.me_ref, bf16[1,128,2048]{2,1,0:T(8,128)(2,1)} %keys.1, bf16[1,128,2048]{2,1,0:T(8,128)(2,1)} %values.1, ...), custom_call_target="tpu_custom_call" | custom-call | bytes 2097152 | tf_op jit(solution)/shard_map/pack/pallas_call | solution.py:82
  2.1 4.0 %collective-permute-start.2 = (bf16[2,128,512]{2,1,0:T(8,128)(2,1)S(1)}, bf16[2,128,512]{2,1,0:T(8,128)(2,1)S(1)}, u32[]{:S(2)}, u32[]{:S(2)}) collective-permute-start(bf16[2,128,512]{2,1,0:T(8,128)(2,1)S(1)} %get-tuple-element.38), channel_id=1, source_target_pairs={{0,24},{4,28},{8,16},{12,20},{16,8},{20,12},{24,0},{28,4},{1,25},{... | collective-permute-start | bytes 786440 | tf_op jit(solution)/shard_map/ppermute | solution.py:34
  6.0 0.5 %collective-permute-start = (bf16[2,128,512]{2,1,0:T(8,128)(2,1)S(1)}, bf16[2,128,512]{2,1,0:T(8,128)(2,1)S(1)}, u32[]{:S(2)}, u32[]{:S(2)}) collective-permute-start(bf16[2,128,512]{2,1,0:T(8,128)(2,1)S(1)} %get-tuple-element.36), channel_id=1, source_target_pairs={{0,8},{4,12},{8,0},{12,4},{16,24},{20,28},{24,16},{28,20},{1,9},{5... | collective-permute-start | bytes 786440 | tf_op jit(solution)/shard_map/ppermute | solution.py:34
  6.6 0.1 collective-permute-start.1
  6.7 1.4 %weigh.1.refs_4_ = bf16[64,1024]{1,0:T(8,128)(2,1)S(1)} custom-call(f32[64,1024]{1,0:T(8,128)} %refs_0_, f32[64,1024]{1,0:T(8,128)} %refs_1_, f32[64,1024]{1,0:T(8,128)} %refs_2_, f32[64,1024]{1,0:T(8,128)} %refs_3_), custom_call_target="tpu_custom_call" | custom-call | bytes 1179648 | tf_op jit(solution)/shard_map/weigh/pallas_call | solution.py:151
  8.1 2.0 %collective-permute-start.3 = (bf16[64,1024]{1,0:T(8,128)(2,1)S(1)}, bf16[64,1024]{1,0:T(8,128)(2,1)S(1)}, u32[]{:S(2)}, u32[]{:S(2)}) collective-permute-start(bf16[64,1024]{1,0:T(8,128)(2,1)S(1)} %weigh.1.refs_4_), channel_id=1, source_target_pairs={{0,1},{1,0},{2,3},{3,2},{4,5},{5,4},{6,7},{7,6},{8,9},{9,8},{10,11... | collective-permute-start | bytes 393224 | tf_op jit(solution)/shard_map/ppermute | solution.py:34
  10.1 2.6 %collective-permute-start.4 = (bf16[64,1024]{1,0:T(8,128)(2,1)S(1)}, bf16[64,1024]{1,0:T(8,128)(2,1)S(1)}, u32[]{:S(2)}, u32[]{:S(2)}) collective-permute-start(bf16[64,1024]{1,0:T(8,128)(2,1)S(1)} %weigh.1.refs_4_), channel_id=1, source_target_pairs={{0,2},{1,3},{2,0},{3,1},{4,6},{5,7},{6,4},{7,5},{8,10},{9,11},{10,... | collective-permute-start | bytes 393224 | tf_op jit(solution)/shard_map/ppermute | solution.py:34
  12.7 1.8 %pack_queries.1 = (bf16[128,512]{1,0:T(8,128)(2,1)}, bf16[128,512]{1,0:T(8,128)(2,1)}, bf16[128,512]{1,0:T(8,128)(2,1)S(1)}) custom-call(s32[1]{0:T(128)} %bitcast.me_ref, bf16[1,128,2048]{2,1,0:T(8,128)(2,1)} %queries.2), custom_call_target="tpu_custom_call" | custom-call | bytes 1048576 | tf_op jit(solution)/shard_map/pack_queries/pallas_call | solution.py:113
  14.5 0.0 collective-permute-done.2.refs_3_
  14.5 3.7 %collective-permute-done.refs_1_ = bf16[2,128,512]{2,1,0:T(8,128)(2,1)S(1)} collective-permute-done((bf16[2,128,512]{2,1,0:T(8,128)(2,1)S(1)}, bf16[2,128,512]{2,1,0:T(8,128)(2,1)S(1)}, u32[]{:S(2)}, u32[]{:S(2)}) %collective-permute-start) | collective-permute-done | bytes 262176 | tf_op jit(solution)/shard_map/ppermute | solution.py:34
  18.2 0.0 collective-permute-done.1.refs_2_
  18.2 0.0 collective-permute-done.3.refs_5_
  18.2 0.0 collective-permute-done.4.refs_6_
  18.2 0.1 stack.1.refs_1_.refs_3_.own
  18.4 0.1 collective-permute-start.8
  18.4 2.4 %collective-permute-start.7 = (bf16[128,512]{1,0:T(8,128)(2,1)S(1)}, bf16[128,512]{1,0:T(8,128)(2,1)S(1)}, u32[]{:S(2)}, u32[]{:S(2)}) collective-permute-start(bf16[128,512]{1,0:T(8,128)(2,1)S(1)} %get-tuple-element.56), channel_id=1, source_target_pairs={{0,24},{4,28},{8,16},{12,20},{16,8},{20,12},{24,0},{28,4},{1,25},{... | collective-permute-start | bytes 393224 | tf_op jit(solution)/shard_map/ppermute | solution.py:34
  20.8 1.6 %collective-permute-start.9 = (bf16[64,1024]{1,0:T(8,128)(2,1)S(1)}, bf16[64,1024]{1,0:T(8,128)(2,1)}, u32[]{:S(2)}, u32[]{:S(2)}) collective-permute-start(bf16[64,1024]{1,0:T(8,128)(2,1)S(1)} %collective-permute-done.4.refs_6_), channel_id=1, source_target_pairs={{0,1},{1,0},{2,3},{3,2},{4,5},{5,4},{6,7},{7,6},{8,9},{9,8},{10,11... | collective-permute-start | bytes 393224 | tf_op jit(solution)/shard_map/ppermute | solution.py:34
  22.4 0.5 %collective-permute-start.5 = (bf16[128,512]{1,0:T(8,128)(2,1)}, bf16[128,512]{1,0:T(8,128)(2,1)S(1)}, u32[]{:S(2)}, u32[]{:S(2)}) collective-permute-start(bf16[128,512]{1,0:T(8,128)(2,1)} %get-tuple-element.54), channel_id=1, source_target_pairs={{0,8},{4,12},{8,0},{12,4},{16,24},{20,28},{24,16},{28,20},{1,9},{5... | collective-permute-start | bytes 393224 | tf_op jit(solution)/shard_map/ppermute | solution.py:34
  22.9 0.6 %collective-permute-start.6 = (bf16[128,512]{1,0:T(8,128)(2,1)}, bf16[128,512]{1,0:T(8,128)(2,1)S(1)}, u32[]{:S(2)}, u32[]{:S(2)}) collective-permute-start(bf16[128,512]{1,0:T(8,128)(2,1)} %get-tuple-element.55), channel_id=1, source_target_pairs={{0,16},{4,20},{8,24},{12,28},{16,0},{20,4},{24,8},{28,12},{1,17},{... | collective-permute-start | bytes 393224 | tf_op jit(solution)/shard_map/ppermute | solution.py:34
  23.6 1.7 %collective-permute-done.7.refs_0_ = bf16[128,512]{1,0:T(8,128)(2,1)S(1)} collective-permute-done((bf16[128,512]{1,0:T(8,128)(2,1)S(1)}, bf16[128,512]{1,0:T(8,128)(2,1)S(1)}, u32[]{:S(2)}, u32[]{:S(2)}) %collective-permute-start.7) | collective-permute-done | bytes 131104 | tf_op jit(solution)/shard_map/ppermute | solution.py:34
  25.3 0.0 collective-permute-done.8.refs_2_.refs_4_.other
  25.3 1.1 %attend.2.attended = bf16[2,128,256]{2,1,0:T(8,128)(2,1)S(1)} custom-call(s32[1]{0:T(128)} %bitcast.me_ref, bf16[128,512]{1,0:T(8,128)(2,1)S(1)} %collective-permute-done.7.refs_0_, bf16[1408,512]{1,0:T(8,128)(2,1)S(1)} %stack.1.refs_1_.refs_3_.own, bf16[1408,512]{1,0:T(8,128)(2,1)S(1)} %collective-permute-done.8.refs_2_.refs_4_.other), custom_call_target="tpu_custom_call" | custom-call | flops 268435456 | bytes 2359296 | tf_op jit(solution)/shard_map/attend/pallas_call | solution.py:322
  26.4 0.2 collective-permute-done.9.last
  26.5 0.0 collective-permute-start.10
  26.5 1.0 %collect.1.weights = bf16[2,256,1024]{2,1,0:T(8,128)(2,1)S(1)} custom-call(s32[1]{0:T(128)} %bitcast.1.index_ref, bf16[1408,512]{1,0:T(8,128)(2,1)S(1)} %stack.1.refs_1_.refs_3_.own, bf16[64,1024]{1,0:T(8,128)(2,1)} %collective-permute-done.9.last, bf16[1408,512]{1,0:T(8,128)(2,1)S(1)} %collective-permute-done.8.refs_2_.refs_4_.other), custom_call_target="tpu_custom_call" | custom-call | bytes 2097152 | tf_op jit(solution)/shard_map/collect/pallas_call | solution.py:235
  27.5 0.5 %collective-permute-done.5.refs_1_ = bf16[128,512]{1,0:T(8,128)(2,1)S(1)} collective-permute-done((bf16[128,512]{1,0:T(8,128)(2,1)}, bf16[128,512]{1,0:T(8,128)(2,1)S(1)}, u32[]{:S(2)}, u32[]{:S(2)}) %collective-permute-start.5) | collective-permute-done | bytes 131104 | tf_op jit(solution)/shard_map/ppermute | solution.py:34
  28.0 0.2 collective-permute-done.6.refs_2_
  28.2 0.0 collective-permute-done.10.last
  28.2 0.4 project.3
  28.5 1.7 %collective-permute-start.12 = (bf16[128,1024]{1,0:T(8,128)(2,1)S(1)}, bf16[128,1024]{1,0:T(8,128)(2,1)S(1)}, u32[]{:S(2)}, u32[]{:S(2)}) collective-permute-start(bf16[128,1024]{1,0:T(8,128)(2,1)S(1)} %project.3), channel_id=1, source_target_pairs={{0,8},{4,20},{8,0},{12,28},{16,24},{20,4},{24,16},{28,12},{1,9},{5... | collective-permute-start | bytes 786440 | tf_op jit(solution)/shard_map/ppermute | solution.py:419
  30.3 1.9 %attend.3.attended = bf16[2,384,256]{2,1,0:T(8,128)(2,1)S(1)} custom-call(s32[1]{0:T(128)} %bitcast.me_ref, bf16[128,512]{1,0:T(8,128)(2,1)S(1)} %get-tuple-element.58.refs_0_, bf16[128,512]{1,0:T(8,128)(2,1)S(1)} %collective-permute-done.5.refs_1_, bf16[128,512]{1,0:T(8,128)(2,1)S(1)} %collective-permute-done.6.refs_2_, ...), custom_call_target="tpu_custom_call" | custom-call | flops 805306368 | bytes 2883584 | tf_op jit(solution)/shard_map/attend/pallas_call | solution.py:322
  32.1 0.0 copy-start
  32.1 0.0 copy-start.1
  32.2 0.0 copy-start.2
  32.2 0.0 copy-start.3
  32.2 0.7 %project.2 = (bf16[128,1024]{1,0:T(8,128)(2,1)S(1)}, f32[128,1024]{1,0:T(8,128)S(1)}, f32[128,1024]{1,0:T(8,128)S(1)}) custom-call(s32[1]{0:T(128)} %bitcast.me_ref, s32[1]{0:T(128)} %bitcast.1.index_ref, bf16[2,384,256]{2,1,0:T(8,128)(2,1)S(1)} %attend.3.attended, bf16[2,256,1024]{2,1,0:T(8,128)(2,1)S(1)} %collect.1.weights, ...), custom_call_target="tpu_custom_call" | custom-call | flops 402653184 | bytes 3538944 | tf_op jit(solution)/shard_map/project/pallas_call | solution.py:383
  32.9 0.7 %collective-permute-start.11 = (bf16[128,1024]{1,0:T(8,128)(2,1)S(1)}, bf16[128,1024]{1,0:T(8,128)(2,1)S(1)}, u32[]{:S(2)}, u32[]{:S(2)}) collective-permute-start(bf16[128,1024]{1,0:T(8,128)(2,1)S(1)} %get-tuple-element.63), channel_id=1, source_target_pairs={{0,8},{4,20},{8,0},{12,28},{16,24},{20,4},{24,16},{28,12},{1,9},{5... | collective-permute-start | bytes 786440 | tf_op jit(solution)/shard_map/ppermute | solution.py:419
  33.6 1.4 %collective-permute-done.12.passed = bf16[128,1024]{1,0:T(8,128)(2,1)S(1)} collective-permute-done((bf16[128,1024]{1,0:T(8,128)(2,1)S(1)}, bf16[128,1024]{1,0:T(8,128)(2,1)S(1)}, u32[]{:S(2)}, u32[]{:S(2)}) %collective-permute-start.12) | collective-permute-done | bytes 262176 | tf_op jit(solution)/shard_map/ppermute | solution.py:419
  35.0 1.4 %collective-permute-start.13 = (bf16[128,1024]{1,0:T(8,128)(2,1)S(1)}, bf16[128,1024]{1,0:T(8,128)(2,1)S(1)}, u32[]{:S(2)}, u32[]{:S(2)}) collective-permute-start(bf16[128,1024]{1,0:T(8,128)(2,1)S(1)} %add.64), channel_id=1, source_target_pairs={{0,16},{4,12},{8,24},{12,4},{16,0},{20,28},{24,8},{28,20},{1,17},{... | collective-permute-start | bytes 786440 | tf_op jit(solution)/shard_map/ppermute | solution.py:419
  36.4 0.0 copy-done
  36.4 0.0 copy-done.1
  36.4 0.0 copy-done.2
  36.4 0.0 copy-done.3
  36.4 0.9 %multiply_subtract_fusion = f32[64,1024]{1,0:T(8,128)} fusion(f32[64,1024]{1,0:T(8,128)S(1)} %copy-done, f32[64,1024]{1,0:T(8,128)S(1)} %copy-done.3, f32[64,1024]{1,0:T(8,128)S(1)} %copy-done.2, f32[64,1024]{1,0:T(8,128)S(1)} %copy-done.1), kind=kLoop, calls=%fused_computation.10 | loop fusion | flops 983040 | bytes 1310720 | tf_op jit(solution)/shard_map/sub | solution.py:28
  37.3 4.5 %collective-permute-done.11 = bf16[128,1024]{1,0:T(8,128)(2,1)S(1)} collective-permute-done((bf16[128,1024]{1,0:T(8,128)(2,1)S(1)}, bf16[128,1024]{1,0:T(8,128)(2,1)S(1)}, u32[]{:S(2)}, u32[]{:S(2)}) %collective-permute-start.11) | collective-permute-done | bytes 262176 | tf_op jit(solution)/shard_map/ppermute | solution.py:419
  41.8 0.1 convert_add_fusion
  41.9 0.0 collective-permute-done.13
  41.9 0.8 %fusion.6 = bf16[1,128,1024]{2,1,0:T(8,128)(2,1)} fusion(f32[128,1024]{1,0:T(8,128)S(1)} %convert_add_fusion, bf16[128,1024]{1,0:T(8,128)(2,1)S(1)} %collective-permute-done.13), kind=kLoop, calls=%fused_computation.9 | loop fusion | flops 393216 | bytes 1048576 | tf_op jit(solution)/shard_map/broadcast_in_dim | solution.py:481
  (1 shorter events, 0.0 us)
Async XLA Ops:
  2.1 12.4 %collective-permute-start.2 = (bf16[2,128,512]{2,1,0:T(8,128)(2,1)S(1)}, bf16[2,128,512]{2,1,0:T(8,128)(2,1)S(1)}, u32[]{:S(2)}, u32[]{:S(2)}) collective-permute-start(bf16[2,128,512]{2,1,0:T(8,128)(2,1)S(1)} %get-tuple-element.38), channel_id=1, source_target_pairs={{0,24},{4,28},{8,16},{12,20},{16,8},{20,12},{24,0},{28,4},{1,25},{... | collective-permute-start | bytes 786440 | tf_op jit(solution)/shard_map/ppermute | solution.py:34
  6.0 12.2 %collective-permute-start = (bf16[2,128,512]{2,1,0:T(8,128)(2,1)S(1)}, bf16[2,128,512]{2,1,0:T(8,128)(2,1)S(1)}, u32[]{:S(2)}, u32[]{:S(2)}) collective-permute-start(bf16[2,128,512]{2,1,0:T(8,128)(2,1)S(1)} %get-tuple-element.36), channel_id=1, source_target_pairs={{0,8},{4,12},{8,0},{12,4},{16,24},{20,28},{24,16},{28,20},{1,9},{5... | collective-permute-start | bytes 786440 | tf_op jit(solution)/shard_map/ppermute | solution.py:34
  6.6 11.7 %collective-permute-start.1 = (bf16[2,128,512]{2,1,0:T(8,128)(2,1)S(1)}, bf16[2,128,512]{2,1,0:T(8,128)(2,1)S(1)}, u32[]{:S(2)}, u32[]{:S(2)}) collective-permute-start(bf16[2,128,512]{2,1,0:T(8,128)(2,1)S(1)} %get-tuple-element.37), channel_id=1, source_target_pairs={{0,16},{4,20},{8,24},{12,28},{16,0},{20,4},{24,8},{28,12},{1,17},{... | collective-permute-start | bytes 786440 | tf_op jit(solution)/shard_map/ppermute | solution.py:34
  8.1 10.1 %collective-permute-start.3 = (bf16[64,1024]{1,0:T(8,128)(2,1)S(1)}, bf16[64,1024]{1,0:T(8,128)(2,1)S(1)}, u32[]{:S(2)}, u32[]{:S(2)}) collective-permute-start(bf16[64,1024]{1,0:T(8,128)(2,1)S(1)} %weigh.1.refs_4_), channel_id=1, source_target_pairs={{0,1},{1,0},{2,3},{3,2},{4,5},{5,4},{6,7},{7,6},{8,9},{9,8},{10,11... | collective-permute-start | bytes 393224 | tf_op jit(solution)/shard_map/ppermute | solution.py:34
  10.1 8.1 %collective-permute-start.4 = (bf16[64,1024]{1,0:T(8,128)(2,1)S(1)}, bf16[64,1024]{1,0:T(8,128)(2,1)S(1)}, u32[]{:S(2)}, u32[]{:S(2)}) collective-permute-start(bf16[64,1024]{1,0:T(8,128)(2,1)S(1)} %weigh.1.refs_4_), channel_id=1, source_target_pairs={{0,2},{1,3},{2,0},{3,1},{4,6},{5,7},{6,4},{7,5},{8,10},{9,11},{10,... | collective-permute-start | bytes 393224 | tf_op jit(solution)/shard_map/ppermute | solution.py:34
  18.4 6.9 %collective-permute-start.8 = (bf16[1408,512]{1,0:T(8,128)(2,1)S(1)}, bf16[1408,512]{1,0:T(8,128)(2,1)S(1)}, u32[]{:S(2)}, u32[]{:S(2)}) collective-permute-start(bf16[1408,512]{1,0:T(8,128)(2,1)S(1)} %stack.1.refs_1_.refs_3_.own), channel_id=1, source_target_pairs={{0,4},{4,0},{8,12},{12,8},{16,20},{20,16},{24,28},{28,24},{1,5},{5... | collective-permute-start | bytes 4325384 | tf_op jit(solution)/shard_map/ppermute | solution.py:34
  18.4 6.8 %collective-permute-start.7 = (bf16[128,512]{1,0:T(8,128)(2,1)S(1)}, bf16[128,512]{1,0:T(8,128)(2,1)S(1)}, u32[]{:S(2)}, u32[]{:S(2)}) collective-permute-start(bf16[128,512]{1,0:T(8,128)(2,1)S(1)} %get-tuple-element.56), channel_id=1, source_target_pairs={{0,24},{4,28},{8,16},{12,20},{16,8},{20,12},{24,0},{28,4},{1,25},{... | collective-permute-start | bytes 393224 | tf_op jit(solution)/shard_map/ppermute | solution.py:34
  20.8 5.7 %collective-permute-start.9 = (bf16[64,1024]{1,0:T(8,128)(2,1)S(1)}, bf16[64,1024]{1,0:T(8,128)(2,1)}, u32[]{:S(2)}, u32[]{:S(2)}) collective-permute-start(bf16[64,1024]{1,0:T(8,128)(2,1)S(1)} %collective-permute-done.4.refs_6_), channel_id=1, source_target_pairs={{0,1},{1,0},{2,3},{3,2},{4,5},{5,4},{6,7},{7,6},{8,9},{9,8},{10,11... | collective-permute-start | bytes 393224 | tf_op jit(solution)/shard_map/ppermute | solution.py:34
  22.4 5.6 %collective-permute-start.5 = (bf16[128,512]{1,0:T(8,128)(2,1)}, bf16[128,512]{1,0:T(8,128)(2,1)S(1)}, u32[]{:S(2)}, u32[]{:S(2)}) collective-permute-start(bf16[128,512]{1,0:T(8,128)(2,1)} %get-tuple-element.54), channel_id=1, source_target_pairs={{0,8},{4,12},{8,0},{12,4},{16,24},{20,28},{24,16},{28,20},{1,9},{5... | collective-permute-start | bytes 393224 | tf_op jit(solution)/shard_map/ppermute | solution.py:34
  22.9 5.2 %collective-permute-start.6 = (bf16[128,512]{1,0:T(8,128)(2,1)}, bf16[128,512]{1,0:T(8,128)(2,1)S(1)}, u32[]{:S(2)}, u32[]{:S(2)}) collective-permute-start(bf16[128,512]{1,0:T(8,128)(2,1)} %get-tuple-element.55), channel_id=1, source_target_pairs={{0,16},{4,20},{8,24},{12,28},{16,0},{20,4},{24,8},{28,12},{1,17},{... | collective-permute-start | bytes 393224 | tf_op jit(solution)/shard_map/ppermute | solution.py:34
  26.5 1.7 %collective-permute-start.10 = (bf16[64,1024]{1,0:T(8,128)(2,1)}, bf16[64,1024]{1,0:T(8,128)(2,1)S(1)}, u32[]{:S(2)}, u32[]{:S(2)}) collective-permute-start(bf16[64,1024]{1,0:T(8,128)(2,1)} %collective-permute-done.9.last), channel_id=1, source_target_pairs={{0,4},{4,0},{8,12},{12,8},{16,20},{20,16},{24,28},{28,24},{1,5},{5... | collective-permute-start | bytes 393224 | tf_op jit(solution)/shard_map/ppermute | solution.py:34
  28.5 6.4 %collective-permute-start.12 = (bf16[128,1024]{1,0:T(8,128)(2,1)S(1)}, bf16[128,1024]{1,0:T(8,128)(2,1)S(1)}, u32[]{:S(2)}, u32[]{:S(2)}) collective-permute-start(bf16[128,1024]{1,0:T(8,128)(2,1)S(1)} %project.3), channel_id=1, source_target_pairs={{0,8},{4,20},{8,0},{12,28},{16,24},{20,4},{24,16},{28,12},{1,9},{5... | collective-permute-start | bytes 786440 | tf_op jit(solution)/shard_map/ppermute | solution.py:419
  32.1 4.3 %copy-start = (f32[64,1024]{1,0:T(8,128)S(1)}, f32[64,1024]{1,0:T(8,128)}, u32[]{:S(2)}) copy-start(f32[64,1024]{1,0:T(8,128)} %refs_0_) | copy-start | bytes 786436
  32.1 4.2 %copy-start.1 = (f32[64,1024]{1,0:T(8,128)S(1)}, f32[64,1024]{1,0:T(8,128)}, u32[]{:S(2)}) copy-start(f32[64,1024]{1,0:T(8,128)} %refs_1_) | copy-start | bytes 786436
  32.2 4.2 %copy-start.2 = (f32[64,1024]{1,0:T(8,128)S(1)}, f32[64,1024]{1,0:T(8,128)}, u32[]{:S(2)}) copy-start(f32[64,1024]{1,0:T(8,128)} %refs_2_) | copy-start | bytes 786436
  32.2 4.2 %copy-start.3 = (f32[64,1024]{1,0:T(8,128)S(1)}, f32[64,1024]{1,0:T(8,128)}, u32[]{:S(2)}) copy-start(f32[64,1024]{1,0:T(8,128)} %refs_3_) | copy-start | bytes 786436
  32.9 9.0 %collective-permute-start.11 = (bf16[128,1024]{1,0:T(8,128)(2,1)S(1)}, bf16[128,1024]{1,0:T(8,128)(2,1)S(1)}, u32[]{:S(2)}, u32[]{:S(2)}) collective-permute-start(bf16[128,1024]{1,0:T(8,128)(2,1)S(1)} %get-tuple-element.63), channel_id=1, source_target_pairs={{0,8},{4,20},{8,0},{12,28},{16,24},{20,4},{24,16},{28,12},{1,9},{5... | collective-permute-start | bytes 786440 | tf_op jit(solution)/shard_map/ppermute | solution.py:419
  35.0 6.9 %collective-permute-start.13 = (bf16[128,1024]{1,0:T(8,128)(2,1)S(1)}, bf16[128,1024]{1,0:T(8,128)(2,1)S(1)}, u32[]{:S(2)}, u32[]{:S(2)}) collective-permute-start(bf16[128,1024]{1,0:T(8,128)(2,1)S(1)} %add.64), channel_id=1, source_target_pairs={{0,16},{4,12},{8,24},{12,4},{16,0},{20,28},{24,8},{28,20},{1,17},{... | collective-permute-start | bytes 786440 | tf_op jit(solution)/shard_map/ppermute | solution.py:419

commit v7 on v6

--- a/solution.py
+++ b/solution.py
@@ -58,38 +58,100 @@
     return pl.ds(pl.multiple_of(((me_ref[0] // 2) ^ distance) * width, width), width)
 
 
-def pack_kernel(me_ref, keys, values, queries, *refs):
-    pairs, (here, sems) = refs[:-2], refs[-2:]
-    width = here.shape[1]
-    copies = []
-
-    def copy(array, distance, part):
-        at = chip_columns(me_ref, distance, width)
-        copies.append(pltpu.make_async_copy(array.at[0, :, at], part, sems.at[len(copies)]))
-        copies[-1].start()
-
-    for distance, pair in enumerate(pairs):
-        copy(keys, distance, pair.at[0])
-        copy(values, distance, pair.at[1])
-    copy(queries, 0, here)
-    for each in copies:
-        each.wait()
-
-
-def pack(me, keys, values, queries, chips):
+def start_copies(copies):
+    for copy in copies:
+        copy.start()
+    return copies
+
+
+def pair_copies(me_ref, distances, keys, values, pairs, sems):
+    width = pairs[0].shape[2]
+    return [
+        pltpu.make_async_copy(
+            array.at[0, :, chip_columns(me_ref, distance, width)],
+            pair.at[which],
+            sems.at[2 * index + which],
+        )
+        for index, (distance, pair) in enumerate(zip(distances, pairs))
+        for which, array in enumerate((keys, values))
+    ]
+
+
+def pack_far_kernel(far, me_ref, keys, values, pair, sems):
+    for copy in start_copies(pair_copies(me_ref, (far,), keys, values, (pair,), sems)):
+        copy.wait()
+
+
+def pack_far(me, keys, values, chips):
+    _, rows, features = keys.shape
+    width = features // chips
+    return pl.pallas_call(
+        functools.partial(pack_far_kernel, chips - 1),
+        out_shape=like((2, rows, width), keys),
+        in_specs=[SMEM] + [HBM] * 2,
+        out_specs=VMEM,
+        scratch_shapes=[pltpu.SemaphoreType.DMA((2,))],
+        compiler_params=PARAMS,
+        cost_estimate=cost(8 * rows * width),
+        name="pack_far",
+    )(me, in_hbm(keys), in_hbm(values))
+
+
+def pack_kernel(far, me_ref, keys, values, queries, *refs):
+    state, refs = refs[:4], refs[4:]
+    pairs, (here, weight, held, sems, state_sems) = refs[:far], refs[far:]
+    copies = start_copies(
+        pair_copies(me_ref, range(far), keys, values, pairs, sems)
+        + [
+            pltpu.make_async_copy(
+                queries.at[0, :, chip_columns(me_ref, 0, here.shape[1])], here, sems.at[2 * far]
+            )
+        ]
+    )
+    pieces = state_sems.shape[1]
+    rows = weight.shape[0] // pieces
+    places = [pl.ds(piece * rows, rows) for piece in range(pieces)]
+    arriving = [
+        start_copies(
+            [
+                pltpu.make_async_copy(
+                    array.at[at], held.at[index, at], state_sems.at[index, piece]
+                )
+                for index, array in enumerate(state)
+            ]
+        )
+        for piece, at in enumerate(places)
+    ]
+    for at, piece in zip(places, arriving):
+        for copy in piece:
+            copy.wait()
+        result = adamw(held[0, at], held[1, at], held[2, at], held[3, at])
+        weight[at, :] = result.astype(weight.dtype)
+    for copy in copies:
+        copy.wait()
+
+
+def pack(me, keys, values, queries, state, chips):
     _, rows, features = queries.shape
-    width = features // chips
-    *pairs, here = pl.pallas_call(
-        pack_kernel,
-        out_shape=[like((2, rows, width), queries)] * chips + [like((rows, width), queries)],
-        in_specs=[SMEM] + [HBM] * 3,
-        out_specs=[VMEM] * (chips + 1),
-        scratch_shapes=[pltpu.SemaphoreType.DMA((2 * chips + 1,))],
-        compiler_params=PARAMS,
-        cost_estimate=cost(8 * rows * features),
+    width, far = features // chips, chips - 1
+    shape = state[0].shape
+    pieces = math.gcd(shape[0] // 16, 4) if shape[0] % 16 == 0 else 1
+    *pairs, here, weight = pl.pallas_call(
+        functools.partial(pack_kernel, far),
+        out_shape=[like((2, rows, width), queries)] * far
+        + [like((rows, width), queries), jax.ShapeDtypeStruct(shape, jnp.bfloat16)],
+        in_specs=[SMEM] + [HBM] * 7,
+        out_specs=[VMEM] * (far + 2),
+        scratch_shapes=[
+            pltpu.VMEM((4, *shape), state[0].dtype),
+            pltpu.SemaphoreType.DMA((2 * far + 1,)),
+            pltpu.SemaphoreType.DMA((4, pieces)),
+        ],
+        compiler_params=PARAMS,
+        cost_estimate=cost(8 * rows * features + 18 * state[0].size),
         name="pack",
-    )(me, *map(in_hbm, (keys, values, queries)))
-    return pairs, here
+    )(me, *map(in_hbm, (keys, values, queries, *state)))
+    return pairs, here, weight
 
 
 def pack_queries_kernel(me_ref, queries, *refs):
@@ -120,44 +182,6 @@
         cost_estimate=cost(4 * rows * features),
         name="pack_queries",
     )(me, in_hbm(queries))
-
-
-def weigh_kernel(*refs):
-    arrays, weight, held, sems = refs[:4], refs[4], refs[5], refs[6]
-    pieces = sems.shape[1]
-    rows = weight.shape[0] // pieces
-    copies = []
-    for piece in range(pieces):
-        at = pl.ds(piece * rows, rows)
-        copies.append(
-            [
-                pltpu.make_async_copy(array.at[at], held.at[index, at], sems.at[index, piece])
-                for index, array in enumerate(arrays)
-            ]
-        )
-        for copy in copies[-1]:
-            copy.start()
-    for piece in range(pieces):
-        for copy in copies[piece]:
-            copy.wait()
-        at = pl.ds(piece * rows, rows)
-        result = adamw(held[0, at], held[1, at], held[2, at], held[3, at])
-        weight[at, :] = result.astype(weight.dtype)
-
-
-def weigh(*arrays):
-    shape, kind = arrays[0].shape, arrays[0].dtype
-    pieces = math.gcd(shape[0] // 16, 4) if shape[0] % 16 == 0 else 1
-    return pl.pallas_call(
-        weigh_kernel,
-        out_shape=jax.ShapeDtypeStruct(shape, jnp.bfloat16),
-        in_specs=[HBM] * 4,
-        out_specs=VMEM,
-        scratch_shapes=[pltpu.VMEM((4, *shape), kind), pltpu.SemaphoreType.DMA((4, pieces))],
-        compiler_params=PARAMS,
-        cost_estimate=cost(18 * arrays[0].size),
-        name="weigh",
-    )(*map(in_hbm, arrays))
 
 
 def merge_kernel(index_ref, *refs):
@@ -433,11 +457,14 @@
         me = lax.axis_index("seq").astype(jnp.int32).reshape(1)
         place = lax.axis_index("dp").astype(jnp.int32)
 
-        sent_pairs, own_queries = pack(me, keys, values, queries, chips)
+        farthest = pack_far(me, keys, values, chips)
+        near_keys, farthest = lax.optimization_barrier((keys, farthest))
+        state = (master, moment, second, gradient)
+        sent_pairs, own_queries, weight = pack(me, near_keys, values, queries, state, chips)
+        sent_pairs.append(farthest)
         pairs = exchange(sent_pairs)
 
-        state, _ = lax.optimization_barrier(((master, moment, second, gradient), sent_pairs))
-        weight = weigh(*state)[None]
+        weight = weight[None]
         span = 1
         while 4 * span < dp_count:
             many = 4 if dp_count // span % 16 == 0 else 2

time: 42.9 us -> 42.4 us (0.988)
  transfers between devices with their start and end apart: 14 -> 14, of which waited for: 7 -> 8; matrix products, arithmetic and copies ran while one was open for 2% -> 2% of each run, Pallas kernels for 18% -> 19%
where the time goes in v7:
time: 42.4 us; the launch traced here: 42.2 us
  starting transfers between devices  18.2 us (43%)
  waiting for transfers between devices  11.8 us (28%)
  Pallas kernels  9.65 us (23%)
  other arithmetic  1.74 us (4%)
  between operations  0.78 us (2%)
    ppermute x11, starting transfers between devices, swap(): return lax.ppermute(array, axis, [(i, i ^ distance) for i in range(count)])  14.3 us
    ppermute x11, waiting for transfers between devices, swap(): return lax.ppermute(array, axis, [(i, i ^ distance) for i in range(count)])  6.18 us
    ppermute x3, waiting for transfers between devices, by_core(): lax.ppermute(part, 'seq', [(i, i ^ 2 * distance(i % 2)) for i in range(se...  5.62 us
    ppermute x3, starting transfers between devices, by_core(): lax.ppermute(part, 'seq', [(i, i ^ 2 * distance(i % 2)) for i in range(se...  3.87 us
    pallas_call x2, Pallas kernels, attend(): pl.pallas_call(functools.partial(attend_kernel, distances, chips), out_sh...  2.95 us
    pallas_call x1, Pallas kernels, pack(): pl.pallas_call(functools.partial(pack_kernel, far), out_shape=[like((2, r...  1.79 us
    pallas_call x1, Pallas kernels, pack_queries(): pl.pallas_call(pack_queries_kernel, out_shape=[like((rows, width), querie...  1.75 us
    pallas_call x2, Pallas kernels, project(): pl.pallas_call(functools.partial(project_kernel, chips), out_shape=[jax.S...  1.05 us
  transfers between devices with their start and end apart: 14, of which 8 were waited for; matrix products, arithmetic and copies ran while one was open for 2% of the time, Pallas kernels for 19%

profile of v7, /device:TPU:0, one launch (start us, length us, event | category | flops | bytes accessed | tf_op | source)
XLA Modules:
  0.0 42.2 jit_solution(7728022718310444553)
XLA Ops:
  0.6 1.0 %pack_far.1 = bf16[2,128,512]{2,1,0:T(8,128)(2,1)S(1)} custom-call(s32[1]{0:T(128)} %bitcast.me_ref, bf16[1,128,2048]{2,1,0:T(8,128)(2,1)} %keys.2, bf16[1,128,2048]{2,1,0:T(8,128)(2,1)} %values.3), custom_call_target="tpu_custom_call" | custom-call | bytes 524288 | tf_op jit(solution)/shard_map/pack_far/pallas_call | solution.py:88
  1.6 4.0 %collective-permute-start.2 = (bf16[2,128,512]{2,1,0:T(8,128)(2,1)S(1)}, bf16[2,128,512]{2,1,0:T(8,128)(2,1)S(1)}, u32[]{:S(2)}, u32[]{:S(2)}) collective-permute-start(bf16[2,128,512]{2,1,0:T(8,128)(2,1)S(1)} %pack_far.1), channel_id=1, source_target_pairs={{0,24},{4,28},{8,16},{12,20},{16,8},{20,12},{24,0},{28,4},{1,25},{... | collective-permute-start | bytes 786440 | tf_op jit(solution)/shard_map/ppermute | solution.py:34
  5.6 1.8 %pack.1 = (bf16[2,128,512]{2,1,0:T(8,128)(2,1)S(1)}, bf16[2,128,512]{2,1,0:T(8,128)(2,1)S(1)}, bf16[2,128,512]{2,1,0:T(8,128)(2,1)S(1)}, bf16[128,512]{1,0:T(8,128)(2,1)S(1)}, bf16[64,1024]{1,0:T(8,128)(2,1)S(1)}) custom-call(s32[1]{0:T(128)} %bitcast.me_ref, bf16[1,128,2048]{2,1,0:T(8,128)(2,1)} %keys.2, bf16[1,128,2048]{2,1,0:T(8,128)(2,1)} %values.3, ...), custom_call_target="tpu_custom_call" | custom-call | bytes 3276800 | tf_op jit(solution)/shard_map/pack/pallas_call | solution.py:139
  7.4 0.6 %collective-permute-start = (bf16[2,128,512]{2,1,0:T(8,128)(2,1)S(1)}, bf16[2,128,512]{2,1,0:T(8,128)(2,1)S(1)}, u32[]{:S(2)}, u32[]{:S(2)}) collective-permute-start(bf16[2,128,512]{2,1,0:T(8,128)(2,1)S(1)} %get-tuple-element.35), channel_id=1, source_target_pairs={{0,8},{4,12},{8,0},{12,4},{16,24},{20,28},{24,16},{28,20},{1,9},{5... | collective-permute-start | bytes 786440 | tf_op jit(solution)/shard_map/ppermute | solution.py:34
  8.0 0.1 collective-permute-start.1
  8.0 2.0 %collective-permute-start.3 = (bf16[64,1024]{1,0:T(8,128)(2,1)S(1)}, bf16[64,1024]{1,0:T(8,128)(2,1)S(1)}, u32[]{:S(2)}, u32[]{:S(2)}) collective-permute-start(bf16[64,1024]{1,0:T(8,128)(2,1)S(1)} %get-tuple-element.38.refs_4_), channel_id=1, source_target_pairs={{0,1},{1,0},{2,3},{3,2},{4,5},{5,4},{6,7},{7,6},{8,9},{9,8},{10,11... | collective-permute-start | bytes 393224 | tf_op jit(solution)/shard_map/ppermute | solution.py:34
  10.1 2.6 %collective-permute-start.4 = (bf16[64,1024]{1,0:T(8,128)(2,1)S(1)}, bf16[64,1024]{1,0:T(8,128)(2,1)S(1)}, u32[]{:S(2)}, u32[]{:S(2)}) collective-permute-start(bf16[64,1024]{1,0:T(8,128)(2,1)S(1)} %get-tuple-element.38.refs_4_), channel_id=1, source_target_pairs={{0,2},{1,3},{2,0},{3,1},{4,6},{5,7},{6,4},{7,5},{8,10},{9,11},{10,... | collective-permute-start | bytes 393224 | tf_op jit(solution)/shard_map/ppermute | solution.py:34
  12.7 1.8 %pack_queries.1 = (bf16[128,512]{1,0:T(8,128)(2,1)}, bf16[128,512]{1,0:T(8,128)(2,1)}, bf16[128,512]{1,0:T(8,128)(2,1)S(1)}) custom-call(s32[1]{0:T(128)} %bitcast.me_ref, bf16[1,128,2048]{2,1,0:T(8,128)(2,1)} %queries.2), custom_call_target="tpu_custom_call" | custom-call | bytes 1048576 | tf_op jit(solution)/shard_map/pack_queries/pallas_call | solution.py:175
  14.4 0.0 collective-permute-done.2.refs_3_
  14.4 3.4 %collective-permute-done.refs_1_ = bf16[2,128,512]{2,1,0:T(8,128)(2,1)S(1)} collective-permute-done((bf16[2,128,512]{2,1,0:T(8,128)(2,1)S(1)}, bf16[2,128,512]{2,1,0:T(8,128)(2,1)S(1)}, u32[]{:S(2)}, u32[]{:S(2)}) %collective-permute-start) | collective-permute-done | bytes 262176 | tf_op jit(solution)/shard_map/ppermute | solution.py:34
  17.8 0.0 collective-permute-done.1.refs_2_
  17.8 0.0 collective-permute-done.3.refs_5_
  17.8 0.1 collective-permute-done.4.refs_6_
  17.9 0.1 stack.1.refs_1_.refs_3_.own
  18.0 0.1 collective-permute-start.8
  18.1 2.5 %collective-permute-start.7 = (bf16[128,512]{1,0:T(8,128)(2,1)S(1)}, bf16[128,512]{1,0:T(8,128)(2,1)S(1)}, u32[]{:S(2)}, u32[]{:S(2)}) collective-permute-start(bf16[128,512]{1,0:T(8,128)(2,1)S(1)} %get-tuple-element.52), channel_id=1, source_target_pairs={{0,24},{4,28},{8,16},{12,20},{16,8},{20,12},{24,0},{28,4},{1,25},{... | collective-permute-start | bytes 393224 | tf_op jit(solution)/shard_map/ppermute | solution.py:34
  20.6 1.3 %collective-permute-start.9 = (bf16[64,1024]{1,0:T(8,128)(2,1)S(1)}, bf16[64,1024]{1,0:T(8,128)(2,1)}, u32[]{:S(2)}, u32[]{:S(2)}) collective-permute-start(bf16[64,1024]{1,0:T(8,128)(2,1)S(1)} %collective-permute-done.4.refs_6_), channel_id=1, source_target_pairs={{0,1},{1,0},{2,3},{3,2},{4,5},{5,4},{6,7},{7,6},{8,9},{9,8},{10,11... | collective-permute-start | bytes 393224 | tf_op jit(solution)/shard_map/ppermute | solution.py:34
  22.0 0.5 %collective-permute-start.5 = (bf16[128,512]{1,0:T(8,128)(2,1)}, bf16[128,512]{1,0:T(8,128)(2,1)S(1)}, u32[]{:S(2)}, u32[]{:S(2)}) collective-permute-start(bf16[128,512]{1,0:T(8,128)(2,1)} %get-tuple-element.50), channel_id=1, source_target_pairs={{0,8},{4,12},{8,0},{12,4},{16,24},{20,28},{24,16},{28,20},{1,9},{5... | collective-permute-start | bytes 393224 | tf_op jit(solution)/shard_map/ppermute | solution.py:34
  22.5 0.6 %collective-permute-start.6 = (bf16[128,512]{1,0:T(8,128)(2,1)}, bf16[128,512]{1,0:T(8,128)(2,1)S(1)}, u32[]{:S(2)}, u32[]{:S(2)}) collective-permute-start(bf16[128,512]{1,0:T(8,128)(2,1)} %get-tuple-element.51), channel_id=1, source_target_pairs={{0,16},{4,20},{8,24},{12,28},{16,0},{20,4},{24,8},{28,12},{1,17},{... | collective-permute-start | bytes 393224 | tf_op jit(solution)/shard_map/ppermute | solution.py:34
  23.1 1.9 %collective-permute-done.7.refs_0_ = bf16[128,512]{1,0:T(8,128)(2,1)S(1)} collective-permute-done((bf16[128,512]{1,0:T(8,128)(2,1)S(1)}, bf16[128,512]{1,0:T(8,128)(2,1)S(1)}, u32[]{:S(2)}, u32[]{:S(2)}) %collective-permute-start.7) | collective-permute-done | bytes 131104 | tf_op jit(solution)/shard_map/ppermute | solution.py:34
  25.1 0.0 collective-permute-done.8.refs_2_.refs_4_.other
  25.1 1.1 %attend.2.attended = bf16[2,128,256]{2,1,0:T(8,128)(2,1)S(1)} custom-call(s32[1]{0:T(128)} %bitcast.me_ref, bf16[128,512]{1,0:T(8,128)(2,1)S(1)} %collective-permute-done.7.refs_0_, bf16[1408,512]{1,0:T(8,128)(2,1)S(1)} %stack.1.refs_1_.refs_3_.own, bf16[1408,512]{1,0:T(8,128)(2,1)S(1)} %collective-permute-done.8.refs_2_.refs_4_.other), custom_call_target="tpu_custom_call" | custom-call | flops 268435456 | bytes 2359296 | tf_op jit(solution)/shard_map/attend/pallas_call | solution.py:346
  26.2 0.2 collective-permute-done.9.last
  26.3 0.0 collective-permute-start.10
  26.3 1.0 %collect.1.weights = bf16[2,256,1024]{2,1,0:T(8,128)(2,1)S(1)} custom-call(s32[1]{0:T(128)} %bitcast.1.index_ref, bf16[1408,512]{1,0:T(8,128)(2,1)S(1)} %stack.1.refs_1_.refs_3_.own, bf16[64,1024]{1,0:T(8,128)(2,1)} %collective-permute-done.9.last, bf16[1408,512]{1,0:T(8,128)(2,1)S(1)} %collective-permute-done.8.refs_2_.refs_4_.other), custom_call_target="tpu_custom_call" | custom-call | bytes 2097152 | tf_op jit(solution)/shard_map/collect/pallas_call | solution.py:259
  27.3 0.5 %collective-permute-done.5.refs_1_ = bf16[128,512]{1,0:T(8,128)(2,1)S(1)} collective-permute-done((bf16[128,512]{1,0:T(8,128)(2,1)}, bf16[128,512]{1,0:T(8,128)(2,1)S(1)}, u32[]{:S(2)}, u32[]{:S(2)}) %collective-permute-start.5) | collective-permute-done | bytes 131104 | tf_op jit(solution)/shard_map/ppermute | solution.py:34
  27.8 0.0 collective-permute-done.6.refs_2_
  27.8 0.1 collective-permute-done.10.last
  27.9 0.4 project.3
  28.2 1.7 %collective-permute-start.12 = (bf16[128,1024]{1,0:T(8,128)(2,1)S(1)}, bf16[128,1024]{1,0:T(8,128)(2,1)S(1)}, u32[]{:S(2)}, u32[]{:S(2)}) collective-permute-start(bf16[128,1024]{1,0:T(8,128)(2,1)S(1)} %project.3), channel_id=1, source_target_pairs={{0,8},{4,20},{8,0},{12,28},{16,24},{20,4},{24,16},{28,12},{1,9},{5... | collective-permute-start | bytes 786440 | tf_op jit(solution)/shard_map/ppermute | solution.py:443
  29.9 1.9 %attend.3.attended = bf16[2,384,256]{2,1,0:T(8,128)(2,1)S(1)} custom-call(s32[1]{0:T(128)} %bitcast.me_ref, bf16[128,512]{1,0:T(8,128)(2,1)S(1)} %get-tuple-element.54.refs_0_, bf16[128,512]{1,0:T(8,128)(2,1)S(1)} %collective-permute-done.5.refs_1_, bf16[128,512]{1,0:T(8,128)(2,1)S(1)} %collective-permute-done.6.refs_2_, ...), custom_call_target="tpu_custom_call" | custom-call | flops 805306368 | bytes 2883584 | tf_op jit(solution)/shard_map/attend/pallas_call | solution.py:346
  31.8 0.0 copy-start
  31.8 0.0 copy-start.1
  31.8 0.0 copy-start.2
  31.8 0.0 copy-start.3
  31.8 0.7 %project.2 = (bf16[128,1024]{1,0:T(8,128)(2,1)S(1)}, f32[128,1024]{1,0:T(8,128)S(1)}, f32[128,1024]{1,0:T(8,128)S(1)}) custom-call(s32[1]{0:T(128)} %bitcast.me_ref, s32[1]{0:T(128)} %bitcast.1.index_ref, bf16[2,384,256]{2,1,0:T(8,128)(2,1)S(1)} %attend.3.attended, bf16[2,256,1024]{2,1,0:T(8,128)(2,1)S(1)} %collect.1.weights, ...), custom_call_target="tpu_custom_call" | custom-call | flops 402653184 | bytes 3538944 | tf_op jit(solution)/shard_map/project/pallas_call | solution.py:407
  32.5 0.7 %collective-permute-start.11 = (bf16[128,1024]{1,0:T(8,128)(2,1)S(1)}, bf16[128,1024]{1,0:T(8,128)(2,1)S(1)}, u32[]{:S(2)}, u32[]{:S(2)}) collective-permute-start(bf16[128,1024]{1,0:T(8,128)(2,1)S(1)} %get-tuple-element.59), channel_id=1, source_target_pairs={{0,8},{4,20},{8,0},{12,28},{16,24},{20,4},{24,16},{28,12},{1,9},{5... | collective-permute-start | bytes 786440 | tf_op jit(solution)/shard_map/ppermute | solution.py:443
  33.3 1.4 %collective-permute-done.12.passed = bf16[128,1024]{1,0:T(8,128)(2,1)S(1)} collective-permute-done((bf16[128,1024]{1,0:T(8,128)(2,1)S(1)}, bf16[128,1024]{1,0:T(8,128)(2,1)S(1)}, u32[]{:S(2)}, u32[]{:S(2)}) %collective-permute-start.12) | collective-permute-done | bytes 262176 | tf_op jit(solution)/shard_map/ppermute | solution.py:443
  34.7 1.5 %collective-permute-start.13 = (bf16[128,1024]{1,0:T(8,128)(2,1)S(1)}, bf16[128,1024]{1,0:T(8,128)(2,1)S(1)}, u32[]{:S(2)}, u32[]{:S(2)}) collective-permute-start(bf16[128,1024]{1,0:T(8,128)(2,1)S(1)} %add.64), channel_id=1, source_target_pairs={{0,16},{4,12},{8,24},{12,4},{16,0},{20,28},{24,8},{28,20},{1,17},{... | collective-permute-start | bytes 786440 | tf_op jit(solution)/shard_map/ppermute | solution.py:443
  36.2 0.0 copy-done
  36.2 0.0 copy-done.1
  36.2 0.0 copy-done.2
  36.2 0.0 copy-done.3
  36.2 0.9 %multiply_subtract_fusion = f32[64,1024]{1,0:T(8,128)} fusion(f32[64,1024]{1,0:T(8,128)S(1)} %copy-done, f32[64,1024]{1,0:T(8,128)S(1)} %copy-done.3, f32[64,1024]{1,0:T(8,128)S(1)} %copy-done.2, f32[64,1024]{1,0:T(8,128)S(1)} %copy-done.1), kind=kLoop, calls=%fused_computation.10 | loop fusion | flops 983040 | bytes 1310720 | tf_op jit(solution)/shard_map/sub | solution.py:28
  37.1 4.2 %collective-permute-done.11 = bf16[128,1024]{1,0:T(8,128)(2,1)S(1)} collective-permute-done((bf16[128,1024]{1,0:T(8,128)(2,1)S(1)}, bf16[128,1024]{1,0:T(8,128)(2,1)S(1)}, u32[]{:S(2)}, u32[]{:S(2)}) %collective-permute-start.11) | collective-permute-done | bytes 262176 | tf_op jit(solution)/shard_map/ppermute | solution.py:443
  41.3 0.1 convert_add_fusion
  41.4 0.0 collective-permute-done.13
  41.4 0.8 %fusion.6 = bf16[1,128,1024]{2,1,0:T(8,128)(2,1)} fusion(f32[128,1024]{1,0:T(8,128)S(1)} %convert_add_fusion, bf16[128,1024]{1,0:T(8,128)(2,1)S(1)} %collective-permute-done.13), kind=kLoop, calls=%fused_computation.9 | loop fusion | flops 393216 | bytes 1048576 | tf_op jit(solution)/shard_map/broadcast_in_dim | solution.py:508
  (1 shorter events, 0.0 us)
Async XLA Ops:
  1.6 12.8 %collective-permute-start.2 = (bf16[2,128,512]{2,1,0:T(8,128)(2,1)S(1)}, bf16[2,128,512]{2,1,0:T(8,128)(2,1)S(1)}, u32[]{:S(2)}, u32[]{:S(2)}) collective-permute-start(bf16[2,128,512]{2,1,0:T(8,128)(2,1)S(1)} %pack_far.1), channel_id=1, source_target_pairs={{0,24},{4,28},{8,16},{12,20},{16,8},{20,12},{24,0},{28,4},{1,25},{... | collective-permute-start | bytes 786440 | tf_op jit(solution)/shard_map/ppermute | solution.py:34
  7.4 10.4 %collective-permute-start = (bf16[2,128,512]{2,1,0:T(8,128)(2,1)S(1)}, bf16[2,128,512]{2,1,0:T(8,128)(2,1)S(1)}, u32[]{:S(2)}, u32[]{:S(2)}) collective-permute-start(bf16[2,128,512]{2,1,0:T(8,128)(2,1)S(1)} %get-tuple-element.35), channel_id=1, source_target_pairs={{0,8},{4,12},{8,0},{12,4},{16,24},{20,28},{24,16},{28,20},{1,9},{5... | collective-permute-start | bytes 786440 | tf_op jit(solution)/shard_map/ppermute | solution.py:34
  8.0 9.8 %collective-permute-start.1 = (bf16[2,128,512]{2,1,0:T(8,128)(2,1)S(1)}, bf16[2,128,512]{2,1,0:T(8,128)(2,1)S(1)}, u32[]{:S(2)}, u32[]{:S(2)}) collective-permute-start(bf16[2,128,512]{2,1,0:T(8,128)(2,1)S(1)} %get-tuple-element.36), channel_id=1, source_target_pairs={{0,16},{4,20},{8,24},{12,28},{16,0},{20,4},{24,8},{28,12},{1,17},{... | collective-permute-start | bytes 786440 | tf_op jit(solution)/shard_map/ppermute | solution.py:34
  8.0 9.8 %collective-permute-start.3 = (bf16[64,1024]{1,0:T(8,128)(2,1)S(1)}, bf16[64,1024]{1,0:T(8,128)(2,1)S(1)}, u32[]{:S(2)}, u32[]{:S(2)}) collective-permute-start(bf16[64,1024]{1,0:T(8,128)(2,1)S(1)} %get-tuple-element.38.refs_4_), channel_id=1, source_target_pairs={{0,1},{1,0},{2,3},{3,2},{4,5},{5,4},{6,7},{7,6},{8,9},{9,8},{10,11... | collective-permute-start | bytes 393224 | tf_op jit(solution)/shard_map/ppermute | solution.py:34
  10.1 7.9 %collective-permute-start.4 = (bf16[64,1024]{1,0:T(8,128)(2,1)S(1)}, bf16[64,1024]{1,0:T(8,128)(2,1)S(1)}, u32[]{:S(2)}, u32[]{:S(2)}) collective-permute-start(bf16[64,1024]{1,0:T(8,128)(2,1)S(1)} %get-tuple-element.38.refs_4_), channel_id=1, source_target_pairs={{0,2},{1,3},{2,0},{3,1},{4,6},{5,7},{6,4},{7,5},{8,10},{9,11},{10,... | collective-permute-start | bytes 393224 | tf_op jit(solution)/shard_map/ppermute | solution.py:34
  18.0 7.0 %collective-permute-start.8 = (bf16[1408,512]{1,0:T(8,128)(2,1)S(1)}, bf16[1408,512]{1,0:T(8,128)(2,1)S(1)}, u32[]{:S(2)}, u32[]{:S(2)}) collective-permute-start(bf16[1408,512]{1,0:T(8,128)(2,1)S(1)} %stack.1.refs_1_.refs_3_.own), channel_id=1, source_target_pairs={{0,4},{4,0},{8,12},{12,8},{16,20},{20,16},{24,28},{28,24},{1,5},{5... | collective-permute-start | bytes 4325384 | tf_op jit(solution)/shard_map/ppermute | solution.py:34
  18.1 7.0 %collective-permute-start.7 = (bf16[128,512]{1,0:T(8,128)(2,1)S(1)}, bf16[128,512]{1,0:T(8,128)(2,1)S(1)}, u32[]{:S(2)}, u32[]{:S(2)}) collective-permute-start(bf16[128,512]{1,0:T(8,128)(2,1)S(1)} %get-tuple-element.52), channel_id=1, source_target_pairs={{0,24},{4,28},{8,16},{12,20},{16,8},{20,12},{24,0},{28,4},{1,25},{... | collective-permute-start | bytes 393224 | tf_op jit(solution)/shard_map/ppermute | solution.py:34
  20.6 5.7 %collective-permute-start.9 = (bf16[64,1024]{1,0:T(8,128)(2,1)S(1)}, bf16[64,1024]{1,0:T(8,128)(2,1)}, u32[]{:S(2)}, u32[]{:S(2)}) collective-permute-start(bf16[64,1024]{1,0:T(8,128)(2,1)S(1)} %collective-permute-done.4.refs_6_), channel_id=1, source_target_pairs={{0,1},{1,0},{2,3},{3,2},{4,5},{5,4},{6,7},{7,6},{8,9},{9,8},{10,11... | collective-permute-start | bytes 393224 | tf_op jit(solution)/shard_map/ppermute | solution.py:34
  22.0 5.8 %collective-permute-start.5 = (bf16[128,512]{1,0:T(8,128)(2,1)}, bf16[128,512]{1,0:T(8,128)(2,1)S(1)}, u32[]{:S(2)}, u32[]{:S(2)}) collective-permute-start(bf16[128,512]{1,0:T(8,128)(2,1)} %get-tuple-element.50), channel_id=1, source_target_pairs={{0,8},{4,12},{8,0},{12,4},{16,24},{20,28},{24,16},{28,20},{1,9},{5... | collective-permute-start | bytes 393224 | tf_op jit(solution)/shard_map/ppermute | solution.py:34
  22.5 5.3 %collective-permute-start.6 = (bf16[128,512]{1,0:T(8,128)(2,1)}, bf16[128,512]{1,0:T(8,128)(2,1)S(1)}, u32[]{:S(2)}, u32[]{:S(2)}) collective-permute-start(bf16[128,512]{1,0:T(8,128)(2,1)} %get-tuple-element.51), channel_id=1, source_target_pairs={{0,16},{4,20},{8,24},{12,28},{16,0},{20,4},{24,8},{28,12},{1,17},{... | collective-permute-start | bytes 393224 | tf_op jit(solution)/shard_map/ppermute | solution.py:34
  26.3 1.6 %collective-permute-start.10 = (bf16[64,1024]{1,0:T(8,128)(2,1)}, bf16[64,1024]{1,0:T(8,128)(2,1)S(1)}, u32[]{:S(2)}, u32[]{:S(2)}) collective-permute-start(bf16[64,1024]{1,0:T(8,128)(2,1)} %collective-permute-done.9.last), channel_id=1, source_target_pairs={{0,4},{4,0},{8,12},{12,8},{16,20},{20,16},{24,28},{28,24},{1,5},{5... | collective-permute-start | bytes 393224 | tf_op jit(solution)/shard_map/ppermute | solution.py:34
  28.2 6.4 %collective-permute-start.12 = (bf16[128,1024]{1,0:T(8,128)(2,1)S(1)}, bf16[128,1024]{1,0:T(8,128)(2,1)S(1)}, u32[]{:S(2)}, u32[]{:S(2)}) collective-permute-start(bf16[128,1024]{1,0:T(8,128)(2,1)S(1)} %project.3), channel_id=1, source_target_pairs={{0,8},{4,20},{8,0},{12,28},{16,24},{20,4},{24,16},{28,12},{1,9},{5... | collective-permute-start | bytes 786440 | tf_op jit(solution)/shard_map/ppermute | solution.py:443
  31.8 4.4 %copy-start = (f32[64,1024]{1,0:T(8,128)S(1)}, f32[64,1024]{1,0:T(8,128)}, u32[]{:S(2)}) copy-start(f32[64,1024]{1,0:T(8,128)} %refs_0_.1) | copy-start | bytes 786436
  31.8 4.4 %copy-start.1 = (f32[64,1024]{1,0:T(8,128)S(1)}, f32[64,1024]{1,0:T(8,128)}, u32[]{:S(2)}) copy-start(f32[64,1024]{1,0:T(8,128)} %refs_1_.1) | copy-start | bytes 786436
  31.8 4.4 %copy-start.2 = (f32[64,1024]{1,0:T(8,128)S(1)}, f32[64,1024]{1,0:T(8,128)}, u32[]{:S(2)}) copy-start(f32[64,1024]{1,0:T(8,128)} %refs_2_.1) | copy-start | bytes 786436
  31.8 4.4 %copy-start.3 = (f32[64,1024]{1,0:T(8,128)S(1)}, f32[64,1024]{1,0:T(8,128)}, u32[]{:S(2)}) copy-start(f32[64,1024]{1,0:T(8,128)} %refs_3_.1) | copy-start | bytes 786436
  32.5 8.8 %collective-permute-start.11 = (bf16[128,1024]{1,0:T(8,128)(2,1)S(1)}, bf16[128,1024]{1,0:T(8,128)(2,1)S(1)}, u32[]{:S(2)}, u32[]{:S(2)}) collective-permute-start(bf16[128,1024]{1,0:T(8,128)(2,1)S(1)} %get-tuple-element.59), channel_id=1, source_target_pairs={{0,8},{4,20},{8,0},{12,28},{16,24},{20,4},{24,16},{28,12},{1,9},{5... | collective-permute-start | bytes 786440 | tf_op jit(solution)/shard_map/ppermute | solution.py:443
  34.7 6.7 %collective-permute-start.13 = (bf16[128,1024]{1,0:T(8,128)(2,1)S(1)}, bf16[128,1024]{1,0:T(8,128)(2,1)S(1)}, u32[]{:S(2)}, u32[]{:S(2)}) collective-permute-start(bf16[128,1024]{1,0:T(8,128)(2,1)S(1)} %add.64), channel_id=1, source_target_pairs={{0,16},{4,12},{8,24},{12,4},{16,0},{20,28},{24,8},{28,20},{1,17},{... | collective-permute-start | bytes 786440 | tf_op jit(solution)/shard_map/ppermute | solution.py:443

commit v8 on v7

--- a/solution.py
+++ b/solution.py
@@ -291,8 +291,7 @@
             return jnp.concatenate([own[at, columns], other[at, columns]], axis=0)
 
         ones = jnp.ones((2 * rows, LANES), own.dtype)
-        for head in range(width // HEAD_DIM):
-            columns = slice(head * HEAD_DIM, (head + 1) * HEAD_DIM)
+        def score_tiles(columns):
             tiles = []
             for c in range(order[-1] + 1):
                 first = min(place[chip] for chip in order if chip >= c)
@@ -307,6 +306,9 @@
                     later = [score[rows:]] if first + rows < many * rows else []
                     score = jnp.concatenate([masked, *later], axis=0)
                 tiles.append((c, first, score))
+            return tiles
+
+        def exponentials(tiles):
             highest = []
             for chip in order:
                 best = None
@@ -317,9 +319,14 @@
                         best = block if best is None else jnp.maximum(best, block)
                 highest.append(jnp.max(best, axis=1, keepdims=True))
             highest = jnp.concatenate(highest, axis=0)
+            return [
+                (c, first, jnp.exp2((score - highest[first:]) * scale).astype(jnp.bfloat16))
+                for c, first, score in tiles
+            ]
+
+        def combine(columns, tiles):
             totals, start = None, 0
-            for c, first, score in tiles:
-                expons = jnp.exp2((score - highest[first:]) * scale).astype(jnp.bfloat16)
+            for c, first, expons in tiles:
                 seen = jnp.concatenate([both(2 * (here ^ c) + 1, columns), ones], axis=1)
                 total = jnp.dot(expons, seen, preferred_element_type=jnp.float32)
                 totals = total if totals is None else totals[first - start :] + total
@@ -328,6 +335,13 @@
                     result[first : first + rows, columns] = (
                         totals[:rows, :HEAD_DIM] / totals[:rows, HEAD_DIM:]
                     ).astype(result.dtype)
+
+        heads = [
+            slice(head * HEAD_DIM, (head + 1) * HEAD_DIM) for head in range(width // HEAD_DIM)
+        ]
+        scores = [score_tiles(columns) for columns in heads]
+        for columns, tiles in zip(heads, scores):
+            combine(columns, exponentials(tiles))
         for index, distance in enumerate(distances):
             at = place[here ^ distance]
             for part in range(2):

time: 42.4 us -> 42.1 us (level)
  Pallas kernels: 9.65 us -> 9.04 us
  waiting for transfers between devices: 11.8 us -> 12.3 us
    pallas_call x2, Pallas kernels: 2.95 us -> 2.34 us  [attend(): pl.pallas_call(functools.partial(attend_kernel, distances, chips), out_sh...]
  transfers between devices with their start and end apart: 14 -> 14, of which waited for: 8 -> 9; matrix products, arithmetic and copies ran while one was open for 2% -> 2% of each run, Pallas kernels for 19% -> 18%
where the time goes in v8:
time: 42.1 us; the launch traced here: 41.9 us
  starting transfers between devices  18 us (43%)
  waiting for transfers between devices  12.3 us (29%)
  Pallas kernels  9.04 us (21%)
  other arithmetic  1.74 us (4%)
  between operations  0.77 us (2%)
    ppermute x11, starting transfers between devices, swap(): return lax.ppermute(array, axis, [(i, i ^ distance) for i in range(count)])  14.3 us
    ppermute x11, waiting for transfers between devices, swap(): return lax.ppermute(array, axis, [(i, i ^ distance) for i in range(count)])  6.34 us
    ppermute x3, waiting for transfers between devices, by_core(): lax.ppermute(part, 'seq', [(i, i ^ 2 * distance(i % 2)) for i in range(se...  6.01 us
    ppermute x3, starting transfers between devices, by_core(): lax.ppermute(part, 'seq', [(i, i ^ 2 * distance(i % 2)) for i in range(se...  3.71 us
    pallas_call x2, Pallas kernels, attend(): pl.pallas_call(functools.partial(attend_kernel, distances, chips), out_sh...  2.34 us
    pallas_call x1, Pallas kernels, pack(): pl.pallas_call(functools.partial(pack_kernel, far), out_shape=[like((2, r...  1.79 us
    pallas_call x1, Pallas kernels, pack_queries(): pl.pallas_call(pack_queries_kernel, out_shape=[like((rows, width), querie...  1.75 us
    pallas_call x2, Pallas kernels, project(): pl.pallas_call(functools.partial(project_kernel, chips), out_shape=[jax.S...  1.04 us
  transfers between devices with their start and end apart: 14, of which 9 were waited for; matrix products, arithmetic and copies ran while one was open for 2% of the time, Pallas kernels for 18%

profile of v8, /device:TPU:0, one launch (start us, length us, event | category | flops | bytes accessed | tf_op | source)
XLA Modules:
  0.0 41.9 jit_solution(15663484314203443454)
XLA Ops:
  0.6 1.0 %pack_far.1 = bf16[2,128,512]{2,1,0:T(8,128)(2,1)S(1)} custom-call(s32[1]{0:T(128)} %bitcast.me_ref, bf16[1,128,2048]{2,1,0:T(8,128)(2,1)} %keys.2, bf16[1,128,2048]{2,1,0:T(8,128)(2,1)} %values.3), custom_call_target="tpu_custom_call" | custom-call | bytes 524288 | tf_op jit(solution)/shard_map/pack_far/pallas_call | solution.py:88
  1.6 4.0 %collective-permute-start.2 = (bf16[2,128,512]{2,1,0:T(8,128)(2,1)S(1)}, bf16[2,128,512]{2,1,0:T(8,128)(2,1)S(1)}, u32[]{:S(2)}, u32[]{:S(2)}) collective-permute-start(bf16[2,128,512]{2,1,0:T(8,128)(2,1)S(1)} %pack_far.1), channel_id=1, source_target_pairs={{0,24},{4,28},{8,16},{12,20},{16,8},{20,12},{24,0},{28,4},{1,25},{... | collective-permute-start | bytes 786440 | tf_op jit(solution)/shard_map/ppermute | solution.py:34
  5.6 1.8 %pack.1 = (bf16[2,128,512]{2,1,0:T(8,128)(2,1)S(1)}, bf16[2,128,512]{2,1,0:T(8,128)(2,1)S(1)}, bf16[2,128,512]{2,1,0:T(8,128)(2,1)S(1)}, bf16[128,512]{1,0:T(8,128)(2,1)S(1)}, bf16[64,1024]{1,0:T(8,128)(2,1)S(1)}) custom-call(s32[1]{0:T(128)} %bitcast.me_ref, bf16[1,128,2048]{2,1,0:T(8,128)(2,1)} %keys.2, bf16[1,128,2048]{2,1,0:T(8,128)(2,1)} %values.3, ...), custom_call_target="tpu_custom_call" | custom-call | bytes 3276800 | tf_op jit(solution)/shard_map/pack/pallas_call | solution.py:139
  7.4 0.6 %collective-permute-start = (bf16[2,128,512]{2,1,0:T(8,128)(2,1)S(1)}, bf16[2,128,512]{2,1,0:T(8,128)(2,1)S(1)}, u32[]{:S(2)}, u32[]{:S(2)}) collective-permute-start(bf16[2,128,512]{2,1,0:T(8,128)(2,1)S(1)} %get-tuple-element.35), channel_id=1, source_target_pairs={{0,8},{4,12},{8,0},{12,4},{16,24},{20,28},{24,16},{28,20},{1,9},{5... | collective-permute-start | bytes 786440 | tf_op jit(solution)/shard_map/ppermute | solution.py:34
  8.0 0.1 collective-permute-start.1
  8.0 2.0 %collective-permute-start.3 = (bf16[64,1024]{1,0:T(8,128)(2,1)S(1)}, bf16[64,1024]{1,0:T(8,128)(2,1)S(1)}, u32[]{:S(2)}, u32[]{:S(2)}) collective-permute-start(bf16[64,1024]{1,0:T(8,128)(2,1)S(1)} %get-tuple-element.38.refs_4_), channel_id=1, source_target_pairs={{0,1},{1,0},{2,3},{3,2},{4,5},{5,4},{6,7},{7,6},{8,9},{9,8},{10,11... | collective-permute-start | bytes 393224 | tf_op jit(solution)/shard_map/ppermute | solution.py:34
  10.1 2.6 %collective-permute-start.4 = (bf16[64,1024]{1,0:T(8,128)(2,1)S(1)}, bf16[64,1024]{1,0:T(8,128)(2,1)S(1)}, u32[]{:S(2)}, u32[]{:S(2)}) collective-permute-start(bf16[64,1024]{1,0:T(8,128)(2,1)S(1)} %get-tuple-element.38.refs_4_), channel_id=1, source_target_pairs={{0,2},{1,3},{2,0},{3,1},{4,6},{5,7},{6,4},{7,5},{8,10},{9,11},{10,... | collective-permute-start | bytes 393224 | tf_op jit(solution)/shard_map/ppermute | solution.py:34
  12.7 1.8 %pack_queries.1 = (bf16[128,512]{1,0:T(8,128)(2,1)}, bf16[128,512]{1,0:T(8,128)(2,1)}, bf16[128,512]{1,0:T(8,128)(2,1)S(1)}) custom-call(s32[1]{0:T(128)} %bitcast.me_ref, bf16[1,128,2048]{2,1,0:T(8,128)(2,1)} %queries.2), custom_call_target="tpu_custom_call" | custom-call | bytes 1048576 | tf_op jit(solution)/shard_map/pack_queries/pallas_call | solution.py:175
  14.4 0.0 collective-permute-done.2.refs_3_
  14.4 3.4 %collective-permute-done.refs_1_ = bf16[2,128,512]{2,1,0:T(8,128)(2,1)S(1)} collective-permute-done((bf16[2,128,512]{2,1,0:T(8,128)(2,1)S(1)}, bf16[2,128,512]{2,1,0:T(8,128)(2,1)S(1)}, u32[]{:S(2)}, u32[]{:S(2)}) %collective-permute-start) | collective-permute-done | bytes 262176 | tf_op jit(solution)/shard_map/ppermute | solution.py:34
  17.8 0.0 collective-permute-done.1.refs_2_
  17.8 0.0 collective-permute-done.3.refs_5_
  17.8 0.1 collective-permute-done.4.refs_6_
  17.9 0.1 stack.1.refs_1_.refs_3_.own
  18.0 0.1 collective-permute-start.8
  18.1 2.5 %collective-permute-start.7 = (bf16[128,512]{1,0:T(8,128)(2,1)S(1)}, bf16[128,512]{1,0:T(8,128)(2,1)S(1)}, u32[]{:S(2)}, u32[]{:S(2)}) collective-permute-start(bf16[128,512]{1,0:T(8,128)(2,1)S(1)} %get-tuple-element.52), channel_id=1, source_target_pairs={{0,24},{4,28},{8,16},{12,20},{16,8},{20,12},{24,0},{28,4},{1,25},{... | collective-permute-start | bytes 393224 | tf_op jit(solution)/shard_map/ppermute | solution.py:34
  20.6 1.3 %collective-permute-start.9 = (bf16[64,1024]{1,0:T(8,128)(2,1)S(1)}, bf16[64,1024]{1,0:T(8,128)(2,1)}, u32[]{:S(2)}, u32[]{:S(2)}) collective-permute-start(bf16[64,1024]{1,0:T(8,128)(2,1)S(1)} %collective-permute-done.4.refs_6_), channel_id=1, source_target_pairs={{0,1},{1,0},{2,3},{3,2},{4,5},{5,4},{6,7},{7,6},{8,9},{9,8},{10,11... | collective-permute-start | bytes 393224 | tf_op jit(solution)/shard_map/ppermute | solution.py:34
  22.0 0.5 %collective-permute-start.5 = (bf16[128,512]{1,0:T(8,128)(2,1)}, bf16[128,512]{1,0:T(8,128)(2,1)S(1)}, u32[]{:S(2)}, u32[]{:S(2)}) collective-permute-start(bf16[128,512]{1,0:T(8,128)(2,1)} %get-tuple-element.50), channel_id=1, source_target_pairs={{0,8},{4,12},{8,0},{12,4},{16,24},{20,28},{24,16},{28,20},{1,9},{5... | collective-permute-start | bytes 393224 | tf_op jit(solution)/shard_map/ppermute | solution.py:34
  22.5 0.6 %collective-permute-start.6 = (bf16[128,512]{1,0:T(8,128)(2,1)}, bf16[128,512]{1,0:T(8,128)(2,1)S(1)}, u32[]{:S(2)}, u32[]{:S(2)}) collective-permute-start(bf16[128,512]{1,0:T(8,128)(2,1)} %get-tuple-element.51), channel_id=1, source_target_pairs={{0,16},{4,20},{8,24},{12,28},{16,0},{20,4},{24,8},{28,12},{1,17},{... | collective-permute-start | bytes 393224 | tf_op jit(solution)/shard_map/ppermute | solution.py:34
  23.1 1.9 %collective-permute-done.7.refs_0_ = bf16[128,512]{1,0:T(8,128)(2,1)S(1)} collective-permute-done((bf16[128,512]{1,0:T(8,128)(2,1)S(1)}, bf16[128,512]{1,0:T(8,128)(2,1)S(1)}, u32[]{:S(2)}, u32[]{:S(2)}) %collective-permute-start.7) | collective-permute-done | bytes 131104 | tf_op jit(solution)/shard_map/ppermute | solution.py:34
  25.1 0.0 collective-permute-done.8.refs_2_.refs_4_.other
  25.1 0.9 %attend.2.attended = bf16[2,128,256]{2,1,0:T(8,128)(2,1)S(1)} custom-call(s32[1]{0:T(128)} %bitcast.me_ref, bf16[128,512]{1,0:T(8,128)(2,1)S(1)} %collective-permute-done.7.refs_0_, bf16[1408,512]{1,0:T(8,128)(2,1)S(1)} %stack.1.refs_1_.refs_3_.own, bf16[1408,512]{1,0:T(8,128)(2,1)S(1)} %collective-permute-done.8.refs_2_.refs_4_.other), custom_call_target="tpu_custom_call" | custom-call | flops 268435456 | bytes 2359296 | tf_op jit(solution)/shard_map/attend/pallas_call | solution.py:360
  26.0 0.3 collective-permute-done.9.last
  26.3 0.0 collective-permute-start.10
  26.3 1.0 %collect.1.weights = bf16[2,256,1024]{2,1,0:T(8,128)(2,1)S(1)} custom-call(s32[1]{0:T(128)} %bitcast.1.index_ref, bf16[1408,512]{1,0:T(8,128)(2,1)S(1)} %stack.1.refs_1_.refs_3_.own, bf16[64,1024]{1,0:T(8,128)(2,1)} %collective-permute-done.9.last, bf16[1408,512]{1,0:T(8,128)(2,1)S(1)} %collective-permute-done.8.refs_2_.refs_4_.other), custom_call_target="tpu_custom_call" | custom-call | bytes 2097152 | tf_op jit(solution)/shard_map/collect/pallas_call | solution.py:259
  27.3 0.5 %collective-permute-done.5.refs_1_ = bf16[128,512]{1,0:T(8,128)(2,1)S(1)} collective-permute-done((bf16[128,512]{1,0:T(8,128)(2,1)}, bf16[128,512]{1,0:T(8,128)(2,1)S(1)}, u32[]{:S(2)}, u32[]{:S(2)}) %collective-permute-start.5) | collective-permute-done | bytes 131104 | tf_op jit(solution)/shard_map/ppermute | solution.py:34
  27.8 0.0 collective-permute-done.6.refs_2_
  27.8 0.1 collective-permute-done.10.last
  27.9 0.4 project.3
  28.2 1.7 %collective-permute-start.12 = (bf16[128,1024]{1,0:T(8,128)(2,1)S(1)}, bf16[128,1024]{1,0:T(8,128)(2,1)S(1)}, u32[]{:S(2)}, u32[]{:S(2)}) collective-permute-start(bf16[128,1024]{1,0:T(8,128)(2,1)S(1)} %project.3), channel_id=1, source_target_pairs={{0,8},{4,20},{8,0},{12,28},{16,24},{20,4},{24,16},{28,12},{1,9},{5... | collective-permute-start | bytes 786440 | tf_op jit(solution)/shard_map/ppermute | solution.py:457
  29.9 1.4 %attend.3.attended = bf16[2,384,256]{2,1,0:T(8,128)(2,1)S(1)} custom-call(s32[1]{0:T(128)} %bitcast.me_ref, bf16[128,512]{1,0:T(8,128)(2,1)S(1)} %get-tuple-element.54.refs_0_, bf16[128,512]{1,0:T(8,128)(2,1)S(1)} %collective-permute-done.5.refs_1_, bf16[128,512]{1,0:T(8,128)(2,1)S(1)} %collective-permute-done.6.refs_2_, ...), custom_call_target="tpu_custom_call" | custom-call | flops 805306368 | bytes 2883584 | tf_op jit(solution)/shard_map/attend/pallas_call | solution.py:360
  31.3 0.0 copy-start
  31.4 0.0 copy-start.1
  31.4 0.0 copy-start.2
  31.4 0.0 copy-start.3
  31.4 0.7 %project.2 = (bf16[128,1024]{1,0:T(8,128)(2,1)S(1)}, f32[128,1024]{1,0:T(8,128)S(1)}, f32[128,1024]{1,0:T(8,128)S(1)}) custom-call(s32[1]{0:T(128)} %bitcast.me_ref, s32[1]{0:T(128)} %bitcast.1.index_ref, bf16[2,384,256]{2,1,0:T(8,128)(2,1)S(1)} %attend.3.attended, bf16[2,256,1024]{2,1,0:T(8,128)(2,1)S(1)} %collect.1.weights, ...), custom_call_target="tpu_custom_call" | custom-call | flops 402653184 | bytes 3538944 | tf_op jit(solution)/shard_map/project/pallas_call | solution.py:421
  32.1 0.6 %collective-permute-start.11 = (bf16[128,1024]{1,0:T(8,128)(2,1)S(1)}, bf16[128,1024]{1,0:T(8,128)(2,1)S(1)}, u32[]{:S(2)}, u32[]{:S(2)}) collective-permute-start(bf16[128,1024]{1,0:T(8,128)(2,1)S(1)} %get-tuple-element.59), channel_id=1, source_target_pairs={{0,8},{4,20},{8,0},{12,28},{16,24},{20,4},{24,16},{28,12},{1,9},{5... | collective-permute-start | bytes 786440 | tf_op jit(solution)/shard_map/ppermute | solution.py:457
  32.7 2.0 %collective-permute-done.12.passed = bf16[128,1024]{1,0:T(8,128)(2,1)S(1)} collective-permute-done((bf16[128,1024]{1,0:T(8,128)(2,1)S(1)}, bf16[128,1024]{1,0:T(8,128)(2,1)S(1)}, u32[]{:S(2)}, u32[]{:S(2)}) %collective-permute-start.12) | collective-permute-done | bytes 262176 | tf_op jit(solution)/shard_map/ppermute | solution.py:457
  34.7 1.5 %collective-permute-start.13 = (bf16[128,1024]{1,0:T(8,128)(2,1)S(1)}, bf16[128,1024]{1,0:T(8,128)(2,1)S(1)}, u32[]{:S(2)}, u32[]{:S(2)}) collective-permute-start(bf16[128,1024]{1,0:T(8,128)(2,1)S(1)} %add.64), channel_id=1, source_target_pairs={{0,16},{4,12},{8,24},{12,4},{16,0},{20,28},{24,8},{28,20},{1,17},{... | collective-permute-start | bytes 786440 | tf_op jit(solution)/shard_map/ppermute | solution.py:457
  36.2 0.0 copy-done
  36.2 0.0 copy-done.1
  36.2 0.0 copy-done.2
  36.2 0.0 copy-done.3
  36.2 0.9 %multiply_subtract_fusion = f32[64,1024]{1,0:T(8,128)} fusion(f32[64,1024]{1,0:T(8,128)S(1)} %copy-done, f32[64,1024]{1,0:T(8,128)S(1)} %copy-done.3, f32[64,1024]{1,0:T(8,128)S(1)} %copy-done.2, f32[64,1024]{1,0:T(8,128)S(1)} %copy-done.1), kind=kLoop, calls=%fused_computation.10 | loop fusion | flops 983040 | bytes 1310720 | tf_op jit(solution)/shard_map/sub | solution.py:28
  37.1 3.2 %collective-permute-done.11 = bf16[128,1024]{1,0:T(8,128)(2,1)S(1)} collective-permute-done((bf16[128,1024]{1,0:T(8,128)(2,1)S(1)}, bf16[128,1024]{1,0:T(8,128)(2,1)S(1)}, u32[]{:S(2)}, u32[]{:S(2)}) %collective-permute-start.11) | collective-permute-done | bytes 262176 | tf_op jit(solution)/shard_map/ppermute | solution.py:457
  40.3 0.1 convert_add_fusion
  40.4 0.8 %collective-permute-done.13 = bf16[128,1024]{1,0:T(8,128)(2,1)S(1)} collective-permute-done((bf16[128,1024]{1,0:T(8,128)(2,1)S(1)}, bf16[128,1024]{1,0:T(8,128)(2,1)S(1)}, u32[]{:S(2)}, u32[]{:S(2)}) %collective-permute-start.13) | collective-permute-done | bytes 262176 | tf_op jit(solution)/shard_map/ppermute | solution.py:457
  41.2 0.8 %fusion.6 = bf16[1,128,1024]{2,1,0:T(8,128)(2,1)} fusion(f32[128,1024]{1,0:T(8,128)S(1)} %convert_add_fusion, bf16[128,1024]{1,0:T(8,128)(2,1)S(1)} %collective-permute-done.13), kind=kLoop, calls=%fused_computation.9 | loop fusion | flops 393216 | bytes 1048576 | tf_op jit(solution)/shard_map/broadcast_in_dim | solution.py:522
  (1 shorter events, 0.0 us)
Async XLA Ops:
  1.6 12.8 %collective-permute-start.2 = (bf16[2,128,512]{2,1,0:T(8,128)(2,1)S(1)}, bf16[2,128,512]{2,1,0:T(8,128)(2,1)S(1)}, u32[]{:S(2)}, u32[]{:S(2)}) collective-permute-start(bf16[2,128,512]{2,1,0:T(8,128)(2,1)S(1)} %pack_far.1), channel_id=1, source_target_pairs={{0,24},{4,28},{8,16},{12,20},{16,8},{20,12},{24,0},{28,4},{1,25},{... | collective-permute-start | bytes 786440 | tf_op jit(solution)/shard_map/ppermute | solution.py:34
  7.4 10.4 %collective-permute-start = (bf16[2,128,512]{2,1,0:T(8,128)(2,1)S(1)}, bf16[2,128,512]{2,1,0:T(8,128)(2,1)S(1)}, u32[]{:S(2)}, u32[]{:S(2)}) collective-permute-start(bf16[2,128,512]{2,1,0:T(8,128)(2,1)S(1)} %get-tuple-element.35), channel_id=1, source_target_pairs={{0,8},{4,12},{8,0},{12,4},{16,24},{20,28},{24,16},{28,20},{1,9},{5... | collective-permute-start | bytes 786440 | tf_op jit(solution)/shard_map/ppermute | solution.py:34
  8.0 9.8 %collective-permute-start.1 = (bf16[2,128,512]{2,1,0:T(8,128)(2,1)S(1)}, bf16[2,128,512]{2,1,0:T(8,128)(2,1)S(1)}, u32[]{:S(2)}, u32[]{:S(2)}) collective-permute-start(bf16[2,128,512]{2,1,0:T(8,128)(2,1)S(1)} %get-tuple-element.36), channel_id=1, source_target_pairs={{0,16},{4,20},{8,24},{12,28},{16,0},{20,4},{24,8},{28,12},{1,17},{... | collective-permute-start | bytes 786440 | tf_op jit(solution)/shard_map/ppermute | solution.py:34
  8.0 9.8 %collective-permute-start.3 = (bf16[64,1024]{1,0:T(8,128)(2,1)S(1)}, bf16[64,1024]{1,0:T(8,128)(2,1)S(1)}, u32[]{:S(2)}, u32[]{:S(2)}) collective-permute-start(bf16[64,1024]{1,0:T(8,128)(2,1)S(1)} %get-tuple-element.38.refs_4_), channel_id=1, source_target_pairs={{0,1},{1,0},{2,3},{3,2},{4,5},{5,4},{6,7},{7,6},{8,9},{9,8},{10,11... | collective-permute-start | bytes 393224 | tf_op jit(solution)/shard_map/ppermute | solution.py:34
  10.1 7.9 %collective-permute-start.4 = (bf16[64,1024]{1,0:T(8,128)(2,1)S(1)}, bf16[64,1024]{1,0:T(8,128)(2,1)S(1)}, u32[]{:S(2)}, u32[]{:S(2)}) collective-permute-start(bf16[64,1024]{1,0:T(8,128)(2,1)S(1)} %get-tuple-element.38.refs_4_), channel_id=1, source_target_pairs={{0,2},{1,3},{2,0},{3,1},{4,6},{5,7},{6,4},{7,5},{8,10},{9,11},{10,... | collective-permute-start | bytes 393224 | tf_op jit(solution)/shard_map/ppermute | solution.py:34
  18.0 7.0 %collective-permute-start.8 = (bf16[1408,512]{1,0:T(8,128)(2,1)S(1)}, bf16[1408,512]{1,0:T(8,128)(2,1)S(1)}, u32[]{:S(2)}, u32[]{:S(2)}) collective-permute-start(bf16[1408,512]{1,0:T(8,128)(2,1)S(1)} %stack.1.refs_1_.refs_3_.own), channel_id=1, source_target_pairs={{0,4},{4,0},{8,12},{12,8},{16,20},{20,16},{24,28},{28,24},{1,5},{5... | collective-permute-start | bytes 4325384 | tf_op jit(solution)/shard_map/ppermute | solution.py:34
  18.1 7.0 %collective-permute-start.7 = (bf16[128,512]{1,0:T(8,128)(2,1)S(1)}, bf16[128,512]{1,0:T(8,128)(2,1)S(1)}, u32[]{:S(2)}, u32[]{:S(2)}) collective-permute-start(bf16[128,512]{1,0:T(8,128)(2,1)S(1)} %get-tuple-element.52), channel_id=1, source_target_pairs={{0,24},{4,28},{8,16},{12,20},{16,8},{20,12},{24,0},{28,4},{1,25},{... | collective-permute-start | bytes 393224 | tf_op jit(solution)/shard_map/ppermute | solution.py:34
  20.6 5.7 %collective-permute-start.9 = (bf16[64,1024]{1,0:T(8,128)(2,1)S(1)}, bf16[64,1024]{1,0:T(8,128)(2,1)}, u32[]{:S(2)}, u32[]{:S(2)}) collective-permute-start(bf16[64,1024]{1,0:T(8,128)(2,1)S(1)} %collective-permute-done.4.refs_6_), channel_id=1, source_target_pairs={{0,1},{1,0},{2,3},{3,2},{4,5},{5,4},{6,7},{7,6},{8,9},{9,8},{10,11... | collective-permute-start | bytes 393224 | tf_op jit(solution)/shard_map/ppermute | solution.py:34
  22.0 5.8 %collective-permute-start.5 = (bf16[128,512]{1,0:T(8,128)(2,1)}, bf16[128,512]{1,0:T(8,128)(2,1)S(1)}, u32[]{:S(2)}, u32[]{:S(2)}) collective-permute-start(bf16[128,512]{1,0:T(8,128)(2,1)} %get-tuple-element.50), channel_id=1, source_target_pairs={{0,8},{4,12},{8,0},{12,4},{16,24},{20,28},{24,16},{28,20},{1,9},{5... | collective-permute-start | bytes 393224 | tf_op jit(solution)/shard_map/ppermute | solution.py:34
  22.5 5.3 %collective-permute-start.6 = (bf16[128,512]{1,0:T(8,128)(2,1)}, bf16[128,512]{1,0:T(8,128)(2,1)S(1)}, u32[]{:S(2)}, u32[]{:S(2)}) collective-permute-start(bf16[128,512]{1,0:T(8,128)(2,1)} %get-tuple-element.51), channel_id=1, source_target_pairs={{0,16},{4,20},{8,24},{12,28},{16,0},{20,4},{24,8},{28,12},{1,17},{... | collective-permute-start | bytes 393224 | tf_op jit(solution)/shard_map/ppermute | solution.py:34
  26.3 1.6 %collective-permute-start.10 = (bf16[64,1024]{1,0:T(8,128)(2,1)}, bf16[64,1024]{1,0:T(8,128)(2,1)S(1)}, u32[]{:S(2)}, u32[]{:S(2)}) collective-permute-start(bf16[64,1024]{1,0:T(8,128)(2,1)} %collective-permute-done.9.last), channel_id=1, source_target_pairs={{0,4},{4,0},{8,12},{12,8},{16,20},{20,16},{24,28},{28,24},{1,5},{5... | collective-permute-start | bytes 393224 | tf_op jit(solution)/shard_map/ppermute | solution.py:34
  28.2 6.4 %collective-permute-start.12 = (bf16[128,1024]{1,0:T(8,128)(2,1)S(1)}, bf16[128,1024]{1,0:T(8,128)(2,1)S(1)}, u32[]{:S(2)}, u32[]{:S(2)}) collective-permute-start(bf16[128,1024]{1,0:T(8,128)(2,1)S(1)} %project.3), channel_id=1, source_target_pairs={{0,8},{4,20},{8,0},{12,28},{16,24},{20,4},{24,16},{28,12},{1,9},{5... | collective-permute-start | bytes 786440 | tf_op jit(solution)/shard_map/ppermute | solution.py:457
  31.3 4.9 %copy-start = (f32[64,1024]{1,0:T(8,128)S(1)}, f32[64,1024]{1,0:T(8,128)}, u32[]{:S(2)}) copy-start(f32[64,1024]{1,0:T(8,128)} %refs_0_.1) | copy-start | bytes 786436
  31.4 4.9 %copy-start.1 = (f32[64,1024]{1,0:T(8,128)S(1)}, f32[64,1024]{1,0:T(8,128)}, u32[]{:S(2)}) copy-start(f32[64,1024]{1,0:T(8,128)} %refs_1_.1) | copy-start | bytes 786436
  31.4 4.8 %copy-start.2 = (f32[64,1024]{1,0:T(8,128)S(1)}, f32[64,1024]{1,0:T(8,128)}, u32[]{:S(2)}) copy-start(f32[64,1024]{1,0:T(8,128)} %refs_2_.1) | copy-start | bytes 786436
  31.4 4.8 %copy-start.3 = (f32[64,1024]{1,0:T(8,128)S(1)}, f32[64,1024]{1,0:T(8,128)}, u32[]{:S(2)}) copy-start(f32[64,1024]{1,0:T(8,128)} %refs_3_.1) | copy-start | bytes 786436
  32.1 8.3 %collective-permute-start.11 = (bf16[128,1024]{1,0:T(8,128)(2,1)S(1)}, bf16[128,1024]{1,0:T(8,128)(2,1)S(1)}, u32[]{:S(2)}, u32[]{:S(2)}) collective-permute-start(bf16[128,1024]{1,0:T(8,128)(2,1)S(1)} %get-tuple-element.59), channel_id=1, source_target_pairs={{0,8},{4,20},{8,0},{12,28},{16,24},{20,4},{24,16},{28,12},{1,9},{5... | collective-permute-start | bytes 786440 | tf_op jit(solution)/shard_map/ppermute | solution.py:457
  34.7 6.4 %collective-permute-start.13 = (bf16[128,1024]{1,0:T(8,128)(2,1)S(1)}, bf16[128,1024]{1,0:T(8,128)(2,1)S(1)}, u32[]{:S(2)}, u32[]{:S(2)}) collective-permute-start(bf16[128,1024]{1,0:T(8,128)(2,1)S(1)} %add.64), channel_id=1, source_target_pairs={{0,16},{4,12},{8,24},{12,4},{16,0},{20,28},{24,8},{28,20},{1,17},{... | collective-permute-start | bytes 786440 | tf_op jit(solution)/shard_map/ppermute | solution.py:457

commit v9 on v8

--- a/solution.py
+++ b/solution.py
@@ -202,6 +202,22 @@
     )(index, *pieces)
 
 
+def hold_kernel(source, target):
+    target[...] = source[...]
+
+
+def hold(array):
+    return pl.pallas_call(
+        hold_kernel,
+        out_shape=like(array.shape, array),
+        in_specs=[VMEM],
+        out_specs=VMEM,
+        compiler_params=PARAMS,
+        cost_estimate=cost(4 * array.size, 3 * 10**10),
+        name="hold",
+    )(array)
+
+
 def places(chips, rows, pieces, width):
     tokens = [slice(index * rows, (index + 1) * rows) for index in range(2 * chips)]
     down, out_features = pieces.shape
@@ -262,7 +278,7 @@
         in_specs=[SMEM] + [VMEM] * 3,
         out_specs=VMEM,
         compiler_params=PARAMS,
-        cost_estimate=cost(4 * math.prod(shape)),
+        cost_estimate=cost(0),
         name="collect",
     )(index, own, last, other)
 
@@ -364,17 +380,13 @@
         out_specs=VMEM,
         scratch_shapes=[pltpu.VMEM((total, width), own.dtype)] * 2,
         compiler_params=PARAMS,
-        cost_estimate=cost(
-            4 * length * width + 4 * total * width,
-            4 * total * length * width,
-            total * length * (width // HEAD_DIM),
-        ),
+        cost_estimate=cost(0, 10**10 * (len(distances) - 1)),
         name="attend",
     )(me, *parts, own, other)
 
 
-def project_kernel(chips, me_ref, index_ref, attended, weights, last, *refs):
-    outs, other = refs[:-1], refs[-1]
+def project_kernel(chips, held, me_ref, index_ref, attended, weights, last, *refs):
+    outs, other = refs[held:-1], refs[-1]
     down = last.shape[0]
     core = me_ref[0] % 2
     other[...] = weights[1]
@@ -415,22 +427,19 @@
     return [d for d in range(1, chips - 1) if d not in (late(chips, 0), late(chips, 1))]
 
 
-def project(me, index, attended, weights, last, chips, kinds):
+def project(me, index, attended, weights, last, chips, kinds, held=()):
     _, total, features = attended.shape
     width = weights.shape[2]
     return pl.pallas_call(
-        functools.partial(project_kernel, chips),
+        functools.partial(project_kernel, chips, len(held)),
         out_shape=[jax.ShapeDtypeStruct((total // len(kinds), width), kind) for kind in kinds],
-        in_specs=[SMEM] * 2 + [VMEM] * 3,
+        in_specs=[SMEM] * 2 + [VMEM] * (3 + len(held)),
         out_specs=[VMEM] * len(kinds),
         scratch_shapes=[pltpu.VMEM(weights.shape[1:], weights.dtype)],
         compiler_params=PARAMS,
-        cost_estimate=cost(
-            4 * total * features + 6 * features * width + 4 * total * width,
-            4 * total * features * width,
-        ),
+        cost_estimate=cost(0),
         name="project",
-    )(me, index, attended, weights, last)
+    )(me, index, attended, weights, last, *held)
 
 
 def add_kernel(product, passed, out):
@@ -490,19 +499,18 @@
         pieces = [weight] + [swap(weight, "dp", dp_count, span * d) for d in (1, 2)]
         queries, _ = lax.optimization_barrier((queries, weight))
         sent_queries = pack_queries(me, queries, chips)
-        pairs, sent_queries = lax.optimization_barrier((pairs, sent_queries))
+        pieces[2], sent_queries = lax.optimization_barrier((pieces[2], sent_queries))
         own = stack(pairs, pieces)
-        forwarded = swap(pieces[2], "dp", dp_count, span)
+        forwarded = hold(swap(pieces[2], "dp", dp_count, span))
 
         other = swap(own, "seq", seq_count, 1)
         sent_queries, _ = lax.optimization_barrier((sent_queries, own))
+        near_parts, forwarded = lax.optimization_barrier((sent_queries[:-1], forwarded))
+        sent_queries = [*near_parts, sent_queries[-1]]
         own_queries = exchange([own_queries, *sent_queries])
 
         attended = attend(me, (far,), own_queries[far:], own, other, chips)
-        attended, forwarded = lax.optimization_barrier((attended, forwarded))
-        near_queries, others = lax.optimization_barrier(
-            (own_queries[:far], swap(forwarded, "seq", seq_count, 1))
-        )
+        near_queries, others = own_queries[:far], swap(forwarded, "seq", seq_count, 1)
         index = (place // span % 4).reshape(1)
         weights = collect(index, chips, rows, own, forwarded, other)
         (product,) = project(me, index, attended, weights, others, chips, [attended.dtype])
@@ -510,7 +518,7 @@
         attended = attend(me, tuple(range(far)), near_queries, own, other, chips)
         kinds = [attended.dtype, jnp.float32, jnp.float32] + [attended.dtype] * (chips - 4)
         sent, waiting, projected, *rest = project(
-            me, index, attended, weights, others, chips, kinds
+            me, index, attended, weights, others, chips, kinds, near_queries
         )
         got = [by_core(sent, functools.partial(early, chips))]
         got += [to_chip(product, d) for d, product in zip(straight(chips), rest)]

time: 42.1 us -> 41.3 us (0.981)
  waiting for transfers between devices: 12.3 us -> 10.7 us
  starting transfers between devices: 18 us -> 18.8 us
    ppermute x11, waiting for transfers between devices: 6.34 us -> 4.48 us  [swap(): return lax.ppermute(array, axis, [(i, i ^ distance) for i in range(count)])]
    ppermute x11, starting transfers between devices: 14.3 us -> 15.5 us  [swap(): return lax.ppermute(array, axis, [(i, i ^ distance) for i in range(count)])]
    pallas_call x2, Pallas kernels: 2.34 us -> 3.25 us  [attend(): pl.pallas_call(functools.partial(attend_kernel, distances, chips), out_sh...]
    pallas_call x1, Pallas kernels: 0.97 us -> 0.07 us  [collect(): pl.pallas_call(functools.partial(collect_kernel, chips, rows), out_shape=...]
    ppermute x3, starting transfers between devices: 3.71 us -> 3.27 us  [by_core(): lax.ppermute(part, 'seq', [(i, i ^ 2 * distance(i % 2)) for i in range(se...]
    pallas_call x2 -> x3, Pallas kernels: 1.04 us -> 1.04 us  [the longest x2 1.03 us: project(): pl.pallas_call(functools.partial(project_kernel, chips, len(held)), out_s...]
  transfers between devices with their start and end apart: 14 -> 14, of which waited for: 9 -> 8; matrix products, arithmetic and copies ran while one was open for 2% -> 2% of each run, Pallas kernels for 18% -> 20%
where the time goes in v9:
time: 41.3 us; the launch traced here: 41.1 us
  starting transfers between devices  18.8 us (46%)
  waiting for transfers between devices  10.7 us (26%)
  Pallas kernels  9.09 us (22%)
  other arithmetic  1.75 us (4%)
  between operations  0.79 us (2%)
    ppermute x11, starting transfers between devices, swap(): return lax.ppermute(array, axis, [(i, i ^ distance) for i in range(count)])  15.5 us
    ppermute x3, waiting for transfers between devices, by_core(): lax.ppermute(part, 'seq', [(i, i ^ 2 * distance(i % 2)) for i in range(se...  6.2 us
    ppermute x11, waiting for transfers between devices, swap(): return lax.ppermute(array, axis, [(i, i ^ distance) for i in range(count)])  4.48 us
    ppermute x3, starting transfers between devices, by_core(): lax.ppermute(part, 'seq', [(i, i ^ 2 * distance(i % 2)) for i in range(se...  3.27 us
    pallas_call x2, Pallas kernels, attend(): pl.pallas_call(functools.partial(attend_kernel, distances, chips), out_sh...  3.25 us
    pallas_call x1, Pallas kernels, pack_queries(): pl.pallas_call(pack_queries_kernel, out_shape=[like((rows, width), querie...  1.79 us
    pallas_call x1, Pallas kernels, pack(): pl.pallas_call(functools.partial(pack_kernel, far), out_shape=[like((2, r...  1.79 us
    pallas_call x2, Pallas kernels, project(): pl.pallas_call(functools.partial(project_kernel, chips, len(held)), out_s...  1.03 us
  transfers between devices with their start and end apart: 14, of which 8 were waited for; matrix products, arithmetic and copies ran while one was open for 2% of the time, Pallas kernels for 20%

profile of v9, /device:TPU:0, one launch (start us, length us, event | category | flops | bytes accessed | tf_op | source)
XLA Modules:
  0.0 41.1 jit_solution(6701499460620358130)
XLA Ops:
  0.6 1.0 %pack_far.1 = bf16[2,128,512]{2,1,0:T(8,128)(2,1)S(1)} custom-call(s32[1]{0:T(128)} %bitcast.me_ref, bf16[1,128,2048]{2,1,0:T(8,128)(2,1)} %keys.2, bf16[1,128,2048]{2,1,0:T(8,128)(2,1)} %values.3), custom_call_target="tpu_custom_call" | custom-call | bytes 524288 | tf_op jit(solution)/shard_map/pack_far/pallas_call | solution.py:88
  1.6 4.0 %collective-permute-start.3 = (bf16[2,128,512]{2,1,0:T(8,128)(2,1)S(1)}, bf16[2,128,512]{2,1,0:T(8,128)(2,1)S(1)}, u32[]{:S(2)}, u32[]{:S(2)}) collective-permute-start(bf16[2,128,512]{2,1,0:T(8,128)(2,1)S(1)} %pack_far.1), channel_id=1, source_target_pairs={{0,24},{4,28},{8,16},{12,20},{16,8},{20,12},{24,0},{28,4},{1,25},{... | collective-permute-start | bytes 786440 | tf_op jit(solution)/shard_map/ppermute | solution.py:34
  5.6 1.8 %pack.1 = (bf16[2,128,512]{2,1,0:T(8,128)(2,1)S(1)}, bf16[2,128,512]{2,1,0:T(8,128)(2,1)S(1)}, bf16[2,128,512]{2,1,0:T(8,128)(2,1)S(1)}, bf16[128,512]{1,0:T(8,128)(2,1)S(1)}, bf16[64,1024]{1,0:T(8,128)(2,1)S(1)}) custom-call(s32[1]{0:T(128)} %bitcast.me_ref, bf16[1,128,2048]{2,1,0:T(8,128)(2,1)} %keys.2, bf16[1,128,2048]{2,1,0:T(8,128)(2,1)} %values.3, ...), custom_call_target="tpu_custom_call" | custom-call | bytes 3276800 | tf_op jit(solution)/shard_map/pack/pallas_call | solution.py:139
  7.4 0.6 %collective-permute-start.1 = (bf16[2,128,512]{2,1,0:T(8,128)(2,1)S(1)}, bf16[2,128,512]{2,1,0:T(8,128)(2,1)S(1)}, u32[]{:S(2)}, u32[]{:S(2)}) collective-permute-start(bf16[2,128,512]{2,1,0:T(8,128)(2,1)S(1)} %get-tuple-element.37), channel_id=1, source_target_pairs={{0,8},{4,12},{8,0},{12,4},{16,24},{20,28},{24,16},{28,20},{1,9},{5... | collective-permute-start | bytes 786440 | tf_op jit(solution)/shard_map/ppermute | solution.py:34
  8.0 0.1 collective-permute-start.2
  8.0 3.0 %collective-permute-start = (bf16[64,1024]{1,0:T(8,128)(2,1)S(1)}, bf16[64,1024]{1,0:T(8,128)(2,1)S(1)}, u32[]{:S(2)}, u32[]{:S(2)}) collective-permute-start(bf16[64,1024]{1,0:T(8,128)(2,1)S(1)} %get-tuple-element.28.refs_4_), channel_id=1, source_target_pairs={{0,2},{1,3},{2,0},{3,1},{4,6},{5,7},{6,4},{7,5},{8,10},{9,11},{10,... | collective-permute-start | bytes 393224 | tf_op jit(solution)/shard_map/ppermute | solution.py:34
  11.1 1.6 %collective-permute-start.4 = (bf16[64,1024]{1,0:T(8,128)(2,1)S(1)}, bf16[64,1024]{1,0:T(8,128)(2,1)S(1)}, u32[]{:S(2)}, u32[]{:S(2)}) collective-permute-start(bf16[64,1024]{1,0:T(8,128)(2,1)S(1)} %get-tuple-element.28.refs_4_), channel_id=1, source_target_pairs={{0,1},{1,0},{2,3},{3,2},{4,5},{5,4},{6,7},{7,6},{8,9},{9,8},{10,11... | collective-permute-start | bytes 393224 | tf_op jit(solution)/shard_map/ppermute | solution.py:34
  12.7 1.8 %pack_queries.1 = (bf16[128,512]{1,0:T(8,128)(2,1)}, bf16[128,512]{1,0:T(8,128)(2,1)}, bf16[128,512]{1,0:T(8,128)(2,1)}) custom-call(s32[1]{0:T(128)} %bitcast.me_ref, bf16[1,128,2048]{2,1,0:T(8,128)(2,1)} %queries.2), custom_call_target="tpu_custom_call" | custom-call | bytes 1048576 | tf_op jit(solution)/shard_map/pack_queries/pallas_call | solution.py:175
  14.5 2.2 %collective-permute-done.refs_6_ = bf16[64,1024]{1,0:T(8,128)(2,1)S(1)} collective-permute-done((bf16[64,1024]{1,0:T(8,128)(2,1)S(1)}, bf16[64,1024]{1,0:T(8,128)(2,1)S(1)}, u32[]{:S(2)}, u32[]{:S(2)}) %collective-permute-start) | collective-permute-done | bytes 131104 | tf_op jit(solution)/shard_map/ppermute | solution.py:34
  16.7 0.6 %collective-permute-start.5 = (bf16[64,1024]{1,0:T(8,128)(2,1)S(1)}, bf16[64,1024]{1,0:T(8,128)(2,1)S(1)}, u32[]{:S(2)}, u32[]{:S(2)}) collective-permute-start(bf16[64,1024]{1,0:T(8,128)(2,1)S(1)} %collective-permute-done.refs_6_), channel_id=1, source_target_pairs={{0,1},{1,0},{2,3},{3,2},{4,5},{5,4},{6,7},{7,6},{8,9},{9,8},{10,11... | collective-permute-start | bytes 393224 | tf_op jit(solution)/shard_map/ppermute | solution.py:34
  17.3 0.0 collective-permute-done.3.refs_3_
  17.3 0.0 collective-permute-done.4.refs_5_
  17.3 0.5 %collective-permute-done.1.refs_1_ = bf16[2,128,512]{2,1,0:T(8,128)(2,1)S(1)} collective-permute-done((bf16[2,128,512]{2,1,0:T(8,128)(2,1)S(1)}, bf16[2,128,512]{2,1,0:T(8,128)(2,1)S(1)}, u32[]{:S(2)}, u32[]{:S(2)}) %collective-permute-start.1) | collective-permute-done | bytes 262176 | tf_op jit(solution)/shard_map/ppermute | solution.py:34
  17.8 0.0 collective-permute-done.2.refs_2_
  17.8 0.1 stack.1.refs_3_.own.refs_1_
  17.9 0.1 collective-permute-start.8
  18.0 2.4 %collective-permute-start.11 = (bf16[128,512]{1,0:T(8,128)(2,1)}, bf16[128,512]{1,0:T(8,128)(2,1)}, u32[]{:S(2)}, u32[]{:S(2)}) collective-permute-start(bf16[128,512]{1,0:T(8,128)(2,1)} %get-tuple-element.49), channel_id=1, source_target_pairs={{0,24},{4,28},{8,16},{12,20},{16,8},{20,12},{24,0},{28,4},{1,25},{... | collective-permute-start | bytes 393224 | tf_op jit(solution)/shard_map/ppermute | solution.py:34
  20.4 1.2 %collective-permute-done.5.source = bf16[64,1024]{1,0:T(8,128)(2,1)S(1)} collective-permute-done((bf16[64,1024]{1,0:T(8,128)(2,1)S(1)}, bf16[64,1024]{1,0:T(8,128)(2,1)S(1)}, u32[]{:S(2)}, u32[]{:S(2)}) %collective-permute-start.5) | collective-permute-done | bytes 131104 | tf_op jit(solution)/shard_map/ppermute | solution.py:34
  21.6 0.1 collective-permute-start.9
  21.7 1.6 %collective-permute-start.6 = (bf16[128,512]{1,0:T(8,128)(2,1)}, bf16[128,512]{1,0:T(8,128)(2,1)S(1)}, u32[]{:S(2)}, u32[]{:S(2)}) collective-permute-start(bf16[128,512]{1,0:T(8,128)(2,1)} %get-tuple-element.43), channel_id=1, source_target_pairs={{0,8},{4,12},{8,0},{12,4},{16,24},{20,28},{24,16},{28,20},{1,9},{5... | collective-permute-start | bytes 393224 | tf_op jit(solution)/shard_map/ppermute | solution.py:34
  23.3 1.5 %collective-permute-start.7 = (bf16[128,512]{1,0:T(8,128)(2,1)}, bf16[128,512]{1,0:T(8,128)(2,1)S(1)}, u32[]{:S(2)}, u32[]{:S(2)}) collective-permute-start(bf16[128,512]{1,0:T(8,128)(2,1)} %get-tuple-element.44), channel_id=1, source_target_pairs={{0,16},{4,20},{8,24},{12,28},{16,0},{20,4},{24,8},{28,12},{1,17},{... | collective-permute-start | bytes 393224 | tf_op jit(solution)/shard_map/ppermute | solution.py:34
  24.8 0.3 collective-permute-done.11.refs_0_
  25.1 0.0 collective-permute-done.8.refs_4_.other.refs_2_
  25.1 1.8 %attend.3.attended = bf16[2,128,256]{2,1,0:T(8,128)(2,1)S(1)} custom-call(s32[1]{0:T(128)} %bitcast.me_ref, bf16[128,512]{1,0:T(8,128)(2,1)} %collective-permute-done.11.refs_0_, bf16[1408,512]{1,0:T(8,128)(2,1)S(1)} %stack.1.refs_3_.own.refs_1_, bf16[1408,512]{1,0:T(8,128)(2,1)S(1)} %collective-permute-done.8.refs_4_.other.refs_2_), custom_call_target="tpu_custom_call" | custom-call | tf_op jit(solution)/shard_map/attend/pallas_call | solution.py:376
  27.0 0.1 collect.1.weights
  27.0 0.0 collective-permute-done.9.last
  27.0 0.4 project.3
  27.4 1.5 %collective-permute-start.12 = (bf16[128,1024]{1,0:T(8,128)(2,1)S(1)}, bf16[128,1024]{1,0:T(8,128)(2,1)S(1)}, u32[]{:S(2)}, u32[]{:S(2)}) collective-permute-start(bf16[128,1024]{1,0:T(8,128)(2,1)S(1)} %project.3), channel_id=1, source_target_pairs={{0,8},{4,20},{8,0},{12,28},{16,24},{20,4},{24,16},{28,12},{1,9},{5... | collective-permute-start | bytes 786440 | tf_op jit(solution)/shard_map/ppermute | solution.py:466
  28.9 0.0 collective-permute-done.6.refs_1_
  28.9 0.2 collective-permute-done.7.refs_2_
  29.1 1.4 %attend.2.attended = bf16[2,384,256]{2,1,0:T(8,128)(2,1)S(1)} custom-call(s32[1]{0:T(128)} %bitcast.me_ref, bf16[128,512]{1,0:T(8,128)(2,1)S(1)} %get-tuple-element.27.refs_0_, bf16[128,512]{1,0:T(8,128)(2,1)S(1)} %collective-permute-done.6.refs_1_, bf16[128,512]{1,0:T(8,128)(2,1)S(1)} %collective-permute-done.7.refs_2_, ...), custom_call_target="tpu_custom_call" | custom-call | flops 20000000000 | tf_op jit(solution)/shard_map/attend/pallas_call | solution.py:376
  30.6 0.0 copy-start
  30.6 0.0 copy-start.1
  30.6 0.0 copy-start.2
  30.6 0.0 copy-start.3
  30.6 0.7 %project.2 = (bf16[128,1024]{1,0:T(8,128)(2,1)S(1)}, f32[128,1024]{1,0:T(8,128)S(1)}, f32[128,1024]{1,0:T(8,128)S(1)}) custom-call(s32[1]{0:T(128)} %bitcast.me_ref, s32[1]{0:T(128)} %bitcast.1.index_ref, bf16[2,384,256]{2,1,0:T(8,128)(2,1)S(1)} %attend.2.attended, bf16[2,256,1024]{2,1,0:T(8,128)(2,1)S(1)} %collect.1.weights, ...), custom_call_target="tpu_custom_call" | custom-call | tf_op jit(solution)/shard_map/project/pallas_call | solution.py:433
  31.3 0.6 %collective-permute-start.10 = (bf16[128,1024]{1,0:T(8,128)(2,1)S(1)}, bf16[128,1024]{1,0:T(8,128)(2,1)S(1)}, u32[]{:S(2)}, u32[]{:S(2)}) collective-permute-start(bf16[128,1024]{1,0:T(8,128)(2,1)S(1)} %get-tuple-element.47), channel_id=1, source_target_pairs={{0,8},{4,20},{8,0},{12,28},{16,24},{20,4},{24,16},{28,12},{1,9},{5... | collective-permute-start | bytes 786440 | tf_op jit(solution)/shard_map/ppermute | solution.py:466
  31.9 1.9 %collective-permute-done.12.passed = bf16[128,1024]{1,0:T(8,128)(2,1)S(1)} collective-permute-done((bf16[128,1024]{1,0:T(8,128)(2,1)S(1)}, bf16[128,1024]{1,0:T(8,128)(2,1)S(1)}, u32[]{:S(2)}, u32[]{:S(2)}) %collective-permute-start.12) | collective-permute-done | bytes 262176 | tf_op jit(solution)/shard_map/ppermute | solution.py:466
  33.8 0.1 add.64
  33.9 1.2 %collective-permute-start.13 = (bf16[128,1024]{1,0:T(8,128)(2,1)S(1)}, bf16[128,1024]{1,0:T(8,128)(2,1)S(1)}, u32[]{:S(2)}, u32[]{:S(2)}) collective-permute-start(bf16[128,1024]{1,0:T(8,128)(2,1)S(1)} %add.64), channel_id=1, source_target_pairs={{0,16},{4,12},{8,24},{12,4},{16,0},{20,28},{24,8},{28,20},{1,17},{... | collective-permute-start | bytes 786440 | tf_op jit(solution)/shard_map/ppermute | solution.py:466
  35.1 0.0 copy-done
  35.1 0.0 copy-done.1
  35.1 0.0 copy-done.2
  35.1 0.9 %multiply_subtract_fusion = f32[64,1024]{1,0:T(8,128)} fusion(f32[64,1024]{1,0:T(8,128)S(1)} %copy-done, f32[64,1024]{1,0:T(8,128)S(1)} %copy-done.3, f32[64,1024]{1,0:T(8,128)S(1)} %copy-done.2, f32[64,1024]{1,0:T(8,128)S(1)} %copy-done.1), kind=kLoop, calls=%fused_computation.10 | loop fusion | flops 983040 | bytes 1310720 | tf_op jit(solution)/shard_map/sub | solution.py:28
  36.0 4.1 %collective-permute-done.10 = bf16[128,1024]{1,0:T(8,128)(2,1)S(1)} collective-permute-done((bf16[128,1024]{1,0:T(8,128)(2,1)S(1)}, bf16[128,1024]{1,0:T(8,128)(2,1)S(1)}, u32[]{:S(2)}, u32[]{:S(2)}) %collective-permute-start.10) | collective-permute-done | bytes 262176 | tf_op jit(solution)/shard_map/ppermute | solution.py:466
  40.1 0.1 convert_add_fusion
  40.2 0.1 collective-permute-done.13
  40.3 0.8 %fusion.6 = bf16[1,128,1024]{2,1,0:T(8,128)(2,1)} fusion(f32[128,1024]{1,0:T(8,128)S(1)} %convert_add_fusion, bf16[128,1024]{1,0:T(8,128)(2,1)S(1)} %collective-permute-done.13), kind=kLoop, calls=%fused_computation.9 | loop fusion | flops 393216 | bytes 1048576 | tf_op jit(solution)/shard_map/broadcast_in_dim | solution.py:530
  (2 shorter events, 0.0 us)
Async XLA Ops:
  1.6 15.6 %collective-permute-start.3 = (bf16[2,128,512]{2,1,0:T(8,128)(2,1)S(1)}, bf16[2,128,512]{2,1,0:T(8,128)(2,1)S(1)}, u32[]{:S(2)}, u32[]{:S(2)}) collective-permute-start(bf16[2,128,512]{2,1,0:T(8,128)(2,1)S(1)} %pack_far.1), channel_id=1, source_target_pairs={{0,24},{4,28},{8,16},{12,20},{16,8},{20,12},{24,0},{28,4},{1,25},{... | collective-permute-start | bytes 786440 | tf_op jit(solution)/shard_map/ppermute | solution.py:34
  7.4 10.4 %collective-permute-start.1 = (bf16[2,128,512]{2,1,0:T(8,128)(2,1)S(1)}, bf16[2,128,512]{2,1,0:T(8,128)(2,1)S(1)}, u32[]{:S(2)}, u32[]{:S(2)}) collective-permute-start(bf16[2,128,512]{2,1,0:T(8,128)(2,1)S(1)} %get-tuple-element.37), channel_id=1, source_target_pairs={{0,8},{4,12},{8,0},{12,4},{16,24},{20,28},{24,16},{28,20},{1,9},{5... | collective-permute-start | bytes 786440 | tf_op jit(solution)/shard_map/ppermute | solution.py:34
  8.0 9.8 %collective-permute-start.2 = (bf16[2,128,512]{2,1,0:T(8,128)(2,1)S(1)}, bf16[2,128,512]{2,1,0:T(8,128)(2,1)S(1)}, u32[]{:S(2)}, u32[]{:S(2)}) collective-permute-start(bf16[2,128,512]{2,1,0:T(8,128)(2,1)S(1)} %get-tuple-element.38), channel_id=1, source_target_pairs={{0,16},{4,20},{8,24},{12,28},{16,0},{20,4},{24,8},{28,12},{1,17},{... | collective-permute-start | bytes 786440 | tf_op jit(solution)/shard_map/ppermute | solution.py:34
  8.0 8.6 %collective-permute-start = (bf16[64,1024]{1,0:T(8,128)(2,1)S(1)}, bf16[64,1024]{1,0:T(8,128)(2,1)S(1)}, u32[]{:S(2)}, u32[]{:S(2)}) collective-permute-start(bf16[64,1024]{1,0:T(8,128)(2,1)S(1)} %get-tuple-element.28.refs_4_), channel_id=1, source_target_pairs={{0,2},{1,3},{2,0},{3,1},{4,6},{5,7},{6,4},{7,5},{8,10},{9,11},{10,... | collective-permute-start | bytes 393224 | tf_op jit(solution)/shard_map/ppermute | solution.py:34
  11.1 6.2 %collective-permute-start.4 = (bf16[64,1024]{1,0:T(8,128)(2,1)S(1)}, bf16[64,1024]{1,0:T(8,128)(2,1)S(1)}, u32[]{:S(2)}, u32[]{:S(2)}) collective-permute-start(bf16[64,1024]{1,0:T(8,128)(2,1)S(1)} %get-tuple-element.28.refs_4_), channel_id=1, source_target_pairs={{0,1},{1,0},{2,3},{3,2},{4,5},{5,4},{6,7},{7,6},{8,9},{9,8},{10,11... | collective-permute-start | bytes 393224 | tf_op jit(solution)/shard_map/ppermute | solution.py:34
  16.7 5.0 %collective-permute-start.5 = (bf16[64,1024]{1,0:T(8,128)(2,1)S(1)}, bf16[64,1024]{1,0:T(8,128)(2,1)S(1)}, u32[]{:S(2)}, u32[]{:S(2)}) collective-permute-start(bf16[64,1024]{1,0:T(8,128)(2,1)S(1)} %collective-permute-done.refs_6_), channel_id=1, source_target_pairs={{0,1},{1,0},{2,3},{3,2},{4,5},{5,4},{6,7},{7,6},{8,9},{9,8},{10,11... | collective-permute-start | bytes 393224 | tf_op jit(solution)/shard_map/ppermute | solution.py:34
  17.9 7.2 %collective-permute-start.8 = (bf16[1408,512]{1,0:T(8,128)(2,1)S(1)}, bf16[1408,512]{1,0:T(8,128)(2,1)S(1)}, u32[]{:S(2)}, u32[]{:S(2)}) collective-permute-start(bf16[1408,512]{1,0:T(8,128)(2,1)S(1)} %stack.1.refs_3_.own.refs_1_), channel_id=1, source_target_pairs={{0,4},{4,0},{8,12},{12,8},{16,20},{20,16},{24,28},{28,24},{1,5},{5... | collective-permute-start | bytes 4325384 | tf_op jit(solution)/shard_map/ppermute | solution.py:34
  18.0 7.1 %collective-permute-start.11 = (bf16[128,512]{1,0:T(8,128)(2,1)}, bf16[128,512]{1,0:T(8,128)(2,1)}, u32[]{:S(2)}, u32[]{:S(2)}) collective-permute-start(bf16[128,512]{1,0:T(8,128)(2,1)} %get-tuple-element.49), channel_id=1, source_target_pairs={{0,24},{4,28},{8,16},{12,20},{16,8},{20,12},{24,0},{28,4},{1,25},{... | collective-permute-start | bytes 393224 | tf_op jit(solution)/shard_map/ppermute | solution.py:34
  21.6 5.4 %collective-permute-start.9 = (bf16[64,1024]{1,0:T(8,128)(2,1)S(1)}, bf16[64,1024]{1,0:T(8,128)(2,1)S(1)}, u32[]{:S(2)}, u32[]{:S(2)}) collective-permute-start(bf16[64,1024]{1,0:T(8,128)(2,1)S(1)} %hold.1.last), channel_id=1, source_target_pairs={{0,4},{4,0},{8,12},{12,8},{16,20},{20,16},{24,28},{28,24},{1,5},{5... | collective-permute-start | bytes 393224 | tf_op jit(solution)/shard_map/ppermute | solution.py:34
  21.7 7.2 %collective-permute-start.6 = (bf16[128,512]{1,0:T(8,128)(2,1)}, bf16[128,512]{1,0:T(8,128)(2,1)S(1)}, u32[]{:S(2)}, u32[]{:S(2)}) collective-permute-start(bf16[128,512]{1,0:T(8,128)(2,1)} %get-tuple-element.43), channel_id=1, source_target_pairs={{0,8},{4,12},{8,0},{12,4},{16,24},{20,28},{24,16},{28,20},{1,9},{5... | collective-permute-start | bytes 393224 | tf_op jit(solution)/shard_map/ppermute | solution.py:34
  23.3 5.8 %collective-permute-start.7 = (bf16[128,512]{1,0:T(8,128)(2,1)}, bf16[128,512]{1,0:T(8,128)(2,1)S(1)}, u32[]{:S(2)}, u32[]{:S(2)}) collective-permute-start(bf16[128,512]{1,0:T(8,128)(2,1)} %get-tuple-element.44), channel_id=1, source_target_pairs={{0,16},{4,20},{8,24},{12,28},{16,0},{20,4},{24,8},{28,12},{1,17},{... | collective-permute-start | bytes 393224 | tf_op jit(solution)/shard_map/ppermute | solution.py:34
  27.4 6.4 %collective-permute-start.12 = (bf16[128,1024]{1,0:T(8,128)(2,1)S(1)}, bf16[128,1024]{1,0:T(8,128)(2,1)S(1)}, u32[]{:S(2)}, u32[]{:S(2)}) collective-permute-start(bf16[128,1024]{1,0:T(8,128)(2,1)S(1)} %project.3), channel_id=1, source_target_pairs={{0,8},{4,20},{8,0},{12,28},{16,24},{20,4},{24,16},{28,12},{1,9},{5... | collective-permute-start | bytes 786440 | tf_op jit(solution)/shard_map/ppermute | solution.py:466
  30.6 4.5 %copy-start = (f32[64,1024]{1,0:T(8,128)S(1)}, f32[64,1024]{1,0:T(8,128)}, u32[]{:S(2)}) copy-start(f32[64,1024]{1,0:T(8,128)} %refs_0_.1) | copy-start | bytes 786436
  30.6 4.5 %copy-start.1 = (f32[64,1024]{1,0:T(8,128)S(1)}, f32[64,1024]{1,0:T(8,128)}, u32[]{:S(2)}) copy-start(f32[64,1024]{1,0:T(8,128)} %refs_1_.1) | copy-start | bytes 786436
  30.6 4.5 %copy-start.2 = (f32[64,1024]{1,0:T(8,128)S(1)}, f32[64,1024]{1,0:T(8,128)}, u32[]{:S(2)}) copy-start(f32[64,1024]{1,0:T(8,128)} %refs_2_.1) | copy-start | bytes 786436
  30.6 4.5 %copy-start.3 = (f32[64,1024]{1,0:T(8,128)S(1)}, f32[64,1024]{1,0:T(8,128)}, u32[]{:S(2)}) copy-start(f32[64,1024]{1,0:T(8,128)} %refs_3_.1) | copy-start | bytes 786436
  31.3 8.9 %collective-permute-start.10 = (bf16[128,1024]{1,0:T(8,128)(2,1)S(1)}, bf16[128,1024]{1,0:T(8,128)(2,1)S(1)}, u32[]{:S(2)}, u32[]{:S(2)}) collective-permute-start(bf16[128,1024]{1,0:T(8,128)(2,1)S(1)} %get-tuple-element.47), channel_id=1, source_target_pairs={{0,8},{4,20},{8,0},{12,28},{16,24},{20,4},{24,16},{28,12},{1,9},{5... | collective-permute-start | bytes 786440 | tf_op jit(solution)/shard_map/ppermute | solution.py:466
  33.9 6.4 %collective-permute-start.13 = (bf16[128,1024]{1,0:T(8,128)(2,1)S(1)}, bf16[128,1024]{1,0:T(8,128)(2,1)S(1)}, u32[]{:S(2)}, u32[]{:S(2)}) collective-permute-start(bf16[128,1024]{1,0:T(8,128)(2,1)S(1)} %add.64), channel_id=1, source_target_pairs={{0,16},{4,12},{8,24},{12,4},{16,0},{20,28},{24,8},{28,20},{1,17},{... | collective-permute-start | bytes 786440 | tf_op jit(solution)/shard_map/ppermute | solution.py:466

commit v10 on v9

--- a/solution.py
+++ b/solution.py
@@ -513,7 +513,9 @@
         near_queries, others = own_queries[:far], swap(forwarded, "seq", seq_count, 1)
         index = (place // span % 4).reshape(1)
         weights = collect(index, chips, rows, own, forwarded, other)
-        (product,) = project(me, index, attended, weights, others, chips, [attended.dtype])
+        (product,) = project(
+            me, index, attended, weights, others, chips, [attended.dtype], own_queries[far:]
+        )
         passed = by_core(product, via)
         attended = attend(me, tuple(range(far)), near_queries, own, other, chips)
         kinds = [attended.dtype, jnp.float32, jnp.float32] + [attended.dtype] * (chips - 4)

time: 41.3 us -> 41.8 us (1.012)
  starting transfers between devices: 18.8 us -> 18 us
  Pallas kernels: 9.09 us -> 9.76 us
  waiting for transfers between devices: 10.7 us -> 11.3 us
    pallas_call x1, Pallas kernels: 0.07 us -> 0.98 us  [collect(): pl.pallas_call(functools.partial(collect_kernel, chips, rows), out_shape=...]
    pallas_call x2, Pallas kernels: 3.25 us -> 2.36 us  [attend(): pl.pallas_call(functools.partial(attend_kernel, distances, chips), out_sh...]
    ppermute x3, starting transfers between devices: 3.27 us -> 2.56 us  [by_core(): lax.ppermute(part, 'seq', [(i, i ^ 2 * distance(i % 2)) for i in range(se...]
    pallas_call x1, Pallas kernels: 0.01 us -> 0.67 us  [hold(): pl.pallas_call(hold_kernel, out_shape=like(array.shape, array), in_specs=...]
  transfers between devices with their start and end apart: 14 -> 14, of which waited for: 8 -> 6; matrix products, arithmetic and copies ran while one was open for 2% -> 2% of each run, Pallas kernels for 20% -> 21%
where the time goes in v10:
time: 41.8 us; the launch traced here: 41.6 us
  starting transfers between devices  18 us (43%)
  waiting for transfers between devices  11.3 us (27%)
  Pallas kernels  9.76 us (23%)
  other arithmetic  1.73 us (4%)
  between operations  0.78 us (2%)
    ppermute x11, starting transfers between devices, swap(): return lax.ppermute(array, axis, [(i, i ^ distance) for i in range(count)])  15.4 us
    ppermute x3, waiting for transfers between devices, by_core(): lax.ppermute(part, 'seq', [(i, i ^ 2 * distance(i % 2)) for i in range(se...  6.46 us
    ppermute x11, waiting for transfers between devices, swap(): return lax.ppermute(array, axis, [(i, i ^ distance) for i in range(count)])  4.89 us
    ppermute x3, starting transfers between devices, by_core(): lax.ppermute(part, 'seq', [(i, i ^ 2 * distance(i % 2)) for i in range(se...  2.56 us
    pallas_call x2, Pallas kernels, attend(): pl.pallas_call(functools.partial(attend_kernel, distances, chips), out_sh...  2.36 us
    pallas_call x1, Pallas kernels, pack_queries(): pl.pallas_call(pack_queries_kernel, out_shape=[like((rows, width), querie...  1.79 us
    pallas_call x1, Pallas kernels, pack(): pl.pallas_call(functools.partial(pack_kernel, far), out_shape=[like((2, r...  1.79 us
    pallas_call x2, Pallas kernels, project(): pl.pallas_call(functools.partial(project_kernel, chips, len(held)), out_s...  1.03 us
  transfers between devices with their start and end apart: 14, of which 6 were waited for; matrix products, arithmetic and copies ran while one was open for 2% of the time, Pallas kernels for 21%

profile of v10, /device:TPU:0, one launch (start us, length us, event | category | flops | bytes accessed | tf_op | source)
XLA Modules:
  0.0 41.6 jit_solution(7926266301791511938)
XLA Ops:
  0.6 1.0 %pack_far.1 = bf16[2,128,512]{2,1,0:T(8,128)(2,1)S(1)} custom-call(s32[1]{0:T(128)} %bitcast.me_ref, bf16[1,128,2048]{2,1,0:T(8,128)(2,1)} %keys.2, bf16[1,128,2048]{2,1,0:T(8,128)(2,1)} %values.3), custom_call_target="tpu_custom_call" | custom-call | bytes 524288 | tf_op jit(solution)/shard_map/pack_far/pallas_call | solution.py:88
  1.6 4.0 %collective-permute-start.3 = (bf16[2,128,512]{2,1,0:T(8,128)(2,1)S(1)}, bf16[2,128,512]{2,1,0:T(8,128)(2,1)S(1)}, u32[]{:S(2)}, u32[]{:S(2)}) collective-permute-start(bf16[2,128,512]{2,1,0:T(8,128)(2,1)S(1)} %pack_far.1), channel_id=1, source_target_pairs={{0,24},{4,28},{8,16},{12,20},{16,8},{20,12},{24,0},{28,4},{1,25},{... | collective-permute-start | bytes 786440 | tf_op jit(solution)/shard_map/ppermute | solution.py:34
  5.6 1.8 %pack.1 = (bf16[2,128,512]{2,1,0:T(8,128)(2,1)S(1)}, bf16[2,128,512]{2,1,0:T(8,128)(2,1)S(1)}, bf16[2,128,512]{2,1,0:T(8,128)(2,1)S(1)}, bf16[128,512]{1,0:T(8,128)(2,1)S(1)}, bf16[64,1024]{1,0:T(8,128)(2,1)S(1)}) custom-call(s32[1]{0:T(128)} %bitcast.me_ref, bf16[1,128,2048]{2,1,0:T(8,128)(2,1)} %keys.2, bf16[1,128,2048]{2,1,0:T(8,128)(2,1)} %values.3, ...), custom_call_target="tpu_custom_call" | custom-call | bytes 3276800 | tf_op jit(solution)/shard_map/pack/pallas_call | solution.py:139
  7.4 0.6 %collective-permute-start.1 = (bf16[2,128,512]{2,1,0:T(8,128)(2,1)S(1)}, bf16[2,128,512]{2,1,0:T(8,128)(2,1)S(1)}, u32[]{:S(2)}, u32[]{:S(2)}) collective-permute-start(bf16[2,128,512]{2,1,0:T(8,128)(2,1)S(1)} %get-tuple-element.37), channel_id=1, source_target_pairs={{0,8},{4,12},{8,0},{12,4},{16,24},{20,28},{24,16},{28,20},{1,9},{5... | collective-permute-start | bytes 786440 | tf_op jit(solution)/shard_map/ppermute | solution.py:34
  8.0 0.1 collective-permute-start.2
  8.0 3.0 %collective-permute-start = (bf16[64,1024]{1,0:T(8,128)(2,1)S(1)}, bf16[64,1024]{1,0:T(8,128)(2,1)S(1)}, u32[]{:S(2)}, u32[]{:S(2)}) collective-permute-start(bf16[64,1024]{1,0:T(8,128)(2,1)S(1)} %get-tuple-element.28.refs_4_), channel_id=1, source_target_pairs={{0,2},{1,3},{2,0},{3,1},{4,6},{5,7},{6,4},{7,5},{8,10},{9,11},{10,... | collective-permute-start | bytes 393224 | tf_op jit(solution)/shard_map/ppermute | solution.py:34
  11.1 1.6 %collective-permute-start.4 = (bf16[64,1024]{1,0:T(8,128)(2,1)S(1)}, bf16[64,1024]{1,0:T(8,128)(2,1)S(1)}, u32[]{:S(2)}, u32[]{:S(2)}) collective-permute-start(bf16[64,1024]{1,0:T(8,128)(2,1)S(1)} %get-tuple-element.28.refs_4_), channel_id=1, source_target_pairs={{0,1},{1,0},{2,3},{3,2},{4,5},{5,4},{6,7},{7,6},{8,9},{9,8},{10,11... | collective-permute-start | bytes 393224 | tf_op jit(solution)/shard_map/ppermute | solution.py:34
  12.7 1.8 %pack_queries.1 = (bf16[128,512]{1,0:T(8,128)(2,1)}, bf16[128,512]{1,0:T(8,128)(2,1)}, bf16[128,512]{1,0:T(8,128)(2,1)}) custom-call(s32[1]{0:T(128)} %bitcast.me_ref, bf16[1,128,2048]{2,1,0:T(8,128)(2,1)} %queries.2), custom_call_target="tpu_custom_call" | custom-call | bytes 1048576 | tf_op jit(solution)/shard_map/pack_queries/pallas_call | solution.py:175
  14.5 2.2 %collective-permute-done.refs_6_ = bf16[64,1024]{1,0:T(8,128)(2,1)S(1)} collective-permute-done((bf16[64,1024]{1,0:T(8,128)(2,1)S(1)}, bf16[64,1024]{1,0:T(8,128)(2,1)S(1)}, u32[]{:S(2)}, u32[]{:S(2)}) %collective-permute-start) | collective-permute-done | bytes 131104 | tf_op jit(solution)/shard_map/ppermute | solution.py:34
  16.7 0.6 %collective-permute-start.5 = (bf16[64,1024]{1,0:T(8,128)(2,1)S(1)}, bf16[64,1024]{1,0:T(8,128)(2,1)S(1)}, u32[]{:S(2)}, u32[]{:S(2)}) collective-permute-start(bf16[64,1024]{1,0:T(8,128)(2,1)S(1)} %collective-permute-done.refs_6_), channel_id=1, source_target_pairs={{0,1},{1,0},{2,3},{3,2},{4,5},{5,4},{6,7},{7,6},{8,9},{9,8},{10,11... | collective-permute-start | bytes 393224 | tf_op jit(solution)/shard_map/ppermute | solution.py:34
  17.3 0.0 collective-permute-done.3.refs_3_
  17.3 0.0 collective-permute-done.4.refs_5_
  17.3 0.5 %collective-permute-done.1.refs_1_ = bf16[2,128,512]{2,1,0:T(8,128)(2,1)S(1)} collective-permute-done((bf16[2,128,512]{2,1,0:T(8,128)(2,1)S(1)}, bf16[2,128,512]{2,1,0:T(8,128)(2,1)S(1)}, u32[]{:S(2)}, u32[]{:S(2)}) %collective-permute-start.1) | collective-permute-done | bytes 262176 | tf_op jit(solution)/shard_map/ppermute | solution.py:34
  17.8 0.0 collective-permute-done.2.refs_2_
  17.8 0.1 stack.1.refs_3_.own.refs_1_
  17.9 0.1 collective-permute-start.8
  18.0 2.4 %collective-permute-start.11 = (bf16[128,512]{1,0:T(8,128)(2,1)}, bf16[128,512]{1,0:T(8,128)(2,1)S(1)}, u32[]{:S(2)}, u32[]{:S(2)}) collective-permute-start(bf16[128,512]{1,0:T(8,128)(2,1)} %get-tuple-element.49), channel_id=1, source_target_pairs={{0,24},{4,28},{8,16},{12,20},{16,8},{20,12},{24,0},{28,4},{1,25},{... | collective-permute-start | bytes 393224 | tf_op jit(solution)/shard_map/ppermute | solution.py:34
  20.4 1.2 %collective-permute-done.5.source = bf16[64,1024]{1,0:T(8,128)(2,1)S(1)} collective-permute-done((bf16[64,1024]{1,0:T(8,128)(2,1)S(1)}, bf16[64,1024]{1,0:T(8,128)(2,1)S(1)}, u32[]{:S(2)}, u32[]{:S(2)}) %collective-permute-start.5) | collective-permute-done | bytes 131104 | tf_op jit(solution)/shard_map/ppermute | solution.py:34
  21.6 0.7 %hold.1.last = bf16[64,1024]{1,0:T(8,128)(2,1)} custom-call(bf16[64,1024]{1,0:T(8,128)(2,1)S(1)} %collective-permute-done.5.source), custom_call_target="tpu_custom_call" | custom-call | flops 30000001024 | bytes 262144 | tf_op jit(solution)/shard_map/hold/pallas_call | solution.py:210
  22.3 0.0 collective-permute-start.9
  22.3 1.5 %collective-permute-start.6 = (bf16[128,512]{1,0:T(8,128)(2,1)}, bf16[128,512]{1,0:T(8,128)(2,1)S(1)}, u32[]{:S(2)}, u32[]{:S(2)}) collective-permute-start(bf16[128,512]{1,0:T(8,128)(2,1)} %get-tuple-element.43), channel_id=1, source_target_pairs={{0,8},{4,12},{8,0},{12,4},{16,24},{20,28},{24,16},{28,20},{1,9},{5... | collective-permute-start | bytes 393224 | tf_op jit(solution)/shard_map/ppermute | solution.py:34
  23.8 1.5 %collective-permute-start.7 = (bf16[128,512]{1,0:T(8,128)(2,1)}, bf16[128,512]{1,0:T(8,128)(2,1)S(1)}, u32[]{:S(2)}, u32[]{:S(2)}) collective-permute-start(bf16[128,512]{1,0:T(8,128)(2,1)} %get-tuple-element.44), channel_id=1, source_target_pairs={{0,16},{4,20},{8,24},{12,28},{16,0},{20,4},{24,8},{28,12},{1,17},{... | collective-permute-start | bytes 393224 | tf_op jit(solution)/shard_map/ppermute | solution.py:34
  25.4 0.0 collective-permute-done.11.refs_0_
  25.4 0.0 collective-permute-done.8.refs_4_.other.refs_2_
  25.4 0.9 %attend.3.attended = bf16[2,128,256]{2,1,0:T(8,128)(2,1)S(1)} custom-call(s32[1]{0:T(128)} %bitcast.me_ref, bf16[128,512]{1,0:T(8,128)(2,1)S(1)} %collective-permute-done.11.refs_0_, bf16[1408,512]{1,0:T(8,128)(2,1)S(1)} %stack.1.refs_3_.own.refs_1_, bf16[1408,512]{1,0:T(8,128)(2,1)S(1)} %collective-permute-done.8.refs_4_.other.refs_2_), custom_call_target="tpu_custom_call" | custom-call | tf_op jit(solution)/shard_map/attend/pallas_call | solution.py:376
  26.3 1.0 %collect.1.weights = bf16[2,256,1024]{2,1,0:T(8,128)(2,1)S(1)} custom-call(s32[1]{0:T(128)} %bitcast.1.index_ref, bf16[1408,512]{1,0:T(8,128)(2,1)S(1)} %stack.1.refs_3_.own.refs_1_, bf16[64,1024]{1,0:T(8,128)(2,1)} %hold.1.last, bf16[1408,512]{1,0:T(8,128)(2,1)S(1)} %collective-permute-done.8.refs_4_.other.refs_2_), custom_call_target="tpu_custom_call" | custom-call | tf_op jit(solution)/shard_map/collect/pallas_call | solution.py:275
  27.3 0.0 collective-permute-done.9.last
  27.3 0.4 project.3
  27.7 1.1 %collective-permute-start.12 = (bf16[128,1024]{1,0:T(8,128)(2,1)S(1)}, bf16[128,1024]{1,0:T(8,128)(2,1)S(1)}, u32[]{:S(2)}, u32[]{:S(2)}) collective-permute-start(bf16[128,1024]{1,0:T(8,128)(2,1)S(1)} %project.3), channel_id=1, source_target_pairs={{0,8},{4,20},{8,0},{12,28},{16,24},{20,4},{24,16},{28,12},{1,9},{5... | collective-permute-start | bytes 786440 | tf_op jit(solution)/shard_map/ppermute | solution.py:466
  28.8 0.0 collective-permute-done.6.refs_1_
  28.8 0.9 %collective-permute-done.7.refs_2_ = bf16[128,512]{1,0:T(8,128)(2,1)S(1)} collective-permute-done((bf16[128,512]{1,0:T(8,128)(2,1)}, bf16[128,512]{1,0:T(8,128)(2,1)S(1)}, u32[]{:S(2)}, u32[]{:S(2)}) %collective-permute-start.7) | collective-permute-done | bytes 131104 | tf_op jit(solution)/shard_map/ppermute | solution.py:34
  29.7 1.4 %attend.2.attended = bf16[2,384,256]{2,1,0:T(8,128)(2,1)S(1)} custom-call(s32[1]{0:T(128)} %bitcast.me_ref, bf16[128,512]{1,0:T(8,128)(2,1)S(1)} %get-tuple-element.27.refs_0_, bf16[128,512]{1,0:T(8,128)(2,1)S(1)} %collective-permute-done.6.refs_1_, bf16[128,512]{1,0:T(8,128)(2,1)S(1)} %collective-permute-done.7.refs_2_, ...), custom_call_target="tpu_custom_call" | custom-call | flops 20000000000 | tf_op jit(solution)/shard_map/attend/pallas_call | solution.py:376
  31.1 0.0 copy-start
  31.1 0.0 copy-start.1
  31.2 0.0 copy-start.2
  31.2 0.0 copy-start.3
  31.2 0.7 %project.2 = (bf16[128,1024]{1,0:T(8,128)(2,1)S(1)}, f32[128,1024]{1,0:T(8,128)S(1)}, f32[128,1024]{1,0:T(8,128)S(1)}) custom-call(s32[1]{0:T(128)} %bitcast.me_ref, s32[1]{0:T(128)} %bitcast.1.index_ref, bf16[2,384,256]{2,1,0:T(8,128)(2,1)S(1)} %attend.2.attended, bf16[2,256,1024]{2,1,0:T(8,128)(2,1)S(1)} %collect.1.weights, ...), custom_call_target="tpu_custom_call" | custom-call | tf_op jit(solution)/shard_map/project/pallas_call | solution.py:433
  31.9 0.6 %collective-permute-start.10 = (bf16[128,1024]{1,0:T(8,128)(2,1)S(1)}, bf16[128,1024]{1,0:T(8,128)(2,1)S(1)}, u32[]{:S(2)}, u32[]{:S(2)}) collective-permute-start(bf16[128,1024]{1,0:T(8,128)(2,1)S(1)} %get-tuple-element.47), channel_id=1, source_target_pairs={{0,8},{4,20},{8,0},{12,28},{16,24},{20,4},{24,16},{28,12},{1,9},{5... | collective-permute-start | bytes 786440 | tf_op jit(solution)/shard_map/ppermute | solution.py:466
  32.5 1.6 %collective-permute-done.12.passed = bf16[128,1024]{1,0:T(8,128)(2,1)S(1)} collective-permute-done((bf16[128,1024]{1,0:T(8,128)(2,1)S(1)}, bf16[128,1024]{1,0:T(8,128)(2,1)S(1)}, u32[]{:S(2)}, u32[]{:S(2)}) %collective-permute-start.12) | collective-permute-done | bytes 262176 | tf_op jit(solution)/shard_map/ppermute | solution.py:466
  34.1 0.1 add.64
  34.2 0.8 %collective-permute-start.13 = (bf16[128,1024]{1,0:T(8,128)(2,1)S(1)}, bf16[128,1024]{1,0:T(8,128)(2,1)S(1)}, u32[]{:S(2)}, u32[]{:S(2)}) collective-permute-start(bf16[128,1024]{1,0:T(8,128)(2,1)S(1)} %add.64), channel_id=1, source_target_pairs={{0,16},{4,12},{8,24},{12,4},{16,0},{20,28},{24,8},{28,20},{1,17},{... | collective-permute-start | bytes 786440 | tf_op jit(solution)/shard_map/ppermute | solution.py:466
  35.0 0.0 copy-done
  35.0 0.0 copy-done.3
  35.0 0.9 %multiply_subtract_fusion = f32[64,1024]{1,0:T(8,128)} fusion(f32[64,1024]{1,0:T(8,128)S(1)} %copy-done, f32[64,1024]{1,0:T(8,128)S(1)} %copy-done.3, f32[64,1024]{1,0:T(8,128)S(1)} %copy-done.2, f32[64,1024]{1,0:T(8,128)S(1)} %copy-done.1), kind=kLoop, calls=%fused_computation.10 | loop fusion | flops 983040 | bytes 1310720 | tf_op jit(solution)/shard_map/sub | solution.py:28
  35.9 4.9 %collective-permute-done.10 = bf16[128,1024]{1,0:T(8,128)(2,1)S(1)} collective-permute-done((bf16[128,1024]{1,0:T(8,128)(2,1)S(1)}, bf16[128,1024]{1,0:T(8,128)(2,1)S(1)}, u32[]{:S(2)}, u32[]{:S(2)}) %collective-permute-start.10) | collective-permute-done | bytes 262176 | tf_op jit(solution)/shard_map/ppermute | solution.py:466
  40.8 0.1 convert_add_fusion
  40.8 0.0 collective-permute-done.13
  40.8 0.8 %fusion.6 = bf16[1,128,1024]{2,1,0:T(8,128)(2,1)} fusion(f32[128,1024]{1,0:T(8,128)S(1)} %convert_add_fusion, bf16[128,1024]{1,0:T(8,128)(2,1)S(1)} %collective-permute-done.13), kind=kLoop, calls=%fused_computation.9 | loop fusion | flops 393216 | bytes 1048576 | tf_op jit(solution)/shard_map/broadcast_in_dim | solution.py:532
  (2 shorter events, 0.0 us)
Async XLA Ops:
  1.6 15.6 %collective-permute-start.3 = (bf16[2,128,512]{2,1,0:T(8,128)(2,1)S(1)}, bf16[2,128,512]{2,1,0:T(8,128)(2,1)S(1)}, u32[]{:S(2)}, u32[]{:S(2)}) collective-permute-start(bf16[2,128,512]{2,1,0:T(8,128)(2,1)S(1)} %pack_far.1), channel_id=1, source_target_pairs={{0,24},{4,28},{8,16},{12,20},{16,8},{20,12},{24,0},{28,4},{1,25},{... | collective-permute-start | bytes 786440 | tf_op jit(solution)/shard_map/ppermute | solution.py:34
  7.4 10.4 %collective-permute-start.1 = (bf16[2,128,512]{2,1,0:T(8,128)(2,1)S(1)}, bf16[2,128,512]{2,1,0:T(8,128)(2,1)S(1)}, u32[]{:S(2)}, u32[]{:S(2)}) collective-permute-start(bf16[2,128,512]{2,1,0:T(8,128)(2,1)S(1)} %get-tuple-element.37), channel_id=1, source_target_pairs={{0,8},{4,12},{8,0},{12,4},{16,24},{20,28},{24,16},{28,20},{1,9},{5... | collective-permute-start | bytes 786440 | tf_op jit(solution)/shard_map/ppermute | solution.py:34
  8.0 9.8 %collective-permute-start.2 = (bf16[2,128,512]{2,1,0:T(8,128)(2,1)S(1)}, bf16[2,128,512]{2,1,0:T(8,128)(2,1)S(1)}, u32[]{:S(2)}, u32[]{:S(2)}) collective-permute-start(bf16[2,128,512]{2,1,0:T(8,128)(2,1)S(1)} %get-tuple-element.38), channel_id=1, source_target_pairs={{0,16},{4,20},{8,24},{12,28},{16,0},{20,4},{24,8},{28,12},{1,17},{... | collective-permute-start | bytes 786440 | tf_op jit(solution)/shard_map/ppermute | solution.py:34
  8.0 8.6 %collective-permute-start = (bf16[64,1024]{1,0:T(8,128)(2,1)S(1)}, bf16[64,1024]{1,0:T(8,128)(2,1)S(1)}, u32[]{:S(2)}, u32[]{:S(2)}) collective-permute-start(bf16[64,1024]{1,0:T(8,128)(2,1)S(1)} %get-tuple-element.28.refs_4_), channel_id=1, source_target_pairs={{0,2},{1,3},{2,0},{3,1},{4,6},{5,7},{6,4},{7,5},{8,10},{9,11},{10,... | collective-permute-start | bytes 393224 | tf_op jit(solution)/shard_map/ppermute | solution.py:34
  11.1 6.2 %collective-permute-start.4 = (bf16[64,1024]{1,0:T(8,128)(2,1)S(1)}, bf16[64,1024]{1,0:T(8,128)(2,1)S(1)}, u32[]{:S(2)}, u32[]{:S(2)}) collective-permute-start(bf16[64,1024]{1,0:T(8,128)(2,1)S(1)} %get-tuple-element.28.refs_4_), channel_id=1, source_target_pairs={{0,1},{1,0},{2,3},{3,2},{4,5},{5,4},{6,7},{7,6},{8,9},{9,8},{10,11... | collective-permute-start | bytes 393224 | tf_op jit(solution)/shard_map/ppermute | solution.py:34
  16.7 5.0 %collective-permute-start.5 = (bf16[64,1024]{1,0:T(8,128)(2,1)S(1)}, bf16[64,1024]{1,0:T(8,128)(2,1)S(1)}, u32[]{:S(2)}, u32[]{:S(2)}) collective-permute-start(bf16[64,1024]{1,0:T(8,128)(2,1)S(1)} %collective-permute-done.refs_6_), channel_id=1, source_target_pairs={{0,1},{1,0},{2,3},{3,2},{4,5},{5,4},{6,7},{7,6},{8,9},{9,8},{10,11... | collective-permute-start | bytes 393224 | tf_op jit(solution)/shard_map/ppermute | solution.py:34
  17.9 7.5 %collective-permute-start.8 = (bf16[1408,512]{1,0:T(8,128)(2,1)S(1)}, bf16[1408,512]{1,0:T(8,128)(2,1)S(1)}, u32[]{:S(2)}, u32[]{:S(2)}) collective-permute-start(bf16[1408,512]{1,0:T(8,128)(2,1)S(1)} %stack.1.refs_3_.own.refs_1_), channel_id=1, source_target_pairs={{0,4},{4,0},{8,12},{12,8},{16,20},{20,16},{24,28},{28,24},{1,5},{5... | collective-permute-start | bytes 4325384 | tf_op jit(solution)/shard_map/ppermute | solution.py:34
  18.0 7.4 %collective-permute-start.11 = (bf16[128,512]{1,0:T(8,128)(2,1)}, bf16[128,512]{1,0:T(8,128)(2,1)S(1)}, u32[]{:S(2)}, u32[]{:S(2)}) collective-permute-start(bf16[128,512]{1,0:T(8,128)(2,1)} %get-tuple-element.49), channel_id=1, source_target_pairs={{0,24},{4,28},{8,16},{12,20},{16,8},{20,12},{24,0},{28,4},{1,25},{... | collective-permute-start | bytes 393224 | tf_op jit(solution)/shard_map/ppermute | solution.py:34
  22.3 5.0 %collective-permute-start.9 = (bf16[64,1024]{1,0:T(8,128)(2,1)}, bf16[64,1024]{1,0:T(8,128)(2,1)S(1)}, u32[]{:S(2)}, u32[]{:S(2)}) collective-permute-start(bf16[64,1024]{1,0:T(8,128)(2,1)} %hold.1.last), channel_id=1, source_target_pairs={{0,4},{4,0},{8,12},{12,8},{16,20},{20,16},{24,28},{28,24},{1,5},{5... | collective-permute-start | bytes 393224 | tf_op jit(solution)/shard_map/ppermute | solution.py:34
  22.3 6.5 %collective-permute-start.6 = (bf16[128,512]{1,0:T(8,128)(2,1)}, bf16[128,512]{1,0:T(8,128)(2,1)S(1)}, u32[]{:S(2)}, u32[]{:S(2)}) collective-permute-start(bf16[128,512]{1,0:T(8,128)(2,1)} %get-tuple-element.43), channel_id=1, source_target_pairs={{0,8},{4,12},{8,0},{12,4},{16,24},{20,28},{24,16},{28,20},{1,9},{5... | collective-permute-start | bytes 393224 | tf_op jit(solution)/shard_map/ppermute | solution.py:34
  23.8 5.8 %collective-permute-start.7 = (bf16[128,512]{1,0:T(8,128)(2,1)}, bf16[128,512]{1,0:T(8,128)(2,1)S(1)}, u32[]{:S(2)}, u32[]{:S(2)}) collective-permute-start(bf16[128,512]{1,0:T(8,128)(2,1)} %get-tuple-element.44), channel_id=1, source_target_pairs={{0,16},{4,20},{8,24},{12,28},{16,0},{20,4},{24,8},{28,12},{1,17},{... | collective-permute-start | bytes 393224 | tf_op jit(solution)/shard_map/ppermute | solution.py:34
  27.7 6.4 %collective-permute-start.12 = (bf16[128,1024]{1,0:T(8,128)(2,1)S(1)}, bf16[128,1024]{1,0:T(8,128)(2,1)S(1)}, u32[]{:S(2)}, u32[]{:S(2)}) collective-permute-start(bf16[128,1024]{1,0:T(8,128)(2,1)S(1)} %project.3), channel_id=1, source_target_pairs={{0,8},{4,20},{8,0},{12,28},{16,24},{20,4},{24,16},{28,12},{1,9},{5... | collective-permute-start | bytes 786440 | tf_op jit(solution)/shard_map/ppermute | solution.py:466
  31.1 3.8 %copy-start = (f32[64,1024]{1,0:T(8,128)S(1)}, f32[64,1024]{1,0:T(8,128)}, u32[]{:S(2)}) copy-start(f32[64,1024]{1,0:T(8,128)} %refs_0_.1) | copy-start | bytes 786436
  31.1 3.8 %copy-start.1 = (f32[64,1024]{1,0:T(8,128)S(1)}, f32[64,1024]{1,0:T(8,128)}, u32[]{:S(2)}) copy-start(f32[64,1024]{1,0:T(8,128)} %refs_1_.1) | copy-start | bytes 786436
  31.2 3.8 %copy-start.2 = (f32[64,1024]{1,0:T(8,128)S(1)}, f32[64,1024]{1,0:T(8,128)}, u32[]{:S(2)}) copy-start(f32[64,1024]{1,0:T(8,128)} %refs_2_.1) | copy-start | bytes 786436
  31.2 3.8 %copy-start.3 = (f32[64,1024]{1,0:T(8,128)S(1)}, f32[64,1024]{1,0:T(8,128)}, u32[]{:S(2)}) copy-start(f32[64,1024]{1,0:T(8,128)} %refs_3_.1) | copy-start | bytes 786436
  31.9 8.9 %collective-permute-start.10 = (bf16[128,1024]{1,0:T(8,128)(2,1)S(1)}, bf16[128,1024]{1,0:T(8,128)(2,1)S(1)}, u32[]{:S(2)}, u32[]{:S(2)}) collective-permute-start(bf16[128,1024]{1,0:T(8,128)(2,1)S(1)} %get-tuple-element.47), channel_id=1, source_target_pairs={{0,8},{4,20},{8,0},{12,28},{16,24},{20,4},{24,16},{28,12},{1,9},{5... | collective-permute-start | bytes 786440 | tf_op jit(solution)/shard_map/ppermute | solution.py:466
  34.2 6.7 %collective-permute-start.13 = (bf16[128,1024]{1,0:T(8,128)(2,1)S(1)}, bf16[128,1024]{1,0:T(8,128)(2,1)S(1)}, u32[]{:S(2)}, u32[]{:S(2)}) collective-permute-start(bf16[128,1024]{1,0:T(8,128)(2,1)S(1)} %add.64), channel_id=1, source_target_pairs={{0,16},{4,12},{8,24},{12,4},{16,0},{20,28},{24,8},{28,20},{1,17},{... | collective-permute-start | bytes 786440 | tf_op jit(solution)/shard_map/ppermute | solution.py:466
